TPU v7x, 32 devices: a whole 2x2x4 slice. The times are simulated.
32 devices in a mesh: scan: 4 (over y, x), cross: 8 (over z, core).
Axes of the slice: x: 2, y: 2, z: 4, core: 2. Of those that a mesh axis runs over, the one named last changes fastest.
Arguments:
- wafer_state: float32 [64, 128, 384], P('scan', 'cross'), may hold values from 0 to 1, as said below
- layer_heat_coefficients: float32 [256], replicated, may hold values from 0.03 to 0.14
- beam_profile: float32 [128], replicated, may hold values from 0.25 to 1.75
- beam_start: int32 [4], replicated, may hold values from 0 to 63
- beam_steps: int32 [4], replicated, may hold values from 1 to 64
Outputs:
- annealed: float32 [64, 128, 384], P('scan', 'cross')
Inputs may be any that keep to these rules, and one draw needn't show every extreme that they name: `wafer_state`: temperatures lie in 0 to 0.6, acid in 0 to 1, protection in 0.5 to 1.
All inputs are finite; a program needn't handle non-finite values.
Results may differ from a plain program's by a relative error of at most 0.00002.
Values sent between devices are 32-bit elements; how exact they have to be, the bound alone decides.
No kernel may reach another device: no remote copies, remote signals or barrier semaphores. Data moves between devices by JAX's collectives and lax.ppermute only.
A program may use at most 64 MiB of HBM per device.

v0:
```python
import jax
import jax.numpy as jnp
from jax import lax
from jax.sharding import PartitionSpec as P

STEPS = 4
SUBSTEPS = 2


heat_power = 0.5
absorb_depth = 6.0
barrier_energy = 3.0
frequency_multiplier = 0.6
proton_mobility = 0.15


def with_halo(shard, sides, width):
    for axis, dim in sides:
        size, length = (lax.axis_size(axis), shard.shape[dim])
        up = [(i, (i + 1) % size) for i in range(size)]
        down = [(j, i) for i, j in up]
        last = lax.slice_in_dim(shard, length - width, length, axis=dim)
        first = lax.slice_in_dim(shard, 0, width, axis=dim)
        before = lax.ppermute(last, axis, up)
        after = lax.ppermute(first, axis, down)
        shard = jnp.concatenate([before, shard, after], axis=dim)
    return shard


def shifted(value, axis, steps):
    count = lax.axis_size(axis)
    pairs = [(source, (source + steps) % count) for source in range(count)]
    return lax.ppermute(value, axis, pairs)


def lateral_heat_current(values, coeffs):
    middle_v = values[1:-1, 1:-1]
    middle_c = coeffs[1:-1, 1:-1]
    flow_sum = jnp.zeros_like(middle_v)
    for other_v, other_c in (
        (values[2:, 1:-1], coeffs[2:, 1:-1]),
        (values[:-2, 1:-1], coeffs[:-2, 1:-1]),
        (values[1:-1, 2:], coeffs[1:-1, 2:]),
        (values[1:-1, :-2], coeffs[1:-1, :-2]),
    ):
        flow_sum = flow_sum + 0.5 * (middle_c + other_c) * (other_v - middle_v)
    return flow_sum


def lower_heat_current(values, coeffs, below_v, below_c):
    upper_v = jnp.concatenate([values[..., :1], values[..., :-1]], axis=-1)
    upper_c = jnp.concatenate([coeffs[..., :1], coeffs[..., :-1]], axis=-1)
    lower_v = jnp.concatenate([values[..., 1:], below_v], axis=-1)
    lower_c = jnp.concatenate([coeffs[..., 1:], below_c], axis=-1)
    return 0.5 * (coeffs + upper_c) * (upper_v - values) + 0.5 * (coeffs + lower_c) * (
        lower_v - values
    )


def substep(
    heated_extent, protected_fraction, layer_heat_coefficients, profile, xcoord, center, spread
):
    vertical_cells = layer_heat_coefficients.shape[0]
    polymer_coating = protected_fraction.shape[-1]
    warmth_grid = heated_extent[..., :vertical_cells]
    acid_ext = heated_extent[..., vertical_cells:]
    local_heat_coupling = layer_heat_coefficients / (1.0 + 0.25 * warmth_grid * warmth_grid)
    midpoint_warmth = warmth_grid[1:-1, 1:-1]
    midpoint_heat_ability = local_heat_coupling[1:-1, 1:-1]
    blank_stack_vector = jnp.zeros_like(midpoint_warmth[..., :1])
    heat_current = lateral_heat_current(warmth_grid, local_heat_coupling) + lower_heat_current(
        midpoint_warmth,
        midpoint_heat_ability,
        blank_stack_vector,
        blank_stack_vector + layer_heat_coefficients[-1],
    )
    depth_level = jnp.arange(vertical_cells, dtype=jnp.float32)
    absorb = jnp.where(
        depth_level >= polymer_coating,
        jnp.exp(-(depth_level - polymer_coating) / absorb_depth),
        0.0,
    )
    beam_spot = jnp.exp(-jnp.square((xcoord - center) / spread))
    energy_input = heat_power * beam_spot[:, None, None] * profile[None, :, None] * absorb
    updated_warmth = midpoint_warmth + heat_current + energy_input
    polymer_warmth = warmth_grid[..., :polymer_coating]
    spread_proton_site = (
        proton_mobility * polymer_warmth * polymer_warmth / (1.0 + polymer_warmth * polymer_warmth)
    )
    middle_a = acid_ext[1:-1, 1:-1]
    middle_d = spread_proton_site[1:-1, 1:-1]
    new_acid = (
        middle_a
        + lateral_heat_current(acid_ext, spread_proton_site)
        + lower_heat_current(middle_a, middle_d, middle_a[..., -1:], middle_d[..., -1:])
    )
    cleavage_rate = frequency_multiplier * jnp.exp(
        -barrier_energy / (1.0 + midpoint_warmth[..., :polymer_coating])
    )
    new_protect = protected_fraction * (1.0 - cleavage_rate * middle_a)
    return (jnp.concatenate([updated_warmth, new_acid], axis=-1), new_protect)


def edge_mask(cross_pos, cols_here, margin, total_y):
    places = jnp.arange(cols_here + 2 * margin, dtype=jnp.int32) + cross_pos * cols_here - margin
    inside = (places >= 0) & (places < total_y)
    return jnp.where(inside, 1.0, 0.0).astype(jnp.float32)[None, :, None]


def advance(
    heated_extent,
    protected_fraction,
    margin,
    centers,
    layer_heat_coefficients,
    profile_pad,
    pad_width,
    block_pos,
    cross_pos,
    rows_here,
    cols_here,
    total_x,
    total_y,
):
    heated_extent = heated_extent * edge_mask(cross_pos, cols_here, margin, total_y)
    spread = float(rows_here // 2)
    for step_no, center in enumerate(centers):
        inner_gap = margin - 1 - step_no
        offsets = (
            jnp.arange(rows_here + 2 * inner_gap, dtype=jnp.int32)
            + block_pos * rows_here
            - inner_gap
        )
        xcoord = jnp.mod(offsets, total_x).astype(jnp.float32)
        profile = lax.dynamic_slice_in_dim(
            profile_pad, cross_pos * cols_here + pad_width - inner_gap, cols_here + 2 * inner_gap
        )
        heated_extent, protected_fraction = substep(
            heated_extent,
            protected_fraction,
            layer_heat_coefficients,
            profile,
            xcoord,
            center,
            spread,
        )
    return (heated_extent, protected_fraction)


def shards(wafer_state, layer_heat_coefficients, beam_profile, beam_start, beam_steps):
    rows_here = wafer_state.shape[0]
    cols_here = wafer_state.shape[1]
    vertical_cells = layer_heat_coefficients.shape[0]
    hot_depth = vertical_cells + (wafer_state.shape[2] - vertical_cells) // 2
    scan_count = lax.axis_size("scan")
    scan_pos = lax.axis_index("scan")
    cross_pos = lax.axis_index("cross")
    total_x = rows_here * scan_count
    total_y = cols_here * lax.axis_size("cross")
    sub_count = SUBSTEPS
    profile_pad = jnp.pad(beam_profile, (sub_count, sub_count))
    for frame_no in range(STEPS):
        block_pos = jnp.mod(scan_pos - frame_no, scan_count)
        centers = [
            (beam_start[frame_no] + sub_no * beam_steps[frame_no]).astype(jnp.float32)
            for sub_no in range(sub_count)
        ]
        for center in centers:
            heated_extent = with_halo(wafer_state[..., :hot_depth], (("scan", 0), ("cross", 1)), 1)
            hot_part, protected_fraction = advance(
                heated_extent,
                wafer_state[..., hot_depth:],
                1,
                [center],
                layer_heat_coefficients,
                profile_pad,
                sub_count,
                block_pos,
                cross_pos,
                rows_here,
                cols_here,
                total_x,
                total_y,
            )
            wafer_state = jnp.concatenate([hot_part, protected_fraction], axis=-1)
        cooled = scan_pos == frame_no % scan_count
        wafer_state = jnp.concatenate(
            [
                jnp.where(cooled, 0.0, wafer_state[..., :vertical_cells]),
                wafer_state[..., vertical_cells:],
            ],
            axis=-1,
        )
    lag_blocks = STEPS % scan_count
    if lag_blocks:
        wafer_state = shifted(wafer_state, "scan", -lag_blocks)
    return wafer_state


def solution(mesh):
    in_specs = (P("scan", "cross", None), P(), P(), P(), P())
    out_specs = P("scan", "cross", None)
    return jax.shard_map(shards, mesh=mesh, in_specs=in_specs, out_specs=out_specs, check_vma=False)
```

profile of v0, /device:TPU:0, one launch (start us, length us, event | category | flops | bytes accessed | tf_op | source)
XLA Modules:
  0.0 119.0 jit_solution(10387750866858385457)
XLA Ops:
  0.8 2.9 %collective-permute-start = (f32[1,16,320]{2,1,0:T(8,128)S(1)}, f32[1,16,320]{2,1,0:T(8,128)S(1)}, u32[]{:S(2)}, u32[]{:S(2)}) collective-permute-start(f32[1,16,320]{2,1,0:T(8,128)S(1)} %get-tuple-element.107), channel_id=1, source_target_pairs={{0,8},{8,16},{16,24},{24,0},{1,9},{9,17},{17,25},{25,1},{2,10},{10... | collective-permute-start | bytes 61448 | tf_op jit(solution)/shard_map/ppermute | solution.py:24
  13.5 1.1 pad_maximum_fusion.31
  14.6 3.5 %collective-permute-start.3 = (f32[18,1,320]{2,1,0:T(1,128)S(1)}, f32[18,1,320]{2,1,0:T(1,128)S(1)}, u32[]{:S(2)}, u32[]{:S(2)}) collective-permute-start(f32[18,1,320]{2,1,0:T(1,128)S(1)} %get-tuple-element.92), channel_id=1, source_target_pairs={{1,0},{2,1},{3,2},{4,3},{5,4},{6,5},{7,6},{0,7},{9,8},{10,9},{11,1... | collective-permute-start | bytes 69128 | tf_op jit(solution)/shard_map/ppermute | solution.py:25
  20.8 1.1 fusion.122
  22.0 1.1 collective-permute-start.4
  23.1 1.9 %collective-permute-start.5 = (f32[1,16,320]{2,1,0:T(8,128)S(1)}, f32[1,16,320]{2,1,0:T(8,128)S(1)}, u32[]{:S(2)}, u32[]{:S(2)}) collective-permute-start(f32[1,16,320]{2,1,0:T(8,128)S(1)} %get-tuple-element.106), channel_id=1, source_target_pairs={{8,0},{16,8},{24,16},{0,24},{9,1},{17,9},{25,17},{1,25},{10,2},{18... | collective-permute-start | bytes 61448 | tf_op jit(solution)/shard_map/ppermute | solution.py:25
  25.0 2.0 %collective-permute-done.4 = f32[1,16,320]{2,1,0:T(8,128)S(1)} collective-permute-done((f32[1,16,320]{2,1,0:T(8,128)S(1)}, f32[1,16,320]{2,1,0:T(8,128)S(1)}, u32[]{:S(2)}, u32[]{:S(2)}) %collective-permute-start.4) | collective-permute-done | bytes 20512 | tf_op jit(solution)/shard_map/ppermute | solution.py:24
  27.6 3.5 %collective-permute-start.7 = (f32[18,1,320]{2,1,0:T(1,128)S(1)}, f32[18,1,320]{2,1,0:T(1,128)S(1)}, u32[]{:S(2)}, u32[]{:S(2)}) collective-permute-start(f32[18,1,320]{2,1,0:T(1,128)S(1)} %get-tuple-element.88), channel_id=1, source_target_pairs={{1,0},{2,1},{3,2},{4,3},{5,4},{6,5},{7,6},{0,7},{9,8},{10,9},{11,1... | collective-permute-start | bytes 69128 | tf_op jit(solution)/shard_map/ppermute | solution.py:25
  31.2 1.5 %collective-permute-done.6 = f32[18,1,320]{2,1,0:T(1,128)S(1)} collective-permute-done((f32[18,1,320]{2,1,0:T(1,128)S(1)}, f32[18,1,320]{2,1,0:T(1,128)S(1)}, u32[]{:S(2)}, u32[]{:S(2)}) %collective-permute-start.6) | collective-permute-done | bytes 23072 | tf_op jit(solution)/shard_map/ppermute | solution.py:24
  34.0 1.1 fusion.108
  35.1 2.7 %collective-permute-start.8 = (f32[1,16,320]{2,1,0:T(8,128)S(1)}, f32[1,16,320]{2,1,0:T(8,128)S(1)}, u32[]{:S(2)}, u32[]{:S(2)}) collective-permute-start(f32[1,16,320]{2,1,0:T(8,128)S(1)} %get-tuple-element.103), channel_id=1, source_target_pairs={{0,8},{8,16},{16,24},{24,0},{1,9},{9,17},{17,25},{25,1},{2,10},{10... | collective-permute-start | bytes 61448 | tf_op jit(solution)/shard_map/ppermute | solution.py:24
  38.1 1.8 %collective-permute-done.8 = f32[1,16,320]{2,1,0:T(8,128)S(1)} collective-permute-done((f32[1,16,320]{2,1,0:T(8,128)S(1)}, f32[1,16,320]{2,1,0:T(8,128)S(1)}, u32[]{:S(2)}, u32[]{:S(2)}) %collective-permute-start.8) | collective-permute-done | bytes 20512 | tf_op jit(solution)/shard_map/ppermute | solution.py:24
  39.9 1.8 %collective-permute-done.9 = f32[1,16,320]{2,1,0:T(8,128)S(1)} collective-permute-done((f32[1,16,320]{2,1,0:T(8,128)S(1)}, f32[1,16,320]{2,1,0:T(8,128)S(1)}, u32[]{:S(2)}, u32[]{:S(2)}) %collective-permute-start.9) | collective-permute-done | bytes 20512 | tf_op jit(solution)/shard_map/ppermute | solution.py:25
  41.8 3.5 %collective-permute-start.11 = (f32[18,1,320]{2,1,0:T(1,128)S(1)}, f32[18,1,320]{2,1,0:T(1,128)S(1)}, u32[]{:S(2)}, u32[]{:S(2)}) collective-permute-start(f32[18,1,320]{2,1,0:T(1,128)S(1)} %get-tuple-element.84), channel_id=1, source_target_pairs={{1,0},{2,1},{3,2},{4,3},{5,4},{6,5},{7,6},{0,7},{9,8},{10,9},{11,1... | collective-permute-start | bytes 69128 | tf_op jit(solution)/shard_map/ppermute | solution.py:25
  45.3 1.5 %collective-permute-done.10 = f32[18,1,320]{2,1,0:T(1,128)S(1)} collective-permute-done((f32[18,1,320]{2,1,0:T(1,128)S(1)}, f32[18,1,320]{2,1,0:T(1,128)S(1)}, u32[]{:S(2)}, u32[]{:S(2)}) %collective-permute-start.10) | collective-permute-done | bytes 23072 | tf_op jit(solution)/shard_map/ppermute | solution.py:24
  47.9 1.1 fusion.93
  49.3 1.0 collective-permute-start.12
  50.3 2.0 %collective-permute-start.13 = (f32[1,16,320]{2,1,0:T(8,128)S(1)}, f32[1,16,320]{2,1,0:T(8,128)S(1)}, u32[]{:S(2)}, u32[]{:S(2)}) collective-permute-start(f32[1,16,320]{2,1,0:T(8,128)S(1)} %get-tuple-element.102), channel_id=1, source_target_pairs={{8,0},{16,8},{24,16},{0,24},{9,1},{17,9},{25,17},{1,25},{10,2},{18... | collective-permute-start | bytes 61448 | tf_op jit(solution)/shard_map/ppermute | solution.py:25
  52.3 1.8 %collective-permute-done.12 = f32[1,16,320]{2,1,0:T(8,128)S(1)} collective-permute-done((f32[1,16,320]{2,1,0:T(8,128)S(1)}, f32[1,16,320]{2,1,0:T(8,128)S(1)}, u32[]{:S(2)}, u32[]{:S(2)}) %collective-permute-start.12) | collective-permute-done | bytes 20512 | tf_op jit(solution)/shard_map/ppermute | solution.py:24
  54.3 3.5 %collective-permute-start.15 = (f32[18,1,320]{2,1,0:T(1,128)S(1)}, f32[18,1,320]{2,1,0:T(1,128)S(1)}, u32[]{:S(2)}, u32[]{:S(2)}) collective-permute-start(f32[18,1,320]{2,1,0:T(1,128)S(1)} %get-tuple-element.80), channel_id=1, source_target_pairs={{1,0},{2,1},{3,2},{4,3},{5,4},{6,5},{7,6},{0,7},{9,8},{10,9},{11,1... | collective-permute-start | bytes 69128 | tf_op jit(solution)/shard_map/ppermute | solution.py:25
  57.8 1.5 %collective-permute-done.14 = f32[18,1,320]{2,1,0:T(1,128)S(1)} collective-permute-done((f32[18,1,320]{2,1,0:T(1,128)S(1)}, f32[18,1,320]{2,1,0:T(1,128)S(1)}, u32[]{:S(2)}, u32[]{:S(2)}) %collective-permute-start.14) | collective-permute-done | bytes 23072 | tf_op jit(solution)/shard_map/ppermute | solution.py:24
  60.7 1.1 fusion.79
  61.8 1.5 %collective-permute-start.16 = (f32[1,16,320]{2,1,0:T(8,128)S(1)}, f32[1,16,320]{2,1,0:T(8,128)S(1)}, u32[]{:S(2)}, u32[]{:S(2)}) collective-permute-start(f32[1,16,320]{2,1,0:T(8,128)S(1)} %get-tuple-element.99), channel_id=1, source_target_pairs={{0,8},{8,16},{16,24},{24,0},{1,9},{9,17},{17,25},{25,1},{2,10},{10... | collective-permute-start | bytes 61448 | tf_op jit(solution)/shard_map/ppermute | solution.py:24
  63.3 1.5 %collective-permute-start.17 = (f32[1,16,320]{2,1,0:T(8,128)S(1)}, f32[1,16,320]{2,1,0:T(8,128)S(1)}, u32[]{:S(2)}, u32[]{:S(2)}) collective-permute-start(f32[1,16,320]{2,1,0:T(8,128)S(1)} %get-tuple-element.100), channel_id=1, source_target_pairs={{8,0},{16,8},{24,16},{0,24},{9,1},{17,9},{25,17},{1,25},{10,2},{18... | collective-permute-start | bytes 61448 | tf_op jit(solution)/shard_map/ppermute | solution.py:25
  64.8 1.8 %collective-permute-done.16 = f32[1,16,320]{2,1,0:T(8,128)S(1)} collective-permute-done((f32[1,16,320]{2,1,0:T(8,128)S(1)}, f32[1,16,320]{2,1,0:T(8,128)S(1)}, u32[]{:S(2)}, u32[]{:S(2)}) %collective-permute-start.16) | collective-permute-done | bytes 20512 | tf_op jit(solution)/shard_map/ppermute | solution.py:24
  67.3 3.5 %collective-permute-start.19 = (f32[18,1,320]{2,1,0:T(1,128)S(1)}, f32[18,1,320]{2,1,0:T(1,128)S(1)}, u32[]{:S(2)}, u32[]{:S(2)}) collective-permute-start(f32[18,1,320]{2,1,0:T(1,128)S(1)} %get-tuple-element.76), channel_id=1, source_target_pairs={{1,0},{2,1},{3,2},{4,3},{5,4},{6,5},{7,6},{0,7},{9,8},{10,9},{11,1... | collective-permute-start | bytes 69128 | tf_op jit(solution)/shard_map/ppermute | solution.py:25
  70.8 1.5 %collective-permute-done.18 = f32[18,1,320]{2,1,0:T(1,128)S(1)} collective-permute-done((f32[18,1,320]{2,1,0:T(1,128)S(1)}, f32[18,1,320]{2,1,0:T(1,128)S(1)}, u32[]{:S(2)}, u32[]{:S(2)}) %collective-permute-start.18) | collective-permute-done | bytes 23072 | tf_op jit(solution)/shard_map/ppermute | solution.py:24
  73.4 1.1 fusion.64
  74.8 1.8 %collective-permute-start.20 = (f32[1,16,320]{2,1,0:T(8,128)S(1)}, f32[1,16,320]{2,1,0:T(8,128)S(1)}, u32[]{:S(2)}, u32[]{:S(2)}) collective-permute-start(f32[1,16,320]{2,1,0:T(8,128)S(1)} %get-tuple-element.97), channel_id=1, source_target_pairs={{0,8},{8,16},{16,24},{24,0},{1,9},{9,17},{17,25},{25,1},{2,10},{10... | collective-permute-start | bytes 61448 | tf_op jit(solution)/shard_map/ppermute | solution.py:24
  76.6 1.2 collective-permute-start.21
  77.8 1.8 %collective-permute-done.20 = f32[1,16,320]{2,1,0:T(8,128)S(1)} collective-permute-done((f32[1,16,320]{2,1,0:T(8,128)S(1)}, f32[1,16,320]{2,1,0:T(8,128)S(1)}, u32[]{:S(2)}, u32[]{:S(2)}) %collective-permute-start.20) | collective-permute-done | bytes 20512 | tf_op jit(solution)/shard_map/ppermute | solution.py:24
  80.5 3.5 %collective-permute-start.23 = (f32[18,1,320]{2,1,0:T(1,128)S(1)}, f32[18,1,320]{2,1,0:T(1,128)S(1)}, u32[]{:S(2)}, u32[]{:S(2)}) collective-permute-start(f32[18,1,320]{2,1,0:T(1,128)S(1)} %get-tuple-element.72), channel_id=1, source_target_pairs={{1,0},{2,1},{3,2},{4,3},{5,4},{6,5},{7,6},{0,7},{9,8},{10,9},{11,1... | collective-permute-start | bytes 69128 | tf_op jit(solution)/shard_map/ppermute | solution.py:25
  84.1 1.6 %collective-permute-done.22 = f32[18,1,320]{2,1,0:T(1,128)S(1)} collective-permute-done((f32[18,1,320]{2,1,0:T(1,128)S(1)}, f32[18,1,320]{2,1,0:T(1,128)S(1)}, u32[]{:S(2)}, u32[]{:S(2)}) %collective-permute-start.22) | collective-permute-done | bytes 23072 | tf_op jit(solution)/shard_map/ppermute | solution.py:24
  87.0 1.1 fusion.50
  88.1 2.6 %collective-permute-start.24 = (f32[1,16,320]{2,1,0:T(8,128)S(1)}, f32[1,16,320]{2,1,0:T(8,128)S(1)}, u32[]{:S(2)}, u32[]{:S(2)}) collective-permute-start(f32[1,16,320]{2,1,0:T(8,128)S(1)} %get-tuple-element.95), channel_id=1, source_target_pairs={{0,8},{8,16},{16,24},{24,0},{1,9},{9,17},{17,25},{25,1},{2,10},{10... | collective-permute-start | bytes 61448 | tf_op jit(solution)/shard_map/ppermute | solution.py:24
  91.1 1.8 %collective-permute-done.24 = f32[1,16,320]{2,1,0:T(8,128)S(1)} collective-permute-done((f32[1,16,320]{2,1,0:T(8,128)S(1)}, f32[1,16,320]{2,1,0:T(8,128)S(1)}, u32[]{:S(2)}, u32[]{:S(2)}) %collective-permute-start.24) | collective-permute-done | bytes 20512 | tf_op jit(solution)/shard_map/ppermute | solution.py:24
  92.9 1.6 %collective-permute-done.25 = f32[1,16,320]{2,1,0:T(8,128)S(1)} collective-permute-done((f32[1,16,320]{2,1,0:T(8,128)S(1)}, f32[1,16,320]{2,1,0:T(8,128)S(1)}, u32[]{:S(2)}, u32[]{:S(2)}) %collective-permute-start.25) | collective-permute-done | bytes 20512 | tf_op jit(solution)/shard_map/ppermute | solution.py:25
  94.7 3.5 %collective-permute-start.27 = (f32[18,1,320]{2,1,0:T(1,128)S(1)}, f32[18,1,320]{2,1,0:T(1,128)S(1)}, u32[]{:S(2)}, u32[]{:S(2)}) collective-permute-start(f32[18,1,320]{2,1,0:T(1,128)S(1)} %get-tuple-element.68), channel_id=1, source_target_pairs={{1,0},{2,1},{3,2},{4,3},{5,4},{6,5},{7,6},{0,7},{9,8},{10,9},{11,1... | collective-permute-start | bytes 69128 | tf_op jit(solution)/shard_map/ppermute | solution.py:25
  98.2 1.5 %collective-permute-done.26 = f32[18,1,320]{2,1,0:T(1,128)S(1)} collective-permute-done((f32[18,1,320]{2,1,0:T(1,128)S(1)}, f32[18,1,320]{2,1,0:T(1,128)S(1)}, u32[]{:S(2)}, u32[]{:S(2)}) %collective-permute-start.26) | collective-permute-done | bytes 23072 | tf_op jit(solution)/shard_map/ppermute | solution.py:24
  100.8 1.1 fusion.35
  102.2 1.0 collective-permute-start.28
  103.2 2.0 %collective-permute-start.29 = (f32[1,16,320]{2,1,0:T(8,128)S(1)}, f32[1,16,320]{2,1,0:T(8,128)S(1)}, u32[]{:S(2)}, u32[]{:S(2)}) collective-permute-start(f32[1,16,320]{2,1,0:T(8,128)S(1)} %get-tuple-element.94), channel_id=1, source_target_pairs={{8,0},{16,8},{24,16},{0,24},{9,1},{17,9},{25,17},{1,25},{10,2},{18... | collective-permute-start | bytes 61448 | tf_op jit(solution)/shard_map/ppermute | solution.py:25
  105.1 1.8 %collective-permute-done.28 = f32[1,16,320]{2,1,0:T(8,128)S(1)} collective-permute-done((f32[1,16,320]{2,1,0:T(8,128)S(1)}, f32[1,16,320]{2,1,0:T(8,128)S(1)}, u32[]{:S(2)}, u32[]{:S(2)}) %collective-permute-start.28) | collective-permute-done | bytes 20512 | tf_op jit(solution)/shard_map/ppermute | solution.py:24
  107.7 3.5 %collective-permute-start.31 = (f32[18,1,320]{2,1,0:T(1,128)}, f32[18,1,320]{2,1,0:T(1,128)}, u32[]{:S(2)}, u32[]{:S(2)}) collective-permute-start(f32[18,1,320]{2,1,0:T(1,128)} %get-tuple-element.64), channel_id=1, source_target_pairs={{1,0},{2,1},{3,2},{4,3},{5,4},{6,5},{7,6},{0,7},{9,8},{10,9},{11,1... | collective-permute-start | bytes 69128 | tf_op jit(solution)/shard_map/ppermute | solution.py:25
  111.2 1.7 %collective-permute-done.30 = f32[18,1,320]{2,1,0:T(1,128)S(1)} collective-permute-done((f32[18,1,320]{2,1,0:T(1,128)}, f32[18,1,320]{2,1,0:T(1,128)S(1)}, u32[]{:S(2)}, u32[]{:S(2)}) %collective-permute-start.30) | collective-permute-done | bytes 23072 | tf_op jit(solution)/shard_map/ppermute | solution.py:24
  113.0 1.1 maximum_multiply_fusion.7
  114.1 1.8 %fusion.169 = f32[16,16,64]{2,1,0:T(8,128)S(1)} fusion(f32[18,18,320]{2,1,0:T(8,128)S(1)} %maximum_multiply_fusion.7, f32[18,18,320]{2,1,0:T(8,128)S(1)} %maximum_multiply_fusion.6, f32[18,18,320]{2,1,0:T(8,128)} %copy-done.1, f32[18,18,320]{2,1,0:T(8,128)S(1)} %maximum_multiply_fusion.4, f32[18,18,320]{2,1,0:T(8,128)} %copy-done, ...), kind=kLoop, calls=%fused_computation.275 | loop fusion | flops 786432 | bytes 1179648 | tf_op jit(solution)/shard_map/mul | solution.py:100
  117.0 1.1 fusion.21
  (157 shorter events, 19.0 us)
Async XLA Ops:
  0.0 4.8 %copy-start.5 = (s32[4]{0:T(128)S(1)}, s32[4]{0:T(128)}, u32[]{:S(2)}) copy-start(s32[4]{0:T(128)} %param.9) | copy-start | bytes 52
  0.0 4.8 %copy-start.6 = (s32[4]{0:T(128)S(1)}, s32[4]{0:T(128)}, u32[]{:S(2)}) copy-start(s32[4]{0:T(128)} %param.8) | copy-start | bytes 52
  0.0 13.3 %copy-start.7 = (f32[128]{0:T(128)S(1)}, f32[128]{0:T(128)}, u32[]{:S(2)}) copy-start(f32[128]{0:T(128)} %param.7) | copy-start | bytes 1540
  0.8 18.9 %copy-start.3 = (f32[16,16,384]{2,1,0:T(8,128)S(1)}, f32[16,16,384]{2,1,0:T(8,128)}, u32[]{:S(2)}) copy-start(f32[16,16,384]{2,1,0:T(8,128)} %param.5) | copy-start | bytes 1179652
  0.8 12.7 %collective-permute-start = (f32[1,16,320]{2,1,0:T(8,128)S(1)}, f32[1,16,320]{2,1,0:T(8,128)S(1)}, u32[]{:S(2)}, u32[]{:S(2)}) collective-permute-start(f32[1,16,320]{2,1,0:T(8,128)S(1)} %get-tuple-element.107), channel_id=1, source_target_pairs={{0,8},{8,16},{16,24},{24,0},{1,9},{9,17},{17,25},{25,1},{2,10},{10... | collective-permute-start | bytes 61448 | tf_op jit(solution)/shard_map/ppermute | solution.py:24
  3.7 9.7 %collective-permute-start.1 = (f32[1,16,320]{2,1,0:T(8,128)S(1)}, f32[1,16,320]{2,1,0:T(8,128)S(1)}, u32[]{:S(2)}, u32[]{:S(2)}) collective-permute-start(f32[1,16,320]{2,1,0:T(8,128)S(1)} %get-tuple-element.108), channel_id=1, source_target_pairs={{8,0},{16,8},{24,16},{0,24},{9,1},{17,9},{25,17},{1,25},{10,2},{18... | collective-permute-start | bytes 61448 | tf_op jit(solution)/shard_map/ppermute | solution.py:25
  14.6 5.1 %collective-permute-start.2 = (f32[18,1,320]{2,1,0:T(1,128)S(1)}, f32[18,1,320]{2,1,0:T(1,128)S(1)}, u32[]{:S(2)}, u32[]{:S(2)}) collective-permute-start(f32[18,1,320]{2,1,0:T(1,128)S(1)} %get-tuple-element.91), channel_id=1, source_target_pairs={{0,1},{1,2},{2,3},{3,4},{4,5},{5,6},{6,7},{7,0},{8,9},{9,10},{10,1... | collective-permute-start | bytes 69128 | tf_op jit(solution)/shard_map/ppermute | solution.py:24
  14.6 3.5 %copy-start.4 = (f32[256]{0:T(256)S(1)}, f32[256]{0:T(256)}, u32[]{:S(2)}) copy-start(f32[256]{0:T(256)} %param.6) | copy-start | bytes 3076
  14.6 5.1 %collective-permute-start.3 = (f32[18,1,320]{2,1,0:T(1,128)S(1)}, f32[18,1,320]{2,1,0:T(1,128)S(1)}, u32[]{:S(2)}, u32[]{:S(2)}) collective-permute-start(f32[18,1,320]{2,1,0:T(1,128)S(1)} %get-tuple-element.92), channel_id=1, source_target_pairs={{1,0},{2,1},{3,2},{4,3},{5,4},{6,5},{7,6},{0,7},{9,8},{10,9},{11,1... | collective-permute-start | bytes 69128 | tf_op jit(solution)/shard_map/ppermute | solution.py:25
  22.0 5.0 %collective-permute-start.4 = (f32[1,16,320]{2,1,0:T(8,128)S(1)}, f32[1,16,320]{2,1,0:T(8,128)S(1)}, u32[]{:S(2)}, u32[]{:S(2)}) collective-permute-start(f32[1,16,320]{2,1,0:T(8,128)S(1)} %get-tuple-element.105), channel_id=1, source_target_pairs={{0,8},{8,16},{16,24},{24,0},{1,9},{9,17},{17,25},{25,1},{2,10},{10... | collective-permute-start | bytes 61448 | tf_op jit(solution)/shard_map/ppermute | solution.py:24
  23.1 4.5 %collective-permute-start.5 = (f32[1,16,320]{2,1,0:T(8,128)S(1)}, f32[1,16,320]{2,1,0:T(8,128)S(1)}, u32[]{:S(2)}, u32[]{:S(2)}) collective-permute-start(f32[1,16,320]{2,1,0:T(8,128)S(1)} %get-tuple-element.106), channel_id=1, source_target_pairs={{8,0},{16,8},{24,16},{0,24},{9,1},{17,9},{25,17},{1,25},{10,2},{18... | collective-permute-start | bytes 61448 | tf_op jit(solution)/shard_map/ppermute | solution.py:25
  27.6 5.1 %collective-permute-start.6 = (f32[18,1,320]{2,1,0:T(1,128)S(1)}, f32[18,1,320]{2,1,0:T(1,128)S(1)}, u32[]{:S(2)}, u32[]{:S(2)}) collective-permute-start(f32[18,1,320]{2,1,0:T(1,128)S(1)} %get-tuple-element.87), channel_id=1, source_target_pairs={{0,1},{1,2},{2,3},{3,4},{4,5},{5,6},{6,7},{7,0},{8,9},{9,10},{10,1... | collective-permute-start | bytes 69128 | tf_op jit(solution)/shard_map/ppermute | solution.py:24
  27.6 5.1 %collective-permute-start.7 = (f32[18,1,320]{2,1,0:T(1,128)S(1)}, f32[18,1,320]{2,1,0:T(1,128)S(1)}, u32[]{:S(2)}, u32[]{:S(2)}) collective-permute-start(f32[18,1,320]{2,1,0:T(1,128)S(1)} %get-tuple-element.88), channel_id=1, source_target_pairs={{1,0},{2,1},{3,2},{4,3},{5,4},{6,5},{7,6},{0,7},{9,8},{10,9},{11,1... | collective-permute-start | bytes 69128 | tf_op jit(solution)/shard_map/ppermute | solution.py:25
  35.1 4.8 %collective-permute-start.8 = (f32[1,16,320]{2,1,0:T(8,128)S(1)}, f32[1,16,320]{2,1,0:T(8,128)S(1)}, u32[]{:S(2)}, u32[]{:S(2)}) collective-permute-start(f32[1,16,320]{2,1,0:T(8,128)S(1)} %get-tuple-element.103), channel_id=1, source_target_pairs={{0,8},{8,16},{16,24},{24,0},{1,9},{9,17},{17,25},{25,1},{2,10},{10... | collective-permute-start | bytes 61448 | tf_op jit(solution)/shard_map/ppermute | solution.py:24
  37.9 3.8 %collective-permute-start.9 = (f32[1,16,320]{2,1,0:T(8,128)S(1)}, f32[1,16,320]{2,1,0:T(8,128)S(1)}, u32[]{:S(2)}, u32[]{:S(2)}) collective-permute-start(f32[1,16,320]{2,1,0:T(8,128)S(1)} %get-tuple-element.104), channel_id=1, source_target_pairs={{8,0},{16,8},{24,16},{0,24},{9,1},{17,9},{25,17},{1,25},{10,2},{18... | collective-permute-start | bytes 61448 | tf_op jit(solution)/shard_map/ppermute | solution.py:25
  41.7 5.1 %collective-permute-start.10 = (f32[18,1,320]{2,1,0:T(1,128)S(1)}, f32[18,1,320]{2,1,0:T(1,128)S(1)}, u32[]{:S(2)}, u32[]{:S(2)}) collective-permute-start(f32[18,1,320]{2,1,0:T(1,128)S(1)} %get-tuple-element.83), channel_id=1, source_target_pairs={{0,1},{1,2},{2,3},{3,4},{4,5},{5,6},{6,7},{7,0},{8,9},{9,10},{10,1... | collective-permute-start | bytes 69128 | tf_op jit(solution)/shard_map/ppermute | solution.py:24
  41.8 5.1 %collective-permute-start.11 = (f32[18,1,320]{2,1,0:T(1,128)S(1)}, f32[18,1,320]{2,1,0:T(1,128)S(1)}, u32[]{:S(2)}, u32[]{:S(2)}) collective-permute-start(f32[18,1,320]{2,1,0:T(1,128)S(1)} %get-tuple-element.84), channel_id=1, source_target_pairs={{1,0},{2,1},{3,2},{4,3},{5,4},{6,5},{7,6},{0,7},{9,8},{10,9},{11,1... | collective-permute-start | bytes 69128 | tf_op jit(solution)/shard_map/ppermute | solution.py:25
  49.3 4.8 %collective-permute-start.12 = (f32[1,16,320]{2,1,0:T(8,128)S(1)}, f32[1,16,320]{2,1,0:T(8,128)S(1)}, u32[]{:S(2)}, u32[]{:S(2)}) collective-permute-start(f32[1,16,320]{2,1,0:T(8,128)S(1)} %get-tuple-element.101), channel_id=1, source_target_pairs={{0,8},{8,16},{16,24},{24,0},{1,9},{9,17},{17,25},{25,1},{2,10},{10... | collective-permute-start | bytes 61448 | tf_op jit(solution)/shard_map/ppermute | solution.py:24
  50.3 3.8 %collective-permute-start.13 = (f32[1,16,320]{2,1,0:T(8,128)S(1)}, f32[1,16,320]{2,1,0:T(8,128)S(1)}, u32[]{:S(2)}, u32[]{:S(2)}) collective-permute-start(f32[1,16,320]{2,1,0:T(8,128)S(1)} %get-tuple-element.102), channel_id=1, source_target_pairs={{8,0},{16,8},{24,16},{0,24},{9,1},{17,9},{25,17},{1,25},{10,2},{18... | collective-permute-start | bytes 61448 | tf_op jit(solution)/shard_map/ppermute | solution.py:25
  54.2 5.1 %collective-permute-start.14 = (f32[18,1,320]{2,1,0:T(1,128)S(1)}, f32[18,1,320]{2,1,0:T(1,128)S(1)}, u32[]{:S(2)}, u32[]{:S(2)}) collective-permute-start(f32[18,1,320]{2,1,0:T(1,128)S(1)} %get-tuple-element.79), channel_id=1, source_target_pairs={{0,1},{1,2},{2,3},{3,4},{4,5},{5,6},{6,7},{7,0},{8,9},{9,10},{10,1... | collective-permute-start | bytes 69128 | tf_op jit(solution)/shard_map/ppermute | solution.py:24
  54.3 5.1 %collective-permute-start.15 = (f32[18,1,320]{2,1,0:T(1,128)S(1)}, f32[18,1,320]{2,1,0:T(1,128)S(1)}, u32[]{:S(2)}, u32[]{:S(2)}) collective-permute-start(f32[18,1,320]{2,1,0:T(1,128)S(1)} %get-tuple-element.80), channel_id=1, source_target_pairs={{1,0},{2,1},{3,2},{4,3},{5,4},{6,5},{7,6},{0,7},{9,8},{10,9},{11,1... | collective-permute-start | bytes 69128 | tf_op jit(solution)/shard_map/ppermute | solution.py:25
  59.5 1.2 copy-start
  61.8 4.8 %collective-permute-start.16 = (f32[1,16,320]{2,1,0:T(8,128)S(1)}, f32[1,16,320]{2,1,0:T(8,128)S(1)}, u32[]{:S(2)}, u32[]{:S(2)}) collective-permute-start(f32[1,16,320]{2,1,0:T(8,128)S(1)} %get-tuple-element.99), channel_id=1, source_target_pairs={{0,8},{8,16},{16,24},{24,0},{1,9},{9,17},{17,25},{25,1},{2,10},{10... | collective-permute-start | bytes 61448 | tf_op jit(solution)/shard_map/ppermute | solution.py:24
  63.3 3.8 %collective-permute-start.17 = (f32[1,16,320]{2,1,0:T(8,128)S(1)}, f32[1,16,320]{2,1,0:T(8,128)S(1)}, u32[]{:S(2)}, u32[]{:S(2)}) collective-permute-start(f32[1,16,320]{2,1,0:T(8,128)S(1)} %get-tuple-element.100), channel_id=1, source_target_pairs={{8,0},{16,8},{24,16},{0,24},{9,1},{17,9},{25,17},{1,25},{10,2},{18... | collective-permute-start | bytes 61448 | tf_op jit(solution)/shard_map/ppermute | solution.py:25
  67.2 5.1 %collective-permute-start.18 = (f32[18,1,320]{2,1,0:T(1,128)S(1)}, f32[18,1,320]{2,1,0:T(1,128)S(1)}, u32[]{:S(2)}, u32[]{:S(2)}) collective-permute-start(f32[18,1,320]{2,1,0:T(1,128)S(1)} %get-tuple-element.75), channel_id=1, source_target_pairs={{0,1},{1,2},{2,3},{3,4},{4,5},{5,6},{6,7},{7,0},{8,9},{9,10},{10,1... | collective-permute-start | bytes 69128 | tf_op jit(solution)/shard_map/ppermute | solution.py:24
  67.3 5.1 %collective-permute-start.19 = (f32[18,1,320]{2,1,0:T(1,128)S(1)}, f32[18,1,320]{2,1,0:T(1,128)S(1)}, u32[]{:S(2)}, u32[]{:S(2)}) collective-permute-start(f32[18,1,320]{2,1,0:T(1,128)S(1)} %get-tuple-element.76), channel_id=1, source_target_pairs={{1,0},{2,1},{3,2},{4,3},{5,4},{6,5},{7,6},{0,7},{9,8},{10,9},{11,1... | collective-permute-start | bytes 69128 | tf_op jit(solution)/shard_map/ppermute | solution.py:25
  74.8 4.8 %collective-permute-start.20 = (f32[1,16,320]{2,1,0:T(8,128)S(1)}, f32[1,16,320]{2,1,0:T(8,128)S(1)}, u32[]{:S(2)}, u32[]{:S(2)}) collective-permute-start(f32[1,16,320]{2,1,0:T(8,128)S(1)} %get-tuple-element.97), channel_id=1, source_target_pairs={{0,8},{8,16},{16,24},{24,0},{1,9},{9,17},{17,25},{25,1},{2,10},{10... | collective-permute-start | bytes 61448 | tf_op jit(solution)/shard_map/ppermute | solution.py:24
  76.6 3.8 %collective-permute-start.21 = (f32[1,16,320]{2,1,0:T(8,128)S(1)}, f32[1,16,320]{2,1,0:T(8,128)S(1)}, u32[]{:S(2)}, u32[]{:S(2)}) collective-permute-start(f32[1,16,320]{2,1,0:T(8,128)S(1)} %get-tuple-element.98), channel_id=1, source_target_pairs={{8,0},{16,8},{24,16},{0,24},{9,1},{17,9},{25,17},{1,25},{10,2},{18... | collective-permute-start | bytes 61448 | tf_op jit(solution)/shard_map/ppermute | solution.py:25
  80.5 5.2 %collective-permute-start.22 = (f32[18,1,320]{2,1,0:T(1,128)S(1)}, f32[18,1,320]{2,1,0:T(1,128)S(1)}, u32[]{:S(2)}, u32[]{:S(2)}) collective-permute-start(f32[18,1,320]{2,1,0:T(1,128)S(1)} %get-tuple-element.71), channel_id=1, source_target_pairs={{0,1},{1,2},{2,3},{3,4},{4,5},{5,6},{6,7},{7,0},{8,9},{9,10},{10,1... | collective-permute-start | bytes 69128 | tf_op jit(solution)/shard_map/ppermute | solution.py:24
  80.5 5.1 %collective-permute-start.23 = (f32[18,1,320]{2,1,0:T(1,128)S(1)}, f32[18,1,320]{2,1,0:T(1,128)S(1)}, u32[]{:S(2)}, u32[]{:S(2)}) collective-permute-start(f32[18,1,320]{2,1,0:T(1,128)S(1)} %get-tuple-element.72), channel_id=1, source_target_pairs={{1,0},{2,1},{3,2},{4,3},{5,4},{6,5},{7,6},{0,7},{9,8},{10,9},{11,1... | collective-permute-start | bytes 69128 | tf_op jit(solution)/shard_map/ppermute | solution.py:25
  85.8 1.2 copy-start.1
  88.1 4.8 %collective-permute-start.24 = (f32[1,16,320]{2,1,0:T(8,128)S(1)}, f32[1,16,320]{2,1,0:T(8,128)S(1)}, u32[]{:S(2)}, u32[]{:S(2)}) collective-permute-start(f32[1,16,320]{2,1,0:T(8,128)S(1)} %get-tuple-element.95), channel_id=1, source_target_pairs={{0,8},{8,16},{16,24},{24,0},{1,9},{9,17},{17,25},{25,1},{2,10},{10... | collective-permute-start | bytes 61448 | tf_op jit(solution)/shard_map/ppermute | solution.py:24
  90.7 3.8 %collective-permute-start.25 = (f32[1,16,320]{2,1,0:T(8,128)S(1)}, f32[1,16,320]{2,1,0:T(8,128)S(1)}, u32[]{:S(2)}, u32[]{:S(2)}) collective-permute-start(f32[1,16,320]{2,1,0:T(8,128)S(1)} %get-tuple-element.96), channel_id=1, source_target_pairs={{8,0},{16,8},{24,16},{0,24},{9,1},{17,9},{25,17},{1,25},{10,2},{18... | collective-permute-start | bytes 61448 | tf_op jit(solution)/shard_map/ppermute | solution.py:25
  94.6 5.1 %collective-permute-start.26 = (f32[18,1,320]{2,1,0:T(1,128)S(1)}, f32[18,1,320]{2,1,0:T(1,128)S(1)}, u32[]{:S(2)}, u32[]{:S(2)}) collective-permute-start(f32[18,1,320]{2,1,0:T(1,128)S(1)} %get-tuple-element.67), channel_id=1, source_target_pairs={{0,1},{1,2},{2,3},{3,4},{4,5},{5,6},{6,7},{7,0},{8,9},{9,10},{10,1... | collective-permute-start | bytes 69128 | tf_op jit(solution)/shard_map/ppermute | solution.py:24
  94.7 5.1 %collective-permute-start.27 = (f32[18,1,320]{2,1,0:T(1,128)S(1)}, f32[18,1,320]{2,1,0:T(1,128)S(1)}, u32[]{:S(2)}, u32[]{:S(2)}) collective-permute-start(f32[18,1,320]{2,1,0:T(1,128)S(1)} %get-tuple-element.68), channel_id=1, source_target_pairs={{1,0},{2,1},{3,2},{4,3},{5,4},{6,5},{7,6},{0,7},{9,8},{10,9},{11,1... | collective-permute-start | bytes 69128 | tf_op jit(solution)/shard_map/ppermute | solution.py:25
  101.9 5.1 %copy-start.2 = (f32[16,16,256]{2,1,0:T(8,128)}, f32[16,16,256]{2,1,0:T(8,128)S(1)}, u32[]{:S(2)}) copy-start(f32[16,16,256]{2,1,0:T(8,128)S(1)} %fusion.35) | copy-start | bytes 786436
  102.2 4.8 %collective-permute-start.28 = (f32[1,16,320]{2,1,0:T(8,128)S(1)}, f32[1,16,320]{2,1,0:T(8,128)S(1)}, u32[]{:S(2)}, u32[]{:S(2)}) collective-permute-start(f32[1,16,320]{2,1,0:T(8,128)S(1)} %get-tuple-element.93), channel_id=1, source_target_pairs={{0,8},{8,16},{16,24},{24,0},{1,9},{9,17},{17,25},{25,1},{2,10},{10... | collective-permute-start | bytes 61448 | tf_op jit(solution)/shard_map/ppermute | solution.py:24
  103.2 3.8 %collective-permute-start.29 = (f32[1,16,320]{2,1,0:T(8,128)S(1)}, f32[1,16,320]{2,1,0:T(8,128)S(1)}, u32[]{:S(2)}, u32[]{:S(2)}) collective-permute-start(f32[1,16,320]{2,1,0:T(8,128)S(1)} %get-tuple-element.94), channel_id=1, source_target_pairs={{8,0},{16,8},{24,16},{0,24},{9,1},{17,9},{25,17},{1,25},{10,2},{18... | collective-permute-start | bytes 61448 | tf_op jit(solution)/shard_map/ppermute | solution.py:25
  107.7 5.3 %collective-permute-start.30 = (f32[18,1,320]{2,1,0:T(1,128)}, f32[18,1,320]{2,1,0:T(1,128)S(1)}, u32[]{:S(2)}, u32[]{:S(2)}) collective-permute-start(f32[18,1,320]{2,1,0:T(1,128)} %get-tuple-element.63), channel_id=1, source_target_pairs={{0,1},{1,2},{2,3},{3,4},{4,5},{5,6},{6,7},{7,0},{8,9},{9,10},{10,1... | collective-permute-start | bytes 69128 | tf_op jit(solution)/shard_map/ppermute | solution.py:24
  107.7 5.3 %collective-permute-start.31 = (f32[18,1,320]{2,1,0:T(1,128)}, f32[18,1,320]{2,1,0:T(1,128)}, u32[]{:S(2)}, u32[]{:S(2)}) collective-permute-start(f32[18,1,320]{2,1,0:T(1,128)} %get-tuple-element.64), channel_id=1, source_target_pairs={{1,0},{2,1},{3,2},{4,3},{5,4},{6,5},{7,6},{0,7},{9,8},{10,9},{11,1... | collective-permute-start | bytes 69128 | tf_op jit(solution)/shard_map/ppermute | solution.py:25
where the time goes:
time: 119 us
  starting transfers between devices  53.4 us (45%)
  waiting for transfers between devices  30.3 us (25%)
  other arithmetic  19.2 us (16%)
  between operations  8.39 us (7%)
  local copies, waits for them, and re-layouts  7.69 us (6%)
    ppermute x16, starting transfers between devices, with_halo(): after = lax.ppermute(first, axis, down)  38.4 us
    ppermute x16, waiting for transfers between devices, with_halo(): before = lax.ppermute(last, axis, up)  24.7 us
    ppermute x16, starting transfers between devices, with_halo(): before = lax.ppermute(last, axis, up)  15.1 us
    ppermute x16, waiting for transfers between devices, with_halo(): after = lax.ppermute(first, axis, down)  5.59 us
    select_n x4, other arithmetic, shards(): jnp.where(cooled, 0.0, wafer_state[..., :vertical_cells])  4.55 us
    add x4, other arithmetic, substep(): updated_warmth = midpoint_warmth + heat_current + energy_input  4.5 us
  transfers between devices with their start and end apart: 32, of which 22 were waited for; matrix products, arithmetic and copies ran while one was open for 1% of the time, Pallas kernels for 0%

commit v1 on v0

v1 whole, which is shorter than its diff:
```python
import jax
import jax.numpy as jnp
from jax import lax
from jax.experimental import pallas as pl
from jax.experimental.pallas import tpu as pltpu
from jax.sharding import PartitionSpec as P

STEPS = 4
SUBSTEPS = 2
HALO = STEPS * SUBSTEPS

heat_power = 0.5
absorb_depth = 6.0
barrier_energy = 3.0
frequency_multiplier = 0.6
proton_mobility = 0.15

SUB = 8
LANE = 128


def pair_swap(size, first, wraps):
    pairs = []
    for low in range(first, size + first, 2):
        high = low + 1
        if high >= size:
            if not wraps:
                continue
            high -= size
        pairs += [(low, high), (high, low)]
    return pairs


def reciprocal(value):
    guess = pl.reciprocal(value, approx=True)
    return guess * (2.0 - value * guess)


def anneal_kernel(
    place,
    beam,
    keep,
    own,
    scan_a,
    scan_b,
    cross_a,
    cross_b,
    coeff_ref,
    bottom_ref,
    dose_ref,
    inside_ref,
    out,
    nat,
    heat,
    cond,
    acid,
    diff,
    left,
):
    rows, cols, _ = own.shape
    wide_rows, tiles, wide_cols, _ = nat.shape
    z_tiles = tiles - 1
    fine = wide_cols // SUB
    resist = (own.shape[2] - z_tiles * LANE) // 2
    lane = lax.broadcasted_iota(jnp.int32, (SUB, LANE), 1)
    last_lane = lane == LANE - 1
    first_lane = lane == 0
    in_resist = lane < resist
    acid_face = jnp.where(lane < resist - 1, 1.0, 0.0).astype(jnp.float32)

    row_a = pl.multiple_of(place[0], SUB)
    row_b = pl.multiple_of(place[1], SUB)
    col_a = pl.multiple_of(place[2], SUB)
    col_b = pl.multiple_of(place[3], SUB)
    for tile in range(tiles):
        width = min(LANE, scan_a.shape[2] - tile * LANE)
        lanes = slice(tile * LANE, tile * LANE + width)
        mid = slice(HALO, HALO + cols)
        nat[HALO : HALO + rows, tile, mid, :] = own[:, :, tile * LANE : (tile + 1) * LANE]
        nat[pl.ds(row_a, HALO), tile, mid, :width] = scan_a[:, :, lanes]
        nat[pl.ds(row_b, HALO), tile, mid, :width] = scan_b[:, :, lanes]
        nat[:, tile, pl.ds(col_a, HALO), :width] = cross_a[:, :, lanes]
        nat[:, tile, pl.ds(col_b, HALO), :width] = cross_b[:, :, lanes]

    def conductivity(square, z):
        return coeff_ref[z] * reciprocal(4.0 + square)

    def mobility(square):
        return 0.5 * proton_mobility - 0.5 * proton_mobility * reciprocal(1.0 + square)

    def load_row(x, carry):
        for y in range(fine):
            at = pl.ds(y, SUB, stride=fine)
            for z in range(z_tiles):
                warm = nat[x, z, at, :]
                heat[x, y * z_tiles + z] = warm
                square = warm * warm
                cond[x, y * z_tiles + z] = conductivity(square, z)
                if z == 0:
                    diff[x, y] = mobility(square)
            acid[x, y] = jnp.where(in_resist, nat[x, z_tiles, at, :], 0.0)
        return carry

    lax.fori_loop(0, wide_rows, load_row, 0)

    def fill(x, carry):
        for y in range(fine):
            left[x, y] = jnp.ones((SUB, LANE), jnp.float32)
        return carry

    lax.fori_loop(0, rows, fill, 0)

    def face(value, other, factor, other_factor):
        return (factor + other_factor) * (other - value)

    def protect_row(x, carry):
        for y in range(fine):
            warm = heat[x + HALO, y * z_tiles]
            rate = frequency_multiplier * jnp.exp(-barrier_energy * reciprocal(1.0 + warm))
            left[x, y] = left[x, y] * (1.0 - rate * acid[x + HALO, y])
        return carry

    def x_faces(x):
        faces = [
            face(heat[x, i], heat[x + 1, i], cond[x, i], cond[x + 1, i])
            for i in range(fine * z_tiles)
        ]
        acid_faces = [
            face(acid[x, y], acid[x + 1, y], diff[x, y], diff[x + 1, y]) for y in range(fine)
        ]
        return faces, acid_faces

    def substep(step):
        def row(x, carry):
            heat_before, acid_before = carry
            heat_after, acid_after = x_faces(x)
            spot = beam[step * wide_rows + x]
            kept = keep[step * wide_rows + x]

            warm = [heat[x, i] for i in range(fine * z_tiles)]
            cnd = [cond[x, i] for i in range(fine * z_tiles)]
            gain = [heat_after[i] - heat_before[i] for i in range(fine * z_tiles)]
            for z in range(z_tiles):
                own_i = [y * z_tiles + z for y in range(fine)]
                faces = []
                for y in range(fine):
                    i = own_i[y]
                    if y + 1 < fine:
                        j = own_i[y + 1]
                        faces.append(face(warm[i], warm[j], cnd[i], cnd[j]))
                    else:
                        j = own_i[0]
                        faces.append(
                            face(
                                warm[i],
                                pltpu.roll(warm[j], SUB - 1, 0),
                                cnd[i],
                                pltpu.roll(cnd[j], SUB - 1, 0),
                            )
                        )
                before = pltpu.roll(faces[-1], 1, 0)
                for y in range(fine):
                    gain[own_i[y]] += faces[y] - before
                    before = faces[y]
            for y in range(fine):
                ids = [y * z_tiles + z for z in range(z_tiles)]
                rolled = [pltpu.roll(warm[i], LANE - 1, 1) for i in ids] + [0.0]
                rolled_c = [pltpu.roll(cnd[i], LANE - 1, 1) for i in ids] + [bottom_ref[...]]
                before = 0.0
                for z, i in enumerate(ids):
                    below = jnp.where(last_lane, rolled[z + 1], rolled[z])
                    below_c = jnp.where(last_lane, rolled_c[z + 1], rolled_c[z])
                    flow = face(warm[i], below, cnd[i], below_c)
                    turned = pltpu.roll(flow, 1, 1)
                    gain[i] += flow - jnp.where(first_lane, before, turned)
                    before = turned
            gain_a = [acid_after[y] - acid_before[y] for y in range(fine)]
            acd = [acid[x, y] for y in range(fine)]
            dif = [diff[x, y] for y in range(fine)]
            faces = [face(acd[y], acd[y + 1], dif[y], dif[y + 1]) for y in range(fine - 1)]
            faces.append(
                face(
                    acd[-1],
                    pltpu.roll(acd[0], SUB - 1, 0),
                    dif[-1],
                    pltpu.roll(dif[0], SUB - 1, 0),
                )
            )
            before = pltpu.roll(faces[-1], 1, 0)
            for y in range(fine):
                gain_a[y] += faces[y] - before
                before = faces[y]
                flow = acid_face * face(
                    acd[y],
                    pltpu.roll(acd[y], LANE - 1, 1),
                    dif[y],
                    pltpu.roll(dif[y], LANE - 1, 1),
                )
                gain_a[y] += flow - pltpu.roll(flow, 1, 1)
                inside = inside_ref[y]
                acid[x, y] = (acd[y] + gain_a[y]) * inside
                held = inside * kept
                for z in range(z_tiles):
                    i = y * z_tiles + z
                    new = (warm[i] + gain[i] + spot * dose_ref[i]) * held
                    heat[x, i] = new
                    square = new * new
                    cond[x, i] = conductivity(square, z)
                    if z == 0:
                        diff[x, y] = mobility(square)
            return heat_after, acid_after

        lax.fori_loop(0, rows, protect_row, 0, unroll=2)
        lax.fori_loop(step + 1, wide_rows - 1 - step, row, x_faces(step))

    for step in range(HALO):
        substep(step)

    def store_row(x, carry):
        for y in range(fine):
            at = pl.ds(y, SUB, stride=fine)
            for z in range(z_tiles):
                nat[x + HALO, z, at, :] = heat[x + HALO, y * z_tiles + z]
            nat[x + HALO, z_tiles, at, :] = jnp.where(
                in_resist, acid[x + HALO, y], pltpu.roll(left[x, y], resist, 1)
            )
        for z in range(z_tiles):
            out[x, :, z * LANE : (z + 1) * LANE] = nat[x + HALO, z, HALO : HALO + cols, :]
        mixed = nat[x + HALO, z_tiles, HALO : HALO + cols, :]
        start = own[x, :, z_tiles * LANE :]
        which = lax.broadcasted_iota(jnp.int32, mixed.shape, 1) < resist
        out[x, :, z_tiles * LANE :] = jnp.where(which, mixed, mixed * start)
        return carry

    lax.fori_loop(0, rows, store_row, 0)


def shards(wafer_state, layer_heat_coefficients, beam_profile, beam_start, beam_steps):
    rows, cols, depth = wafer_state.shape
    deep = layer_heat_coefficients.shape[0]
    resist = (depth - deep) // 2
    hot = deep + resist
    scan_count, cross_count = lax.axis_size("scan"), lax.axis_size("cross")
    scan_pos, cross_pos = lax.axis_index("scan"), lax.axis_index("cross")
    total_x, total_y = rows * scan_count, cols * cross_count
    wide_rows, wide_cols = rows + 2 * HALO, cols + 2 * HALO
    z_tiles = deep // LANE
    fine = wide_cols // SUB
    odd_x, odd_y = scan_pos % 2, cross_pos % 2

    hot_part = wafer_state[..., :hot]
    far_x, far_y = rows - HALO, cols - HALO
    send_a = lax.dynamic_slice_in_dim(hot_part, (1 - odd_x) * far_x, HALO, 0)
    send_b = lax.dynamic_slice_in_dim(hot_part, odd_x * far_x, HALO, 0)
    scan_b = lax.ppermute(send_b, "scan", pair_swap(scan_count, 1, True))
    scan_a = lax.ppermute(send_a, "scan", pair_swap(scan_count, 0, True))
    before = jnp.where(odd_x == 1, scan_a, scan_b)
    after = jnp.where(odd_x == 1, scan_b, scan_a)
    tall = jnp.concatenate([before, hot_part, after], 0)
    send_a = lax.dynamic_slice_in_dim(tall, (1 - odd_y) * far_y, HALO, 1)
    send_b = lax.dynamic_slice_in_dim(tall, odd_y * far_y, HALO, 1)
    cross_b = lax.ppermute(send_b, "cross", pair_swap(cross_count, 1, False))
    cross_a = lax.ppermute(send_a, "cross", pair_swap(cross_count, 0, False))

    place = jnp.stack(
        [
            (1 - odd_x) * (rows + HALO),
            odd_x * (rows + HALO),
            (1 - odd_y) * (cols + HALO),
            odd_y * (cols + HALO),
        ]
    ).astype(jnp.int32)

    near = jnp.arange(wide_rows, dtype=jnp.int32) - HALO
    spread = float(rows // 2)
    beam, keep = [], []
    for frame in range(STEPS):
        block = jnp.mod(scan_pos - frame, scan_count)
        xcoord = jnp.mod(block * rows + near, total_x)
        kept = jnp.where(xcoord < rows, 0.0, 1.0)
        for sub in range(SUBSTEPS):
            center = (beam_start[frame] + sub * beam_steps[frame]).astype(jnp.float32)
            beam.append(jnp.exp(-jnp.square((xcoord.astype(jnp.float32) - center) / spread)))
            keep.append(kept if sub == SUBSTEPS - 1 else jnp.ones_like(kept))
    beam = jnp.concatenate(beam).astype(jnp.float32)
    keep = jnp.concatenate(keep).astype(jnp.float32)

    def by_column(value):
        value = value.reshape(SUB, fine).T
        return jnp.broadcast_to(value[:, :, None], (fine, SUB, LANE))

    level = jnp.arange(deep, dtype=jnp.float32)
    absorb = jnp.where(level >= resist, jnp.exp(-(level - resist) / absorb_depth), 0.0)
    profile = lax.dynamic_slice_in_dim(
        jnp.pad(beam_profile, (HALO, HALO)), cross_pos * cols, wide_cols
    )
    dose = by_column(heat_power * profile)[:, None] * absorb.reshape(z_tiles, 1, LANE)
    dose = dose.reshape(fine * z_tiles, SUB, LANE)
    places = jnp.arange(wide_cols, dtype=jnp.int32) - HALO + cross_pos * cols
    inside = by_column(jnp.where((places >= 0) & (places < total_y), 1.0, 0.0).astype(jnp.float32))
    coeff = jnp.broadcast_to(
        (2.0 * layer_heat_coefficients).reshape(z_tiles, 1, LANE), (z_tiles, SUB, LANE)
    )
    bottom = jnp.broadcast_to(0.5 * layer_heat_coefficients[-1], (SUB, LANE))

    smem = pl.BlockSpec(memory_space=pltpu.SMEM)
    vmem = pl.BlockSpec(memory_space=pltpu.VMEM)
    result = pl.pallas_call(
        anneal_kernel,
        out_shape=jax.ShapeDtypeStruct(wafer_state.shape, wafer_state.dtype),
        in_specs=[smem] * 3 + [vmem] * 9,
        out_specs=vmem,
        scratch_shapes=[
            pltpu.VMEM((wide_rows, z_tiles + 1, wide_cols, LANE), jnp.float32),
            pltpu.VMEM((wide_rows, fine * z_tiles, SUB, LANE), jnp.float32),
            pltpu.VMEM((wide_rows, fine * z_tiles, SUB, LANE), jnp.float32),
            pltpu.VMEM((wide_rows, fine, SUB, LANE), jnp.float32),
            pltpu.VMEM((wide_rows, fine, SUB, LANE), jnp.float32),
            pltpu.VMEM((rows, fine, SUB, LANE), jnp.float32),
        ],
        compiler_params=pltpu.CompilerParams(vmem_limit_bytes=48 * 2**20),
        name="anneal",
    )(
        place,
        beam,
        keep,
        wafer_state,
        scan_a,
        scan_b,
        cross_a,
        cross_b,
        coeff,
        bottom,
        dose,
        inside,
    )
    lag_blocks = STEPS % scan_count
    if lag_blocks:
        pairs = [(source, (source - lag_blocks) % scan_count) for source in range(scan_count)]
        result = lax.ppermute(result, "scan", pairs)
    return result


def solution(mesh):
    in_specs = (P("scan", "cross", None), P(), P(), P(), P())
    out_specs = P("scan", "cross", None)
    return jax.shard_map(shards, mesh=mesh, in_specs=in_specs, out_specs=out_specs, check_vma=False)
```

time: 119 us -> 67.1 us (0.56)
  the two profiles are of different devices: /device:TPU:0 before, /device:TPU:1 now
where the time goes in v1:
time: 67.1 us; the launch traced here: 66.8 us
  Pallas kernels  38 us (57%)
  between operations  8.47 us (13%)
  starting transfers between devices  7.72 us (12%)
  local copies, waits for them, and re-layouts  6.33 us (9%)
  waiting for transfers between devices  5.81 us (9%)
    pallas_call x1, Pallas kernels, shards(): pl.pallas_call(anneal_kernel, out_shape=jax.ShapeDtypeStruct(wafer_state....  38 us
    ppermute x1, waiting for transfers between devices, shards(): cross_b = lax.ppermute(send_b, 'cross', pair_swap(cross_count, 1, False))  5.81 us
    ppermute x1, starting transfers between devices, shards(): cross_b = lax.ppermute(send_b, 'cross', pair_swap(cross_count, 1, False))  3.1 us
    unnamed x10, local copies, waits for them, and re-layouts  2.91 us
    ppermute x1, starting transfers between devices, shards(): scan_a = lax.ppermute(send_a, 'scan', pair_swap(scan_count, 0, True))  2.11 us
  transfers between devices with their start and end apart: 4, of which 1 were waited for; matrix products, arithmetic and copies ran while one was open for 4% of the time, Pallas kernels for 0%

profile of v1, /device:TPU:1, one launch (start us, length us, event | category | flops | bytes accessed | tf_op | source)
XLA Modules:
  0.0 66.8 jit_solution(3298063198637853663)
XLA Ops:
  0.0 1.0 %constant_dynamic-slice_fusion.2 = (f32[8,16,320]{2,1,0:T(8,128)S(1)}, f32[8,16,320]{2,1,0:T(8,128)S(1)}) fusion(f32[16,16,320]{2,1,0:T(8,128)} %bitcast.19, s32[]{:T(128)S(6)} %select_n.113, s32[]{:T(128)S(6)} %select_n.112), kind=kLoop, calls=%fused_computation.30 | loop fusion | bytes 655368 | tf_op jit(solution)/shard_map/dynamic_slice | solution.py:254
  1.1 2.1 %collective-permute-start = (f32[8,16,320]{2,1,0:T(8,128)S(1)}, f32[8,16,320]{2,1,0:T(8,128)S(1)}, u32[]{:S(2)}, u32[]{:S(2)}) collective-permute-start(f32[8,16,320]{2,1,0:T(8,128)S(1)} %get-tuple-element.10), channel_id=1, source_target_pairs={{0,8},{8,0},{16,24},{24,16},{1,9},{9,1},{17,25},{25,17},{2,10},{10... | collective-permute-start | bytes 491528 | tf_op jit(solution)/shard_map/ppermute | solution.py:256
  3.2 1.2 %collective-permute-start.1 = (f32[8,16,320]{2,1,0:T(8,128)S(1)}, f32[8,16,320]{2,1,0:T(8,128)S(1)}, u32[]{:S(2)}, u32[]{:S(2)}) collective-permute-start(f32[8,16,320]{2,1,0:T(8,128)S(1)} %get-tuple-element.9), channel_id=1, source_target_pairs={{8,16},{16,8},{24,0},{0,24},{9,17},{17,9},{25,1},{1,25},{10,18},{1... | collective-permute-start | bytes 491528 | tf_op jit(solution)/shard_map/ppermute | solution.py:255
  4.4 0.0 copy-start.2
  4.4 0.0 copy-start.1
  4.4 0.7 copy-done.1
  5.0 0.7 fusion.10
  5.7 0.0 copy-done.2
  5.7 0.6 fusion.9
  14.1 0.0 copy-start.3
  14.1 0.7 %copy-done.3 = f32[256]{0:T(256)S(1)} copy-done((f32[256]{0:T(256)S(1)}, f32[256]{0:T(256)}, u32[]{:S(2)}) %copy-start.3) | copy-done | bytes 1048
  14.9 0.0 copy-start.4
  14.9 0.6 copy-done.4
  15.5 0.1 fusion.4
  15.6 0.6 slice.43
  16.2 0.1 reshape.39
  16.3 0.1 copy.7
  17.0 0.1 concatenate.10.keep
  17.1 0.1 concatenate.9.beam
  17.2 0.0 copy-start
  17.2 0.0 collective-permute-done.scan_a
  17.2 0.0 collective-permute-done.1.scan_b
  17.3 0.9 %copy-done = f32[16,16,384]{2,1,0:T(8,128)S(1)} copy-done((f32[16,16,384]{2,1,0:T(8,128)S(1)}, f32[16,16,384]{2,1,0:T(8,128)}, u32[]{:S(2)}) %copy-start) | copy-done | bytes 393240
  18.2 0.1 pad_maximum_fusion
  18.3 0.1 constant_dynamic-slice_fusion
  18.3 1.3 %collective-permute-start.2 = (f32[32,8,320]{2,1,0:T(8,128)S(1)}, f32[32,8,320]{2,1,0:T(8,128)S(1)}, u32[]{:S(2)}, u32[]{:S(2)}) collective-permute-start(f32[32,8,320]{2,1,0:T(8,128)S(1)} %get-tuple-element.6), channel_id=1, source_target_pairs={{0,1},{1,0},{2,3},{3,2},{4,5},{5,4},{6,7},{7,6},{8,9},{9,8},{10,11... | collective-permute-start | bytes 983048 | tf_op jit(solution)/shard_map/ppermute | solution.py:263
  19.6 3.1 %collective-permute-start.3 = (f32[32,8,320]{2,1,0:T(8,128)S(1)}, f32[32,8,320]{2,1,0:T(8,128)S(1)}, u32[]{:S(2)}, u32[]{:S(2)}) collective-permute-start(f32[32,8,320]{2,1,0:T(8,128)S(1)} %get-tuple-element.5), channel_id=1, source_target_pairs={{1,2},{2,1},{3,4},{4,3},{5,6},{6,5},{9,10},{10,9},{11,12},{12,11},... | collective-permute-start | bytes 983048 | tf_op jit(solution)/shard_map/ppermute | solution.py:262
  22.8 0.1 pad_add_fusion.place
  22.8 0.1 broadcast_multiply_fusion.dose_ref
  22.9 0.0 collective-permute-done.2.cross_a
  22.9 5.8 %collective-permute-done.3.cross_b = f32[32,8,320]{2,1,0:T(8,128)S(1)} collective-permute-done((f32[32,8,320]{2,1,0:T(8,128)S(1)}, f32[32,8,320]{2,1,0:T(8,128)S(1)}, u32[]{:S(2)}, u32[]{:S(2)}) %collective-permute-start.3) | collective-permute-done | bytes 327712 | tf_op jit(solution)/shard_map/ppermute | solution.py:262
  28.7 0.1 broadcast_in_dim.40.inside_ref
  28.8 38.0 %anneal.1 = f32[16,16,384]{2,1,0:T(8,128)} custom-call(s32[4]{0:T(128)S(1)} %pad_add_fusion.place, f32[256]{0:T(256)S(1)} %concatenate.9.beam, f32[256]{0:T(256)S(1)} %concatenate.10.keep, f32[16,16,384]{2,1,0:T(8,128)S(1)} %copy-done, f32[8,16,320]{2,1,0:T(8,128)S(1)} %collective-permute-done.scan_a, f32[8,16,320]{2,1,0:T(8,128)S(1)} %collective-permute-done.1.scan_b, ...), custom_call_target="tpu_custom_call" | custom-call | tf_op jit(solution)/shard_map/anneal/pallas_call | solution.py:308
  (15 shorter events, 0.2 us)
Async XLA Ops:
  1.1 16.2 %collective-permute-start = (f32[8,16,320]{2,1,0:T(8,128)S(1)}, f32[8,16,320]{2,1,0:T(8,128)S(1)}, u32[]{:S(2)}, u32[]{:S(2)}) collective-permute-start(f32[8,16,320]{2,1,0:T(8,128)S(1)} %get-tuple-element.10), channel_id=1, source_target_pairs={{0,8},{8,0},{16,24},{24,16},{1,9},{9,1},{17,25},{25,17},{2,10},{10... | collective-permute-start | bytes 491528 | tf_op jit(solution)/shard_map/ppermute | solution.py:256
  3.2 14.1 %collective-permute-start.1 = (f32[8,16,320]{2,1,0:T(8,128)S(1)}, f32[8,16,320]{2,1,0:T(8,128)S(1)}, u32[]{:S(2)}, u32[]{:S(2)}) collective-permute-start(f32[8,16,320]{2,1,0:T(8,128)S(1)} %get-tuple-element.9), channel_id=1, source_target_pairs={{8,16},{16,8},{24,0},{0,24},{9,17},{17,9},{25,1},{1,25},{10,18},{1... | collective-permute-start | bytes 491528 | tf_op jit(solution)/shard_map/ppermute | solution.py:255
  4.4 1.3 %copy-start.2 = (s32[4]{0:T(128)S(1)}, s32[4]{0:T(128)}, u32[]{:S(2)}) copy-start(s32[4]{0:T(128)} %param.9) | copy-start | bytes 52
  4.4 0.7 copy-start.1
  14.1 0.7 %copy-start.3 = (f32[256]{0:T(256)S(1)}, f32[256]{0:T(256)}, u32[]{:S(2)}) copy-start(f32[256]{0:T(256)} %param.6) | copy-start | bytes 3076
  14.9 0.7 copy-start.4
  17.2 1.0 %copy-start = (f32[16,16,384]{2,1,0:T(8,128)S(1)}, f32[16,16,384]{2,1,0:T(8,128)}, u32[]{:S(2)}) copy-start(f32[16,16,384]{2,1,0:T(8,128)} %own.1) | copy-start | bytes 1179652
  18.3 4.6 %collective-permute-start.2 = (f32[32,8,320]{2,1,0:T(8,128)S(1)}, f32[32,8,320]{2,1,0:T(8,128)S(1)}, u32[]{:S(2)}, u32[]{:S(2)}) collective-permute-start(f32[32,8,320]{2,1,0:T(8,128)S(1)} %get-tuple-element.6), channel_id=1, source_target_pairs={{0,1},{1,0},{2,3},{3,2},{4,5},{5,4},{6,7},{7,6},{8,9},{9,8},{10,11... | collective-permute-start | bytes 983048 | tf_op jit(solution)/shard_map/ppermute | solution.py:263
  19.6 9.1 %collective-permute-start.3 = (f32[32,8,320]{2,1,0:T(8,128)S(1)}, f32[32,8,320]{2,1,0:T(8,128)S(1)}, u32[]{:S(2)}, u32[]{:S(2)}) collective-permute-start(f32[32,8,320]{2,1,0:T(8,128)S(1)} %get-tuple-element.5), channel_id=1, source_target_pairs={{1,2},{2,1},{3,4},{4,3},{5,6},{6,5},{9,10},{10,9},{11,12},{12,11},... | collective-permute-start | bytes 983048 | tf_op jit(solution)/shard_map/ppermute | solution.py:262

commit v2 on v1

v2 whole, which is shorter than its diff:
```python
import jax
import jax.numpy as jnp
from jax import lax
from jax.experimental import pallas as pl
from jax.experimental.pallas import tpu as pltpu
from jax.sharding import PartitionSpec as P

STEPS = 4
SUBSTEPS = 2
HALO = STEPS * SUBSTEPS
UNROLL = 2

heat_power = 0.5
absorb_depth = 6.0
barrier_energy = 3.0
frequency_multiplier = 0.6
proton_mobility = 0.15

SUB = 8
LANE = 128


def pair_swap(size, first, wraps):
    pairs = []
    for low in range(first, size + first, 2):
        high = low + 1
        if high >= size:
            if not wraps:
                continue
            high -= size
        pairs += [(low, high), (high, low)]
    return pairs


def reciprocal(value):
    return pltpu.reciprocal(value, approx=True)


def anneal_kernel(
    place,
    beam,
    keep,
    own,
    scan_a,
    scan_b,
    cross_a,
    cross_b,
    coeff_ref,
    under_ref,
    dose_ref,
    inside_ref,
    out,
    nat,
    heat,
    cond,
    acid,
    diff,
    soft,
    left,
    part,
    deep,
    flow,
):
    rows, cols, _ = own.shape
    wide_rows, tiles, wide_cols, _ = nat.shape
    pairs = wide_rows // 2
    z_tiles = tiles - 1
    fine = wide_cols // SUB
    resist = (own.shape[2] - z_tiles * LANE) // 2
    edge_cols = {(HALO - 1) % fine, (HALO + cols) % fine}
    lane = lax.broadcasted_iota(jnp.int32, (SUB, LANE), 1)
    last_lane = lane == LANE - 1
    first_lane = lane == 0
    in_first = lane < resist
    acid_face = jnp.where(lane % resist == resist - 1, 0.0, 1.0).astype(jnp.float32)

    def at(side, y, z):
        return (side * fine + y) * z_tiles + z

    def turn(value):
        return pltpu.roll(value, resist, 1)

    row_a = pl.multiple_of(place[0], SUB)
    row_b = pl.multiple_of(place[1], SUB)
    col_a = pl.multiple_of(place[2], SUB)
    col_b = pl.multiple_of(place[3], SUB)
    for tile in range(tiles):
        width = min(LANE, scan_a.shape[2] - tile * LANE)
        lanes = slice(tile * LANE, tile * LANE + width)
        mid = slice(HALO, HALO + cols)
        nat[HALO : HALO + rows, tile, mid, :] = own[:, :, tile * LANE : (tile + 1) * LANE]
        nat[pl.ds(row_a, HALO), tile, mid, :width] = scan_a[:, :, lanes]
        nat[pl.ds(row_b, HALO), tile, mid, :width] = scan_b[:, :, lanes]
        nat[:, tile, pl.ds(col_a, HALO), :width] = cross_a[:, :, lanes]
        nat[:, tile, pl.ds(col_b, HALO), :width] = cross_b[:, :, lanes]

    def conductivity(warm, z):
        return coeff_ref[z] * reciprocal(4.0 + warm * warm)

    def mobility(warm):
        return 0.5 * proton_mobility - 0.5 * proton_mobility * reciprocal(1.0 + warm * warm)

    def load_pair(x, carry):
        row = (x, wide_rows - 1 - x)
        for y in range(fine):
            take = pl.ds(y, SUB, stride=fine)
            for z in range(z_tiles):
                for side in range(2):
                    warm = nat[row[side], z, take, :]
                    heat[x + 1, at(side, y, z)] = warm
                    cond[x + 1, at(side, y, z)] = conductivity(warm, z)
            warm = jnp.where(
                in_first, nat[row[0], 0, take, :], turn(nat[row[1], 0, take, :])
            )
            soft[x + 1, y] = warm
            diff[x + 1, y] = mobility(warm)
            acid[x + 1, y] = jnp.where(
                in_first, nat[row[0], z_tiles, take, :], turn(nat[row[1], z_tiles, take, :])
            )
        return carry

    for ref in (heat, cond, acid, diff, soft):
        for i in range(ref.shape[1]):
            for x in (0, pairs + 2):
                ref[x, i] = jnp.zeros((SUB, LANE), jnp.float32)
    lax.fori_loop(0, pairs, load_pair, 0)

    def fill(x, carry):
        for y in range(fine):
            left[x, y] = jnp.ones((SUB, LANE), jnp.float32)
        return carry

    lax.fori_loop(0, pairs - HALO, fill, 0)

    def face(value, other, factor, other_factor):
        return (factor + other_factor) * (other - value)

    def protect_pair(x, carry):
        for y in range(fine):
            warm = soft[x + HALO + 1, y]
            rate = frequency_multiplier * jnp.exp(-barrier_energy * reciprocal(1.0 + warm))
            left[x, y] = left[x, y] * (1.0 - rate * acid[x + HALO + 1, y])
        return carry

    def window(x):
        return [ref.at[pl.ds(x, UNROLL + 3)] for ref in (heat, cond, acid, diff, soft)]

    def x_faces(near, k):
        heat, cond, acid, diff, _ = near
        faces = [
            face(heat[k, i], heat[k + 1, i], cond[k, i], cond[k + 1, i])
            for i in range(2 * fine * z_tiles)
        ]
        acid_faces = [
            face(acid[k, y], acid[k + 1, y], diff[k, y], diff[k + 1, y]) for y in range(fine)
        ]
        return faces + acid_faces

    def y_gain(value, factor):
        faces = [
            face(value[y], value[y + 1], factor[y], factor[y + 1]) for y in range(fine - 1)
        ]
        faces.append(
            face(
                value[-1],
                pltpu.roll(value[0], SUB - 1, 0),
                factor[-1],
                pltpu.roll(factor[0], SUB - 1, 0),
            )
        )
        before = [pltpu.roll(faces[-1], 1, 0)] + faces[:-1]
        return [after - b for after, b in zip(faces, before)]

    def z_faces(value, factor):
        rolled = [pltpu.roll(v, LANE - 1, 1) for v in value] + [0.0]
        faces = []
        for z in range(z_tiles):
            below = jnp.where(last_lane, rolled[z + 1], rolled[z])
            below_f = under_ref[z] * reciprocal(4.0 + below * below)
            faces.append(face(value[z], below, factor[z], below_f))
        return faces

    def z_gain(faces):
        gain, before = [], 0.0
        for face_flow in faces:
            turned = pltpu.roll(face_flow, 1, 1)
            gain.append(face_flow - jnp.where(first_lane, before, turned))
            before = turned
        return gain

    def substep(step, cooling):
        for i in range(2 * fine * z_tiles):
            j = (i + fine * z_tiles) % (2 * fine * z_tiles)
            heat[pairs + 1, i] = heat[pairs, j]
            cond[pairs + 1, i] = cond[pairs, j]
        for y in range(fine):
            acid[pairs + 1, y] = turn(acid[pairs, y])
            diff[pairs + 1, y] = turn(diff[pairs, y])

        def sink(near, k):
            heat, cond, acid, diff, _ = near
            for side in range(2):
                for y in range(fine):
                    ids = [at(side, y, z) for z in range(z_tiles)]
                    faces = z_faces([heat[k, i] for i in ids], [cond[k, i] for i in ids])
                    for i, value in zip(ids, faces):
                        deep[i] = value
            for y in range(fine):
                acd, dif = acid[k, y], diff[k, y]
                deep[2 * fine * z_tiles + y] = acid_face * face(
                    acd, pltpu.roll(acd, LANE - 1, 1), dif, pltpu.roll(dif, LANE - 1, 1)
                )

        def gather(near, k, x):
            heat, cond, acid, diff, _ = near
            for side in range(2):
                row = x if side == 0 else wide_rows - 1 - x
                spot = beam[step * wide_rows + row]
                warm = [
                    [heat[k, at(side, y, z)] for z in range(z_tiles)] for y in range(fine)
                ]
                cnd = [[cond[k, at(side, y, z)] for z in range(z_tiles)] for y in range(fine)]
                across = [
                    y_gain([w[z] for w in warm], [c[z] for c in cnd]) for z in range(z_tiles)
                ]
                for y in range(fine):
                    down = z_gain([deep[at(side, y, z)] for z in range(z_tiles)])
                    for z in range(z_tiles):
                        new = warm[y][z] + spot * dose_ref[y * z_tiles + z]
                        part[at(side, y, z)] = new + across[z][y] + down[z]
            acd = [acid[k, y] for y in range(fine)]
            dif = [diff[k, y] for y in range(fine)]
            across = y_gain(acd, dif)
            for y in range(fine):
                i = 2 * fine * z_tiles + y
                down = deep[i]
                part[i] = acd[y] + across[y] + (down - pltpu.roll(down, 1, 1))

        def soften(near, k):
            heat, _, _, diff, soft = near
            for y in range(fine):
                warm = jnp.where(
                    in_first, heat[k, at(0, y, 0)], turn(heat[k, at(1, y, 0)])
                )
                soft[k, y] = warm
                diff[k, y] = mobility(warm)

        def finish(near, k, x, before):
            heat, cond, acid, _, _ = near
            after = x_faces(near, k)
            for side in range(2):
                row = x if side == 0 else wide_rows - 1 - x
                kept = keep[step * wide_rows + row]
                for y in range(fine):
                    for z in range(z_tiles):
                        i = at(side, y, z)
                        new = part[i] + (after[i] - before[i])
                        if cooling:
                            new = new * kept
                        if y in edge_cols:
                            new = new * inside_ref[y]
                        heat[k, i] = new
                        cond[k, i] = conductivity(new, z)
            for y in range(fine):
                i = 2 * fine * z_tiles + y
                new = part[i] + (after[i] - before[i])
                if y in edge_cols:
                    new = new * inside_ref[y]
                acid[k, y] = new
            return after

        def some_pairs(number, carry):
            x = begin + number * UNROLL
            near = window(x)
            before = [flow[i] for i in range(flow.shape[0])]
            for ahead in range(UNROLL):
                k = ahead + 1
                before = finish(near, k, x + ahead, before)
                gather(near, k + 1, x + ahead + 1)
                sink(near, k + 2)
                soften(near, k - 1)
            for i, value in enumerate(before):
                flow[i] = value
            return carry

        lax.fori_loop(0, pairs - HALO, protect_pair, 0, unroll=pairs - HALO)
        count = (pairs - 1 - step + UNROLL - 1) // UNROLL
        begin = pairs - count * UNROLL
        first = window(begin)
        sink(first, 1)
        gather(first, 1, begin)
        sink(first, 2)
        for i, value in enumerate(x_faces(first, 0)):
            flow[i] = value
        lax.fori_loop(0, count, some_pairs, 0)
        soften(window(pairs - 1), 1)

    def frame(number, carry):
        for sub in range(SUBSTEPS):
            substep(number * SUBSTEPS + sub, sub == SUBSTEPS - 1)
        return carry

    lax.fori_loop(0, STEPS, frame, 0)

    def store_pair(x, carry):
        row = (x + HALO, wide_rows - 1 - HALO - x)
        for y in range(fine):
            put = pl.ds(y, SUB, stride=fine)
            for side in range(2):
                for z in range(z_tiles):
                    nat[row[side], z, put, :] = heat[x + HALO + 1, at(side, y, z)]
            acd, kept = acid[x + HALO + 1, y], left[x, y]
            nat[row[0], z_tiles, put, :] = jnp.where(in_first, acd, turn(kept))
            nat[row[1], z_tiles, put, :] = jnp.where(in_first, turn(acd), kept)
        for side in range(2):
            here = row[side] - HALO
            for z in range(z_tiles):
                out[here, :, z * LANE : (z + 1) * LANE] = nat[
                    row[side], z, HALO : HALO + cols, :
                ]
            mixed = nat[row[side], z_tiles, HALO : HALO + cols, :]
            start = own[here, :, z_tiles * LANE :]
            which = lax.broadcasted_iota(jnp.int32, mixed.shape, 1) < resist
            out[here, :, z_tiles * LANE :] = jnp.where(which, mixed, mixed * start)
        return carry

    lax.fori_loop(0, pairs - HALO, store_pair, 0)


def shards(wafer_state, layer_heat_coefficients, beam_profile, beam_start, beam_steps):
    rows, cols, depth = wafer_state.shape
    deep = layer_heat_coefficients.shape[0]
    resist = (depth - deep) // 2
    hot = deep + resist
    scan_count, cross_count = lax.axis_size("scan"), lax.axis_size("cross")
    scan_pos, cross_pos = lax.axis_index("scan"), lax.axis_index("cross")
    total_x, total_y = rows * scan_count, cols * cross_count
    wide_rows, wide_cols = rows + 2 * HALO, cols + 2 * HALO
    z_tiles = deep // LANE
    fine = wide_cols // SUB
    pairs = wide_rows // 2
    odd_x, odd_y = scan_pos % 2, cross_pos % 2

    hot_part = wafer_state[..., :hot]
    far_x, far_y = rows - HALO, cols - HALO
    send_a = lax.dynamic_slice_in_dim(hot_part, (1 - odd_x) * far_x, HALO, 0)
    send_b = lax.dynamic_slice_in_dim(hot_part, odd_x * far_x, HALO, 0)
    scan_b = lax.ppermute(send_b, "scan", pair_swap(scan_count, 1, True))
    scan_a = lax.ppermute(send_a, "scan", pair_swap(scan_count, 0, True))
    before = jnp.where(odd_x == 1, scan_a, scan_b)
    after = jnp.where(odd_x == 1, scan_b, scan_a)
    tall = jnp.concatenate([before, hot_part, after], 0)
    send_a = lax.dynamic_slice_in_dim(tall, (1 - odd_y) * far_y, HALO, 1)
    send_b = lax.dynamic_slice_in_dim(tall, odd_y * far_y, HALO, 1)
    cross_b = lax.ppermute(send_b, "cross", pair_swap(cross_count, 1, False))
    cross_a = lax.ppermute(send_a, "cross", pair_swap(cross_count, 0, False))

    place = jnp.stack(
        [
            (1 - odd_x) * (rows + HALO),
            odd_x * (rows + HALO),
            (1 - odd_y) * (cols + HALO),
            odd_y * (cols + HALO),
        ]
    ).astype(jnp.int32)

    near = jnp.arange(wide_rows, dtype=jnp.int32) - HALO
    spread = float(rows // 2)
    beam, keep = [], []
    for frame in range(STEPS):
        block = jnp.mod(scan_pos - frame, scan_count)
        xcoord = jnp.mod(block * rows + near, total_x)
        kept = jnp.where(xcoord < rows, 0.0, 1.0)
        for sub in range(SUBSTEPS):
            center = (beam_start[frame] + sub * beam_steps[frame]).astype(jnp.float32)
            beam.append(jnp.exp(-jnp.square((xcoord.astype(jnp.float32) - center) / spread)))
            keep.append(kept if sub == SUBSTEPS - 1 else jnp.ones_like(kept))
    beam = jnp.concatenate(beam).astype(jnp.float32)
    keep = jnp.concatenate(keep).astype(jnp.float32)

    def by_column(value):
        value = value.reshape(SUB, fine).T
        return jnp.broadcast_to(value[:, :, None], (fine, SUB, LANE))

    level = jnp.arange(deep, dtype=jnp.float32)
    absorb = jnp.where(level >= resist, jnp.exp(-(level - resist) / absorb_depth), 0.0)
    profile = lax.dynamic_slice_in_dim(
        jnp.pad(beam_profile, (HALO, HALO)), cross_pos * cols, wide_cols
    )
    dose = by_column(heat_power * profile)[:, None] * absorb.reshape(z_tiles, 1, LANE)
    dose = dose.reshape(fine * z_tiles, SUB, LANE)
    places = jnp.arange(wide_cols, dtype=jnp.int32) - HALO + cross_pos * cols
    inside = by_column(jnp.where((places >= 0) & (places < total_y), 1.0, 0.0).astype(jnp.float32))
    coeff = jnp.broadcast_to(
        (2.0 * layer_heat_coefficients).reshape(z_tiles, 1, LANE), (z_tiles, SUB, LANE)
    )
    under = jnp.concatenate([layer_heat_coefficients[1:], layer_heat_coefficients[-1:]])
    under = jnp.broadcast_to((2.0 * under).reshape(z_tiles, 1, LANE), (z_tiles, SUB, LANE))

    smem = pl.BlockSpec(memory_space=pltpu.SMEM)
    vmem = pl.BlockSpec(memory_space=pltpu.VMEM)
    result = pl.pallas_call(
        anneal_kernel,
        out_shape=jax.ShapeDtypeStruct(wafer_state.shape, wafer_state.dtype),
        in_specs=[smem] * 3 + [vmem] * 9,
        out_specs=vmem,
        scratch_shapes=[
            pltpu.VMEM((wide_rows, z_tiles + 1, wide_cols, LANE), jnp.float32),
            pltpu.VMEM((pairs + 4, 2 * fine * z_tiles, SUB, LANE), jnp.float32),
            pltpu.VMEM((pairs + 4, 2 * fine * z_tiles, SUB, LANE), jnp.float32),
            pltpu.VMEM((pairs + 4, fine, SUB, LANE), jnp.float32),
            pltpu.VMEM((pairs + 4, fine, SUB, LANE), jnp.float32),
            pltpu.VMEM((pairs + 4, fine, SUB, LANE), jnp.float32),
            pltpu.VMEM((pairs - HALO, fine, SUB, LANE), jnp.float32),
            pltpu.VMEM(((2 * z_tiles + 1) * fine, SUB, LANE), jnp.float32),
            pltpu.VMEM(((2 * z_tiles + 1) * fine, SUB, LANE), jnp.float32),
            pltpu.VMEM(((2 * z_tiles + 1) * fine, SUB, LANE), jnp.float32),
        ],
        compiler_params=pltpu.CompilerParams(vmem_limit_bytes=48 * 2**20),
        name="anneal",
    )(
        place,
        beam,
        keep,
        wafer_state,
        scan_a,
        scan_b,
        cross_a,
        cross_b,
        coeff,
        under,
        dose,
        inside,
    )
    lag_blocks = STEPS % scan_count
    if lag_blocks:
        pairs = [(source, (source - lag_blocks) % scan_count) for source in range(scan_count)]
        result = lax.ppermute(result, "scan", pairs)
    return result


def solution(mesh):
    in_specs = (P("scan", "cross", None), P(), P(), P(), P())
    out_specs = P("scan", "cross", None)
    return jax.shard_map(shards, mesh=mesh, in_specs=in_specs, out_specs=out_specs, check_vma=False)
```

time: 67.1 us -> 44.6 us (0.66)
  Pallas kernels: 38 us -> 15.5 us
  between operations: 8.47 us -> 7.55 us
  other arithmetic: 0.46 us -> 1.24 us
    pallas_call x1, Pallas kernels: 38 us -> 15.5 us  [shards(): pl.pallas_call(anneal_kernel, out_shape=jax.ShapeDtypeStruct(wafer_state....]
    mul x0 -> x1, other arithmetic: none -> 0.77 us  [shards(): 2.0 * under]
  transfers between devices with their start and end apart: 4 -> 4, of which waited for: 1 -> 1; matrix products, arithmetic and copies ran while one was open for 4% -> 8% of each run, Pallas kernels for 0% -> 0%
where the time goes in v2:
time: 44.6 us; the launch traced here: 44.3 us
  Pallas kernels  15.5 us (35%)
  starting transfers between devices  7.72 us (17%)
  between operations  7.55 us (17%)
  local copies, waits for them, and re-layouts  6.43 us (14%)
  waiting for transfers between devices  5.81 us (13%)
  other arithmetic  1.24 us (3%)
    pallas_call x1, Pallas kernels, shards(): pl.pallas_call(anneal_kernel, out_shape=jax.ShapeDtypeStruct(wafer_state....  15.5 us
    ppermute x1, waiting for transfers between devices, shards(): cross_b = lax.ppermute(send_b, 'cross', pair_swap(cross_count, 1, False))  5.81 us
    ppermute x1, starting transfers between devices, shards(): cross_b = lax.ppermute(send_b, 'cross', pair_swap(cross_count, 1, False))  3.1 us
    unnamed x10, local copies, waits for them, and re-layouts  2.92 us
    ppermute x1, starting transfers between devices, shards(): scan_a = lax.ppermute(send_a, 'scan', pair_swap(scan_count, 0, True))  2.11 us
    ppermute x1, starting transfers between devices, shards(): cross_a = lax.ppermute(send_a, 'cross', pair_swap(cross_count, 0, False))  1.3 us
    slice x2, local copies, waits for them, and re-layouts, shards(): center = (beam_start[frame] + sub * beam_steps[frame]).astype(jnp.float32)  1.27 us
    ppermute x1, starting transfers between devices, shards(): scan_b = lax.ppermute(send_b, 'scan', pair_swap(scan_count, 1, True))  1.21 us
  transfers between devices with their start and end apart: 4, of which 1 were waited for; matrix products, arithmetic and copies ran while one was open for 8% of the time, Pallas kernels for 0%

profile of v2, /device:TPU:1, one launch (start us, length us, event | category | flops | bytes accessed | tf_op | source)
XLA Modules:
  0.0 44.3 jit_solution(8560919740828647880)
XLA Ops:
  0.0 1.0 %constant_dynamic-slice_fusion.2 = (f32[8,16,320]{2,1,0:T(8,128)S(1)}, f32[8,16,320]{2,1,0:T(8,128)S(1)}) fusion(f32[16,16,320]{2,1,0:T(8,128)} %bitcast.20, s32[]{:T(128)S(6)} %select_n.113, s32[]{:T(128)S(6)} %select_n.112), kind=kLoop, calls=%fused_computation.32 | loop fusion | bytes 655368 | tf_op jit(solution)/shard_map/dynamic_slice | solution.py:347
  1.1 2.1 %collective-permute-start = (f32[8,16,320]{2,1,0:T(8,128)S(1)}, f32[8,16,320]{2,1,0:T(8,128)S(1)}, u32[]{:S(2)}, u32[]{:S(2)}) collective-permute-start(f32[8,16,320]{2,1,0:T(8,128)S(1)} %get-tuple-element.10), channel_id=1, source_target_pairs={{0,8},{8,0},{16,24},{24,16},{1,9},{9,1},{17,25},{25,17},{2,10},{10... | collective-permute-start | bytes 491528 | tf_op jit(solution)/shard_map/ppermute | solution.py:349
  3.2 1.2 %collective-permute-start.1 = (f32[8,16,320]{2,1,0:T(8,128)S(1)}, f32[8,16,320]{2,1,0:T(8,128)S(1)}, u32[]{:S(2)}, u32[]{:S(2)}) collective-permute-start(f32[8,16,320]{2,1,0:T(8,128)S(1)} %get-tuple-element.9), channel_id=1, source_target_pairs={{8,16},{16,8},{24,0},{0,24},{9,17},{17,9},{25,1},{1,25},{10,18},{1... | collective-permute-start | bytes 491528 | tf_op jit(solution)/shard_map/ppermute | solution.py:348
  4.4 0.0 copy-start.3
  4.4 0.7 %copy-done.3 = f32[256]{0:T(256)S(1)} copy-done((f32[256]{0:T(256)S(1)}, f32[256]{0:T(256)}, u32[]{:S(2)}) %copy-start.3) | copy-done | bytes 1048
  5.1 0.7 %slice.47 = f32[1]{0:T(128)} slice(f32[256]{0:T(256)S(1)} %copy-done.3), slice={[255:256]} | slice | bytes 8 | tf_op jit(solution)/shard_map/slice | solution.py:397
  5.7 0.1 slice.46
  5.8 0.0 copy-start.2
  5.8 0.0 copy-start.1
  5.8 0.7 %copy-done.1 = s32[4]{0:T(128)S(1)} copy-done((s32[4]{0:T(128)S(1)}, s32[4]{0:T(128)}, u32[]{:S(2)}) %copy-start.1) | copy-done | bytes 40
  6.5 0.6 %fusion.11 = (s32[1]{0:T(128)}, s32[1]{0:T(128)}, s32[1]{0:T(128)}, s32[1]{0:T(128)}) fusion(s32[4]{0:T(128)S(1)} %copy-done.1), kind=kLoop, calls=%fused_computation.50 | loop fusion | bytes 32 | tf_op jit(solution)/shard_map/slice | solution.py:375
  7.1 0.0 copy-done.2
  7.1 0.7 %fusion.10 = (s32[1]{0:T(128)}, s32[1]{0:T(128)}, s32[1]{0:T(128)}, s32[1]{0:T(128)}) fusion(s32[4]{0:T(128)S(1)} %copy-done.2), kind=kLoop, calls=%fused_computation.49 | loop fusion | bytes 32 | tf_op jit(solution)/shard_map/slice | solution.py:375
  15.3 0.8 %fusion.4 = f32[2,128]{1,0:T(2,128)S(1)} fusion(f32[1]{0:T(128)} %slice.47, f32[255]{0:T(256)S(1)} %slice.46), kind=kLoop, calls=%fused_computation.27 | loop fusion | flops 512 | bytes 2048 | tf_op jit(solution)/shard_map/mul | solution.py:398
  16.1 0.0 copy-start.4
  16.1 0.7 %copy-done.4 = f32[128]{0:T(128)S(1)} copy-done((f32[128]{0:T(128)S(1)}, f32[128]{0:T(128)}, u32[]{:S(2)}) %copy-start.4) | copy-done | bytes 536
  16.8 0.1 fusion.5
  16.8 0.1 reshape.45
  16.9 0.1 copy.7
  17.0 0.1 concatenate.13.keep
  17.1 0.1 concatenate.12.beam
  17.2 0.0 copy-start
  17.2 0.0 collective-permute-done.scan_a
  17.2 0.0 collective-permute-done.1.scan_b
  17.2 0.9 %copy-done = f32[16,16,384]{2,1,0:T(8,128)S(1)} copy-done((f32[16,16,384]{2,1,0:T(8,128)S(1)}, f32[16,16,384]{2,1,0:T(8,128)}, u32[]{:S(2)}) %copy-start) | copy-done | bytes 393240
  18.2 0.1 pad_maximum_fusion
  18.2 0.1 constant_dynamic-slice_fusion
  18.3 1.3 %collective-permute-start.2 = (f32[32,8,320]{2,1,0:T(8,128)S(1)}, f32[32,8,320]{2,1,0:T(8,128)S(1)}, u32[]{:S(2)}, u32[]{:S(2)}) collective-permute-start(f32[32,8,320]{2,1,0:T(8,128)S(1)} %get-tuple-element.6), channel_id=1, source_target_pairs={{0,1},{1,0},{2,3},{3,2},{4,5},{5,4},{6,7},{7,6},{8,9},{9,8},{10,11... | collective-permute-start | bytes 983048 | tf_op jit(solution)/shard_map/ppermute | solution.py:356
  19.6 3.1 %collective-permute-start.3 = (f32[32,8,320]{2,1,0:T(8,128)S(1)}, f32[32,8,320]{2,1,0:T(8,128)S(1)}, u32[]{:S(2)}, u32[]{:S(2)}) collective-permute-start(f32[32,8,320]{2,1,0:T(8,128)S(1)} %get-tuple-element.5), channel_id=1, source_target_pairs={{1,2},{2,1},{3,4},{4,3},{5,6},{6,5},{9,10},{10,9},{11,12},{12,11},... | collective-permute-start | bytes 983048 | tf_op jit(solution)/shard_map/ppermute | solution.py:355
  22.7 0.1 pad_add_fusion.place
  22.8 0.1 broadcast_multiply_fusion.dose_ref
  22.9 0.0 collective-permute-done.2.cross_a
  22.9 5.8 %collective-permute-done.3.cross_b = f32[32,8,320]{2,1,0:T(8,128)S(1)} collective-permute-done((f32[32,8,320]{2,1,0:T(8,128)S(1)}, f32[32,8,320]{2,1,0:T(8,128)S(1)}, u32[]{:S(2)}, u32[]{:S(2)}) %collective-permute-start.3) | collective-permute-done | bytes 327712 | tf_op jit(solution)/shard_map/ppermute | solution.py:355
  28.7 0.1 broadcast_in_dim.42.inside_ref
  28.8 15.5 %anneal.1 = f32[16,16,384]{2,1,0:T(8,128)} custom-call(s32[4]{0:T(128)S(1)} %pad_add_fusion.place, f32[256]{0:T(256)S(1)} %concatenate.12.beam, f32[256]{0:T(256)S(1)} %concatenate.13.keep, f32[16,16,384]{2,1,0:T(8,128)S(1)} %copy-done, f32[8,16,320]{2,1,0:T(8,128)S(1)} %collective-permute-done.scan_a, f32[8,16,320]{2,1,0:T(8,128)S(1)} %collective-permute-done.1.scan_b, ...), custom_call_target="tpu_custom_call" | custom-call | tf_op jit(solution)/shard_map/anneal/pallas_call | solution.py:402
  (15 shorter events, 0.2 us)
Async XLA Ops:
  1.1 16.1 %collective-permute-start = (f32[8,16,320]{2,1,0:T(8,128)S(1)}, f32[8,16,320]{2,1,0:T(8,128)S(1)}, u32[]{:S(2)}, u32[]{:S(2)}) collective-permute-start(f32[8,16,320]{2,1,0:T(8,128)S(1)} %get-tuple-element.10), channel_id=1, source_target_pairs={{0,8},{8,0},{16,24},{24,16},{1,9},{9,1},{17,25},{25,17},{2,10},{10... | collective-permute-start | bytes 491528 | tf_op jit(solution)/shard_map/ppermute | solution.py:349
  3.2 14.0 %collective-permute-start.1 = (f32[8,16,320]{2,1,0:T(8,128)S(1)}, f32[8,16,320]{2,1,0:T(8,128)S(1)}, u32[]{:S(2)}, u32[]{:S(2)}) collective-permute-start(f32[8,16,320]{2,1,0:T(8,128)S(1)} %get-tuple-element.9), channel_id=1, source_target_pairs={{8,16},{16,8},{24,0},{0,24},{9,17},{17,9},{25,1},{1,25},{10,18},{1... | collective-permute-start | bytes 491528 | tf_op jit(solution)/shard_map/ppermute | solution.py:348
  4.4 0.7 %copy-start.3 = (f32[256]{0:T(256)S(1)}, f32[256]{0:T(256)}, u32[]{:S(2)}) copy-start(f32[256]{0:T(256)} %param.6) | copy-start | bytes 3076
  5.8 1.3 %copy-start.2 = (s32[4]{0:T(128)S(1)}, s32[4]{0:T(128)}, u32[]{:S(2)}) copy-start(s32[4]{0:T(128)} %param.9) | copy-start | bytes 52
  5.8 0.7 %copy-start.1 = (s32[4]{0:T(128)S(1)}, s32[4]{0:T(128)}, u32[]{:S(2)}) copy-start(s32[4]{0:T(128)} %param.8) | copy-start | bytes 52
  16.1 0.7 %copy-start.4 = (f32[128]{0:T(128)S(1)}, f32[128]{0:T(128)}, u32[]{:S(2)}) copy-start(f32[128]{0:T(128)} %param.7) | copy-start | bytes 1540
  17.2 1.0 %copy-start = (f32[16,16,384]{2,1,0:T(8,128)S(1)}, f32[16,16,384]{2,1,0:T(8,128)}, u32[]{:S(2)}) copy-start(f32[16,16,384]{2,1,0:T(8,128)} %own.1) | copy-start | bytes 1179652
  18.3 4.6 %collective-permute-start.2 = (f32[32,8,320]{2,1,0:T(8,128)S(1)}, f32[32,8,320]{2,1,0:T(8,128)S(1)}, u32[]{:S(2)}, u32[]{:S(2)}) collective-permute-start(f32[32,8,320]{2,1,0:T(8,128)S(1)} %get-tuple-element.6), channel_id=1, source_target_pairs={{0,1},{1,0},{2,3},{3,2},{4,5},{5,4},{6,7},{7,6},{8,9},{9,8},{10,11... | collective-permute-start | bytes 983048 | tf_op jit(solution)/shard_map/ppermute | solution.py:356
  19.6 9.1 %collective-permute-start.3 = (f32[32,8,320]{2,1,0:T(8,128)S(1)}, f32[32,8,320]{2,1,0:T(8,128)S(1)}, u32[]{:S(2)}, u32[]{:S(2)}) collective-permute-start(f32[32,8,320]{2,1,0:T(8,128)S(1)} %get-tuple-element.5), channel_id=1, source_target_pairs={{1,2},{2,1},{3,4},{4,3},{5,6},{6,5},{9,10},{10,9},{11,12},{12,11},... | collective-permute-start | bytes 983048 | tf_op jit(solution)/shard_map/ppermute | solution.py:355

commit v3 on v0

v3 whole, which is shorter than its diff:
```python
import functools

import jax
import jax.numpy as jnp
from jax import lax
from jax.experimental import pallas as pl
from jax.experimental.pallas import tpu as pltpu
from jax.sharding import PartitionSpec as P

STEPS = 4
SUBSTEPS = 2
HALO = STEPS * SUBSTEPS

heat_power = 0.5
absorb_depth = 6.0
barrier_energy = 3.0
frequency_multiplier = 0.6
proton_mobility = 0.15

SUB = 8
LANE = 128
UNROLL = 2
PAD = UNROLL + 4


def pair_swap(size, first, wraps):
    pairs = []
    for low in range(first, size + first, 2):
        high = low + 1
        if high >= size:
            if not wraps:
                continue
            high -= size
        pairs += [(low, high), (high, low)]
    return pairs


def reciprocal(value):
    return pltpu.reciprocal(value, approx=True)


def turn(value):
    return pltpu.roll(value, value.shape[-1] // 2, value.ndim - 1)


def lanes_of(shape):
    return lax.broadcasted_iota(jnp.int32, shape, len(shape) - 1)


def halves(low, high):
    return jnp.where(lanes_of(low.shape) < LANE // 2, low, turn(high))


def pack_kernel(z_tiles, place, own, scan_a, scan_b, cross_a, cross_b):
    rows, cols, _ = own.shape
    odd_x, odd_y = place[0] % 2, place[1] % 2

    def acid_pair(first, second, span):
        tile = slice(z_tiles * LANE, (z_tiles + 1) * LANE)
        return halves(own[first, span, tile], own[second, span, tile])

    for out, low_end in ((scan_a, 1 - odd_x), (scan_b, odd_x)):
        def row(d):
            return jnp.where(low_end == 1, rows - 1 - d, d)

        for d in range(HALO):
            for z in range(z_tiles):
                out[d * z_tiles + z] = own[row(d), :, z * LANE : (z + 1) * LANE]
        for d in range(HALO // 2):
            out[HALO * z_tiles + d] = acid_pair(row(d), row(d + HALO // 2), slice(None))
    for out, right_end in ((cross_a, 1 - odd_y), (cross_b, odd_y)):
        span = pl.ds(pl.multiple_of(right_end * (cols - HALO), SUB), HALO)
        for x in range(rows):
            for z in range(z_tiles):
                out[x * z_tiles + z] = own[x, span, z * LANE : (z + 1) * LANE]
        for x in range(rows // 2):
            out[rows * z_tiles + x] = acid_pair(x, x + rows // 2, span)


def corner_kernel(z_tiles, place, cross_a, cross_b, corner_a, corner_b):
    rows = cross_a.shape[0] * 2 // (2 * z_tiles + 1)
    odd_x, odd_y = place[0] % 2, place[1] % 2
    half = HALO // 2
    spot = lax.broadcasted_iota(jnp.int32, (SUB, LANE), 0)
    for out, low_end in ((corner_a, 1 - odd_x), (corner_b, odd_x)):
        for right in range(2):

            def tile(i, z):
                x = jnp.where(low_end == 1, rows - i, i - 1)
                if z < z_tiles:
                    index = x * z_tiles + z
                else:
                    index = rows * z_tiles + x % (rows // 2)
                from_a = (odd_y == 1) if right == 0 else (odd_y == 0)
                value = jnp.where(from_a, cross_a[index], cross_b[index])
                if z == z_tiles:
                    value = jnp.where(x >= rows // 2, turn(value), value)
                return value

            def slot(i, z):
                near, far = tile(i, z), tile(HALO - i, z)
                if right:
                    return jnp.where(spot < HALO - i, near, pltpu.roll(far, HALO - i, 0))
                return jnp.where(spot >= i, near, pltpu.roll(far, i, 0))

            base = right * out.shape[0] // 2
            for i in range(1, half + 1):
                for z in range(z_tiles):
                    out[base + (i - 1) * z_tiles + z] = slot(i, z)
            for i in range(1, half + 1, 2):
                out[base + half * z_tiles + (i - 1) // 2] = halves(
                    slot(i, z_tiles), slot(i + 1, z_tiles)
                )


def restored(corner, right, i, z, z_tiles):
    half = HALO // 2
    base = right * corner.shape[0] // 2
    slot = i if i <= half else max(HALO - i, 1)
    if z < z_tiles:
        value = corner[base + (slot - 1) * z_tiles + z]
    else:
        value = corner[base + half * z_tiles + (slot - 1) // 2]
        if slot % 2 == 0:
            value = turn(value)
    if i > half:
        value = pltpu.roll(value, slot if right else HALO - slot, 0)
    return value


def face(value, other, factor, other_factor):
    return (factor + other_factor) * (other - value)


def mobility(warm):
    return 0.5 * proton_mobility - 0.5 * proton_mobility * reciprocal(1.0 + warm * warm)


class Block:
    def __init__(self, sizes, first, state, tables):
        self.rows, self.cols, self.z_tiles, self.fine = sizes
        self.wide_rows = self.rows + 2 * HALO
        self.pairs = self.wide_rows // 2
        self.first = first
        self.heat, self.cond, self.acid, self.diff, self.soft, self.left = state[:6]
        self.part, self.deep, self.flow = state[6:]
        self.spots, self.keeps, self.dose, self.inside, self.coeff, self.under = tables
        lane = lanes_of((SUB, LANE))
        self.last_lane = lane == LANE - 1
        self.first_lane = lane == 0
        resist = LANE // 2
        self.acid_face = jnp.where(lane % resist == resist - 1, 0.0, 1.0).astype(jnp.float32)
        self.edge_cols = {(HALO - 1) % self.fine, (HALO + self.cols) % self.fine}
        self.lines = 2 * self.fine * self.z_tiles

    def at(self, side, y, z):
        return (side * self.fine + y) * self.z_tiles + z

    def conductivity(self, warm, z):
        return self.coeff[z] * reciprocal(4.0 + warm * warm)

    def fill(self, slot, warm, acid):
        for y in range(self.fine):
            for z in range(self.z_tiles):
                for side in range(2):
                    value = warm(side, y, z)
                    self.heat[slot, self.at(side, y, z)] = value
                    self.cond[slot, self.at(side, y, z)] = self.conductivity(value, z)
            self.acid[slot, y] = acid(y)
            value = halves(warm(0, y, 0), warm(1, y, 0))
            self.soft[slot, y] = value
            self.diff[slot, y] = mobility(value)

    def fill_natural(self, slot, nat, x):
        fine, z_tiles = self.fine, self.z_tiles

        def take(side, y, z):
            return nat[side, x, z, pl.ds(y, SUB, stride=fine), :]

        self.fill(slot, take, lambda y: halves(take(0, y, z_tiles), take(1, y, z_tiles)))

    def window(self, x):
        place = pl.ds(x - self.first, UNROLL + 3)
        return [
            ref.at[place]
            for ref in (self.heat, self.cond, self.acid, self.diff, self.soft, self.left)
        ]

    def x_faces(self, near, k):
        heat, cond, acid, diff = near[:4]
        faces = [
            face(heat[k, i], heat[k + 1, i], cond[k, i], cond[k + 1, i])
            for i in range(self.lines)
        ]
        return faces + [
            face(acid[k, y], acid[k + 1, y], diff[k, y], diff[k + 1, y])
            for y in range(self.fine)
        ]

    def y_gain(self, value, factor):
        faces = [
            face(value[y], value[y + 1], factor[y], factor[y + 1])
            for y in range(self.fine - 1)
        ]
        faces.append(
            face(
                value[-1],
                pltpu.roll(value[0], SUB - 1, 0),
                factor[-1],
                pltpu.roll(factor[0], SUB - 1, 0),
            )
        )
        before = [pltpu.roll(faces[-1], 1, 0)] + faces[:-1]
        return [after - b for after, b in zip(faces, before)]

    def z_faces(self, value, factor):
        rolled = [pltpu.roll(v, LANE - 1, 1) for v in value] + [0.0]
        faces = []
        for z in range(self.z_tiles):
            below = jnp.where(self.last_lane, rolled[z + 1], rolled[z])
            below_f = self.under[z] * reciprocal(4.0 + below * below)
            faces.append(face(value[z], below, factor[z], below_f))
        return faces

    def z_gain(self, faces):
        gain, before = [], 0.0
        for value in faces:
            turned = pltpu.roll(value, 1, 1)
            gain.append(value - jnp.where(self.first_lane, before, turned))
            before = turned
        return gain

    def sink(self, near, k):
        heat, cond, acid, diff = near[:4]
        for side in range(2):
            for y in range(self.fine):
                ids = [self.at(side, y, z) for z in range(self.z_tiles)]
                faces = self.z_faces([heat[k, i] for i in ids], [cond[k, i] for i in ids])
                for i, value in zip(ids, faces):
                    self.deep[i] = value
        for y in range(self.fine):
            acd, dif = acid[k, y], diff[k, y]
            self.deep[self.lines + y] = self.acid_face * face(
                acd, pltpu.roll(acd, LANE - 1, 1), dif, pltpu.roll(dif, LANE - 1, 1)
            )

    def gather(self, near, k, x, step):
        heat, cond, acid, diff = near[:4]
        fine, z_tiles = self.fine, self.z_tiles
        for side in range(2):
            row = x if side == 0 else self.wide_rows - 1 - x
            spot = self.spots[pl.ds(step * self.wide_rows + row, 1), :]
            ids = [[self.at(side, y, z) for y in range(fine)] for z in range(z_tiles)]
            across = [
                self.y_gain([heat[k, i] for i in ids[z]], [cond[k, i] for i in ids[z]])
                for z in range(z_tiles)
            ]
            for y in range(fine):
                down = self.z_gain([self.deep[ids[z][y]] for z in range(z_tiles)])
                for z in range(z_tiles):
                    i = ids[z][y]
                    new = heat[k, i] + spot * self.dose[y * z_tiles + z]
                    self.part[i] = new + across[z][y] + down[z]
        acd = [acid[k, y] for y in range(fine)]
        across = self.y_gain(acd, [diff[k, y] for y in range(fine)])
        for y in range(fine):
            i = self.lines + y
            down = self.deep[i]
            self.part[i] = acd[y] + across[y] + (down - pltpu.roll(down, 1, 1))

    def finish(self, near, k, x, step, cooling, before):
        heat, cond, acid, _, soft, left = near
        after = self.x_faces(near, k)
        for y in range(self.fine):
            rate = frequency_multiplier * jnp.exp(
                -barrier_energy * reciprocal(1.0 + soft[k, y])
            )
            left[k, y] = left[k, y] * (1.0 - rate * acid[k, y])
        for side in range(2):
            row = x if side == 0 else self.wide_rows - 1 - x
            if cooling:
                kept = self.keeps[pl.ds(step // SUBSTEPS * self.wide_rows + row, 1), :]
            for y in range(self.fine):
                for z in range(self.z_tiles):
                    i = self.at(side, y, z)
                    new = self.part[i] + (after[i] - before[i])
                    if cooling:
                        new = new * kept
                    if y in self.edge_cols:
                        new = new * self.inside[y]
                    heat[k, i] = new
                    cond[k, i] = self.conductivity(new, z)
        for y in range(self.fine):
            i = self.lines + y
            new = self.part[i] + (after[i] - before[i])
            if y in self.edge_cols:
                new = new * self.inside[y]
            acid[k, y] = new
        return after

    def soften(self, near, k):
        heat, diff, soft = near[0], near[3], near[4]
        for y in range(self.fine):
            warm = halves(heat[k, self.at(0, y, 0)], heat[k, self.at(1, y, 0)])
            soft[k, y] = warm
            diff[k, y] = mobility(warm)

    def substep(self, step, cooling, begin, count):
        first = self.window(begin)
        self.sink(first, 1)
        self.gather(first, 1, begin, step)
        self.sink(first, 2)
        for i, value in enumerate(self.x_faces(first, 0)):
            self.flow[i] = value

        def some_pairs(number, carry):
            x = begin + number * UNROLL
            near = self.window(x)
            before = [self.flow[i] for i in range(self.flow.shape[0])]
            for ahead in range(UNROLL):
                k = ahead + 1
                before = self.finish(near, k, x + ahead, step, cooling, before)
                self.gather(near, k + 1, x + ahead + 1, step)
                self.sink(near, k + 2)
                self.soften(near, k - 1)
            for i, value in enumerate(before):
                self.flow[i] = value
            return carry

        lax.fori_loop(0, count, some_pairs, 0)
        self.soften(self.window(begin + count * UNROLL), 0)


def for_substeps(body):
    def frame(number, carry):
        for sub in range(SUBSTEPS):
            body(number * SUBSTEPS + sub, sub == SUBSTEPS - 1)
        return carry

    lax.fori_loop(0, STEPS, frame, 0)


def make_tables(sizes, mesh_sizes, place, profile, start, steps, coeff, tables, column):
    rows, cols, z_tiles, fine = sizes
    spots, keeps, dose, inside, coeffs, under = tables
    scan_pos, cross_pos = place[0], place[1]
    scan_count, cross_count = mesh_sizes
    total_x, total_y = rows * scan_count, cols * cross_count
    wide_rows, wide_cols = rows + 2 * HALO, cols + 2 * HALO
    spread = float(rows // 2)

    def frame(number, carry):
        block = lax.rem(scan_pos - number + STEPS * scan_count, scan_count)
        x = lax.broadcasted_iota(jnp.int32, (wide_rows, LANE), 0) + (block * rows - HALO)
        x = jnp.where(x < 0, x + total_x, x)
        x = jnp.where(x >= total_x, x - total_x, x)
        place = pl.ds(pl.multiple_of(number * wide_rows, SUB), wide_rows)
        keeps[place, :] = jnp.where(x < rows, 0.0, 1.0).astype(jnp.float32)
        for sub in range(SUBSTEPS):
            center = (start[number] + sub * steps[number]).astype(jnp.float32)
            away = (x.astype(jnp.float32) - center) / spread
            place = pl.multiple_of((number * SUBSTEPS + sub) * wide_rows, SUB)
            spots[pl.ds(place, wide_rows), :] = jnp.exp(-(away * away))
        return carry

    lax.fori_loop(0, STEPS, frame, 0)

    for y in range(wide_cols):
        at = cross_pos * cols + (y - HALO)
        here = jnp.where(
            (at >= 0) & (at < total_y), profile[jnp.clip(at, 0, total_y - 1)], 0.0
        )
        column[pl.ds(y, 1), :] = jnp.full((1, LANE), heat_power * here, jnp.float32)
    lane = lanes_of((SUB, LANE))
    level = lane.astype(jnp.float32)
    resist = LANE // 2
    for z in range(z_tiles):
        depth = level + float(z * LANE)
        absorb = jnp.exp(-(depth - float(resist)) / absorb_depth)
        absorb = jnp.where(depth >= float(resist), absorb, 0.0)
        for y in range(fine):
            dose[y * z_tiles + z] = absorb * column[pl.ds(y, SUB, stride=fine), :]
        here = jnp.broadcast_to(coeff[z : z + 1, :], (SUB, LANE))
        if z + 1 < z_tiles:
            below = jnp.broadcast_to(coeff[z + 1 : z + 2, :], (SUB, LANE))
            below = pltpu.roll(below, LANE - 1, 1)
        else:
            below = here
        coeffs[z] = 2.0 * here
        under[z] = 2.0 * jnp.where(lane == LANE - 1, below, pltpu.roll(here, LANE - 1, 1))
    spot = lax.broadcasted_iota(jnp.int32, (SUB, LANE), 0)
    for y in range(fine):
        at = spot * fine + (y - HALO + cross_pos * cols)
        inside[y] = jnp.where((at >= 0) & (at < total_y), 1.0, 0.0).astype(jnp.float32)


def inner_kernel(
    sizes, mesh_sizes, place, start, steps, profile, coeff, own, cross_a, cross_b, *refs
):
    row_heat, row_acid, row_left, next_heat, next_acid = refs[:5]
    tables, (nat, column), state = refs[5:11], refs[11:13], refs[13:]
    rows, cols, z_tiles, fine = sizes
    make_tables(sizes, mesh_sizes, place, profile, start, steps, coeff, tables, column)
    block = Block(sizes, HALO, state, tables)
    odd_y = place[1] % 2
    mine = block.pairs - HALO
    col_a = pl.multiple_of((1 - odd_y) * (cols + HALO), SUB)
    col_b = pl.multiple_of(odd_y * (cols + HALO), SUB)
    for pair in range(mine):
        for side in range(2):
            x = pair if side == 0 else rows - 1 - pair
            for z in range(z_tiles + 1):
                nat[side, pair, z, HALO : HALO + cols, :] = own[x, :, z * LANE : (z + 1) * LANE]
                for message, column_at in ((cross_a, col_a), (cross_b, col_b)):
                    if z < z_tiles:
                        value = message[x * z_tiles + z]
                    else:
                        value = message[rows * z_tiles + x % (rows // 2)]
                        if x >= rows // 2:
                            value = turn(value)
                    nat[side, pair, z, pl.ds(column_at, HALO), :] = value

    blank = jnp.zeros((SUB, LANE), jnp.float32)
    for ref in (block.heat, block.cond, block.acid, block.diff, block.soft):
        for i in range(ref.shape[1]):
            ref[0, i] = blank

    def load(x, carry):
        block.fill_natural(x + 1, nat, x)
        for y in range(fine):
            block.left[x + 1, y] = jnp.ones((SUB, LANE), jnp.float32)
        return carry

    lax.fori_loop(0, mine, load, 0)

    def step_body(step, cooling):
        for i in range(block.lines):
            j = (i + block.lines // 2) % block.lines
            block.heat[mine + 1, i] = block.heat[mine, j]
            block.cond[mine + 1, i] = block.cond[mine, j]
            row_heat[step, i] = block.heat[step + 1, i]
        for y in range(fine):
            block.acid[mine + 1, y] = turn(block.acid[mine, y])
            block.diff[mine + 1, y] = turn(block.diff[mine, y])
            row_acid[step, y] = block.acid[step + 1, y]
            row_left[step, y] = block.left[step + 1, y]
        for i in range(block.lines):
            next_heat[step, i] = block.heat[step + 2, i]
        for y in range(fine):
            next_acid[step, y] = block.acid[step + 2, y]
        count = (mine - 1 - step + UNROLL - 1) // UNROLL
        block.substep(step, cooling, block.pairs - count * UNROLL, count)

    for_substeps(step_body)


def outer_kernel(
    sizes,
    place,
    own,
    scan_a,
    scan_b,
    corner_a,
    corner_b,
    row_heat,
    row_acid,
    row_left,
    next_heat,
    next_acid,
    *refs,
):
    tables, out, nat, state = refs[:6], refs[6], refs[7], refs[8:]
    rows, cols, z_tiles, fine = sizes
    block = Block(sizes, 0, state, tables)
    odd_x = place[0] % 2
    mine = block.pairs - HALO
    for scan, corner, side in ((scan_a, corner_a, 1 - odd_x), (scan_b, corner_b, odd_x)):
        for d in range(HALO):
            x = HALO - 1 - d
            for z in range(z_tiles + 1):
                if z < z_tiles:
                    value = scan[d * z_tiles + z]
                else:
                    value = scan[HALO * z_tiles + d % (HALO // 2)]
                    if d >= HALO // 2:
                        value = turn(value)
                nat[side, x, z, HALO : HALO + cols, :] = value
                nat[side, x, z, :HALO, :] = restored(corner, 0, d + 1, z, z_tiles)
                nat[side, x, z, HALO + cols :, :] = restored(corner, 1, d + 1, z, z_tiles)

    blank = jnp.zeros((SUB, LANE), jnp.float32)
    for ref in (block.heat, block.cond, block.acid, block.diff, block.soft):
        for i in range(ref.shape[1]):
            ref[0, i] = blank

    def load(x, carry):
        block.fill_natural(x + 1, nat, x)
        return carry

    lax.fori_loop(0, HALO, load, 0)

    def step_body(step, cooling):
        slot = step + HALO + 1
        block.fill(
            slot,
            lambda side, y, z: row_heat[step, block.at(side, y, z)],
            lambda y: row_acid[step, y],
        )
        for y in range(fine):
            block.left[slot, y] = row_left[step, y]
        block.fill(
            slot + 1,
            lambda side, y, z: next_heat[step, block.at(side, y, z)],
            lambda y: next_acid[step, y],
        )
        block.substep(step, cooling, step + 1, HALO // UNROLL)

    for_substeps(step_body)

    def store(pair, carry):
        slot = pair + HALO + 1
        row = (pair, rows - 1 - pair)
        for y in range(fine):
            put = pl.ds(y, SUB, stride=fine)
            for side in range(2):
                for z in range(z_tiles):
                    nat[side, pair, z, put, :] = block.heat[slot, block.at(side, y, z)]
            acd, kept = block.acid[slot, y], block.left[slot, y]
            low = lanes_of(acd.shape) < LANE // 2
            nat[0, pair, z_tiles, put, :] = jnp.where(low, acd, turn(kept))
            nat[1, pair, z_tiles, put, :] = jnp.where(low, turn(acd), kept)
        for side in range(2):
            for z in range(z_tiles):
                out[row[side], :, z * LANE : (z + 1) * LANE] = nat[
                    side, pair, z, HALO : HALO + cols, :
                ]
            mixed = nat[side, pair, z_tiles, HALO : HALO + cols, :]
            begun = own[row[side], :, z_tiles * LANE :]
            low = lanes_of(mixed.shape) < LANE // 2
            out[row[side], :, z_tiles * LANE :] = jnp.where(low, mixed, mixed * begun)
        return carry

    lax.fori_loop(0, mine, store, 0)


def shards(wafer_state, layer_heat_coefficients, beam_profile, beam_start, beam_steps):
    rows, cols, depth = wafer_state.shape
    deep = layer_heat_coefficients.shape[0]
    scan_count, cross_count = lax.axis_size("scan"), lax.axis_size("cross")
    place = jnp.stack([lax.axis_index("scan"), lax.axis_index("cross")]).astype(jnp.int32)
    wide_rows, wide_cols = rows + 2 * HALO, cols + 2 * HALO
    z_tiles = deep // LANE
    fine = wide_cols // SUB
    mine = rows // 2
    sizes = (rows, cols, z_tiles, fine)
    lines = 2 * fine * z_tiles
    smem = pl.BlockSpec(memory_space=pltpu.SMEM)
    vmem = pl.BlockSpec(memory_space=pltpu.VMEM)
    params = pltpu.CompilerParams(vmem_limit_bytes=40 * 2**20)

    def array(*shape):
        return jax.ShapeDtypeStruct(shape, jnp.float32)

    def state(pairs):
        return [
            pltpu.VMEM((pairs + PAD, lines, SUB, LANE), jnp.float32),
            pltpu.VMEM((pairs + PAD, lines, SUB, LANE), jnp.float32),
            pltpu.VMEM((pairs + PAD, fine, SUB, LANE), jnp.float32),
            pltpu.VMEM((pairs + PAD, fine, SUB, LANE), jnp.float32),
            pltpu.VMEM((pairs + PAD, fine, SUB, LANE), jnp.float32),
            pltpu.VMEM((pairs + PAD, fine, SUB, LANE), jnp.float32),
            pltpu.VMEM((lines + fine, SUB, LANE), jnp.float32),
            pltpu.VMEM((lines + fine, SUB, LANE), jnp.float32),
            pltpu.VMEM((lines + fine, SUB, LANE), jnp.float32),
        ]

    scan_message = array(HALO * z_tiles + HALO // 2, cols, LANE)
    cross_message = array(rows * z_tiles + rows // 2, HALO, LANE)
    corner_message = array(HALO * z_tiles + HALO // 2, HALO, LANE)
    scan_a, scan_b, cross_a, cross_b = pl.pallas_call(
        functools.partial(pack_kernel, z_tiles),
        out_shape=(scan_message, scan_message, cross_message, cross_message),
        in_specs=[smem, vmem],
        out_specs=(vmem,) * 4,
        compiler_params=params,
        name="pack",
    )(place, wafer_state)

    cross_b = lax.ppermute(cross_b, "cross", pair_swap(cross_count, 1, False))
    cross_a = lax.ppermute(cross_a, "cross", pair_swap(cross_count, 0, False))
    scan_b = lax.ppermute(scan_b, "scan", pair_swap(scan_count, 1, True))
    scan_a = lax.ppermute(scan_a, "scan", pair_swap(scan_count, 0, True))

    corner_a, corner_b = pl.pallas_call(
        functools.partial(corner_kernel, z_tiles),
        out_shape=(corner_message, corner_message),
        in_specs=[smem, vmem, vmem],
        out_specs=(vmem,) * 2,
        compiler_params=params,
        name="corners",
    )(place, cross_a, cross_b)
    corner_b = lax.ppermute(corner_b, "scan", pair_swap(scan_count, 1, True))
    corner_a = lax.ppermute(corner_a, "scan", pair_swap(scan_count, 0, True))

    row_shapes = (
        array(HALO, lines, SUB, LANE),
        array(HALO, fine, SUB, LANE),
        array(HALO, fine, SUB, LANE),
        array(HALO, lines, SUB, LANE),
        array(HALO, fine, SUB, LANE),
    )
    table_shapes = (
        array(HALO * wide_rows, LANE),
        array(STEPS * wide_rows, LANE),
        array(fine * z_tiles, SUB, LANE),
        array(fine, SUB, LANE),
        array(z_tiles, SUB, LANE),
        array(z_tiles, SUB, LANE),
    )
    inner = pl.pallas_call(
        functools.partial(inner_kernel, sizes, (scan_count, cross_count)),
        out_shape=row_shapes + table_shapes,
        in_specs=[smem] * 4 + [vmem] * 4,
        out_specs=(vmem,) * (len(row_shapes) + len(table_shapes)),
        scratch_shapes=[
            pltpu.VMEM((2, mine, z_tiles + 1, wide_cols, LANE), jnp.float32),
            pltpu.VMEM((wide_cols, LANE), jnp.float32),
        ]
        + state(mine),
        compiler_params=params,
        cost_estimate=pl.CostEstimate(
            flops=50_000_000, bytes_accessed=8_000_000, transcendentals=1_000_000
        ),
        name="inner",
    )(
        place,
        beam_start,
        beam_steps,
        beam_profile,
        layer_heat_coefficients.reshape(z_tiles, LANE),
        wafer_state,
        cross_a,
        cross_b,
    )
    result = pl.pallas_call(
        functools.partial(outer_kernel, sizes),
        out_shape=jax.ShapeDtypeStruct(wafer_state.shape, wafer_state.dtype),
        in_specs=[smem] + [vmem] * (5 + len(inner)),
        out_specs=vmem,
        scratch_shapes=[pltpu.VMEM((2, mine, z_tiles + 1, wide_cols, LANE), jnp.float32)]
        + state(HALO + mine),
        compiler_params=params,
        name="outer",
    )(place, wafer_state, scan_a, scan_b, corner_a, corner_b, *inner)
    lag_blocks = STEPS % scan_count
    if lag_blocks:
        pairs = [(source, (source - lag_blocks) % scan_count) for source in range(scan_count)]
        result = lax.ppermute(result, "scan", pairs)
    return result


def solution(mesh):
    in_specs = (P("scan", "cross", None), P(), P(), P(), P())
    out_specs = P("scan", "cross", None)
    return jax.shard_map(shards, mesh=mesh, in_specs=in_specs, out_specs=out_specs, check_vma=False)
```

time: 119 us -> 31.7 us (0.27)
  the two profiles are of different devices: /device:TPU:0 before, /device:TPU:1 now
where the time goes in v3:
time: 31.7 us; the launch traced here: 31.5 us
  Pallas kernels  19.3 us (61%)
  starting transfers between devices  10.5 us (33%)
  local copies, waits for them, and re-layouts  1.01 us (3%)
  waiting for transfers between devices  0.51 us (2%)
    pallas_call x1, Pallas kernels, shards(): pl.pallas_call(functools.partial(outer_kernel, sizes), out_shape=jax.Shap...  10.8 us
    pallas_call x1, Pallas kernels, shards(): pl.pallas_call(functools.partial(inner_kernel, sizes, (scan_count, cross_...  7.14 us
    ppermute x1, starting transfers between devices, shards(): cross_b = lax.ppermute(cross_b, 'cross', pair_swap(cross_count, 1, False))  4.55 us
    ppermute x1, starting transfers between devices, shards(): corner_a = lax.ppermute(corner_a, 'scan', pair_swap(scan_count, 0, True))  2.1 us
    ppermute x1, starting transfers between devices, shards(): scan_a = lax.ppermute(scan_a, 'scan', pair_swap(scan_count, 0, True))  1.28 us
    ppermute x1, starting transfers between devices, shards(): corner_b = lax.ppermute(corner_b, 'scan', pair_swap(scan_count, 1, True))  1.28 us
    ppermute x1, starting transfers between devices, shards(): scan_b = lax.ppermute(scan_b, 'scan', pair_swap(scan_count, 1, True))  1.21 us
    unnamed x12, local copies, waits for them, and re-layouts  1.01 us
  transfers between devices with their start and end apart: 6, of which 1 were waited for; matrix products, arithmetic and copies ran while one was open for 0% of the time, Pallas kernels for 25%

profile of v3, /device:TPU:1, one launch (start us, length us, event | category | flops | bytes accessed | tf_op | source)
XLA Modules:
  0.0 31.5 jit_solution(10987002998740493419)
XLA Ops:
  0.0 0.1 pad_add_fusion.place
  0.1 0.0 copy-start
  0.1 1.0 %copy-done = f32[16,16,384]{2,1,0:T(8,128)S(1)} copy-done((f32[16,16,384]{2,1,0:T(8,128)S(1)}, f32[16,16,384]{2,1,0:T(8,128)}, u32[]{:S(2)}) %copy-start) | copy-done | bytes 393240
  1.1 0.0 copy-start.1
  1.1 0.7 %pack.1 = (f32[20,16,128]{2,1,0:T(8,128)S(1)}, f32[20,16,128]{2,1,0:T(8,128)S(1)}, f32[40,8,128]{2,1,0:T(8,128)S(1)}, f32[40,8,128]{2,1,0:T(8,128)S(1)}) custom-call(s32[2]{0:T(128)S(1)} %pad_add_fusion.place, f32[16,16,384]{2,1,0:T(8,128)S(1)} %copy-done), custom_call_target="tpu_custom_call" | custom-call | tf_op jit(solution)/shard_map/pack/pallas_call | solution.py:580
  1.7 0.1 collective-permute-start.2
  1.9 4.6 %collective-permute-start.3 = (f32[40,8,128]{2,1,0:T(8,128)S(1)}, f32[40,8,128]{2,1,0:T(8,128)S(1)}, u32[]{:S(2)}, u32[]{:S(2)}) collective-permute-start(f32[40,8,128]{2,1,0:T(8,128)S(1)} %get-tuple-element.25), channel_id=1, source_target_pairs={{1,2},{2,1},{3,4},{4,3},{5,6},{6,5},{9,10},{10,9},{11,12},{12,11},... | collective-permute-start | bytes 491528 | tf_op jit(solution)/shard_map/ppermute | solution.py:589
  6.4 1.3 %collective-permute-start = (f32[20,16,128]{2,1,0:T(8,128)S(1)}, f32[20,16,128]{2,1,0:T(8,128)S(1)}, u32[]{:S(2)}, u32[]{:S(2)}) collective-permute-start(f32[20,16,128]{2,1,0:T(8,128)S(1)} %get-tuple-element.22), channel_id=1, source_target_pairs={{0,8},{8,0},{16,24},{24,16},{1,9},{9,1},{17,25},{25,17},{2,10},{10... | collective-permute-start | bytes 491528 | tf_op jit(solution)/shard_map/ppermute | solution.py:592
  7.7 1.2 %collective-permute-start.1 = (f32[20,16,128]{2,1,0:T(8,128)S(1)}, f32[20,16,128]{2,1,0:T(8,128)S(1)}, u32[]{:S(2)}, u32[]{:S(2)}) collective-permute-start(f32[20,16,128]{2,1,0:T(8,128)S(1)} %get-tuple-element.23), channel_id=1, source_target_pairs={{8,16},{16,8},{24,0},{0,24},{9,17},{17,9},{25,1},{1,25},{10,18},{1... | collective-permute-start | bytes 491528 | tf_op jit(solution)/shard_map/ppermute | solution.py:591
  8.9 0.0 collective-permute-done.2.cross_a
  8.9 0.5 %collective-permute-done.3.cross_b = f32[40,8,128]{2,1,0:T(8,128)S(1)} collective-permute-done((f32[40,8,128]{2,1,0:T(8,128)S(1)}, f32[40,8,128]{2,1,0:T(8,128)S(1)}, u32[]{:S(2)}, u32[]{:S(2)}) %collective-permute-start.3) | collective-permute-done | bytes 163872 | tf_op jit(solution)/shard_map/ppermute | solution.py:589
  9.4 0.7 %corners.1 = (f32[20,8,128]{2,1,0:T(8,128)S(1)}, f32[20,8,128]{2,1,0:T(8,128)S(1)}) custom-call(s32[2]{0:T(128)S(1)} %pad_add_fusion.place, f32[40,8,128]{2,1,0:T(8,128)S(1)} %collective-permute-done.2.cross_a, f32[40,8,128]{2,1,0:T(8,128)S(1)} %collective-permute-done.3.cross_b), custom_call_target="tpu_custom_call" | custom-call | tf_op jit(solution)/shard_map/corners/pallas_call | solution.py:594
  10.1 2.1 %collective-permute-start.4 = (f32[20,8,128]{2,1,0:T(8,128)S(1)}, f32[20,8,128]{2,1,0:T(8,128)S(1)}, u32[]{:S(2)}, u32[]{:S(2)}) collective-permute-start(f32[20,8,128]{2,1,0:T(8,128)S(1)} %get-tuple-element.26), channel_id=1, source_target_pairs={{0,8},{8,0},{16,24},{24,16},{1,9},{9,1},{17,25},{25,17},{2,10},{10... | collective-permute-start | bytes 245768 | tf_op jit(solution)/shard_map/ppermute | solution.py:603
  12.2 0.0 copy-start.4
  12.2 0.0 copy-start.5
  12.2 0.0 copy-start.2
  12.2 0.0 copy-start.3
  12.2 1.3 %collective-permute-start.5 = (f32[20,8,128]{2,1,0:T(8,128)S(1)}, f32[20,8,128]{2,1,0:T(8,128)S(1)}, u32[]{:S(2)}, u32[]{:S(2)}) collective-permute-start(f32[20,8,128]{2,1,0:T(8,128)S(1)} %get-tuple-element.27), channel_id=1, source_target_pairs={{8,16},{16,8},{24,0},{0,24},{9,17},{17,9},{25,1},{1,25},{10,18},{1... | collective-permute-start | bytes 245768 | tf_op jit(solution)/shard_map/ppermute | solution.py:602
  13.5 0.0 copy-done.1
  13.5 0.0 copy-done.4
  13.5 0.0 copy-done.5
  13.5 0.0 copy-done.2
  13.5 0.0 copy-done.3
  13.5 7.1 %inner.1 = (f32[8,16,8,128]{3,2,1,0:T(8,128)S(1)}, f32[8,4,8,128]{3,2,1,0:T(8,128)S(1)}, f32[8,4,8,128]{3,2,1,0:T(8,128)S(1)}, f32[8,16,8,128]{3,2,1,0:T(8,128)S...) custom-call(s32[2]{0:T(128)S(1)} %pad_add_fusion.place, ...), custom_call_target="tpu_custom_call" | custom-call | flops 50000000 | bytes 8000000 | tf_op jit(solution)/shard_map/inner/pallas_call | solution.py:620
  20.7 0.0 collective-permute-done.scan_a
  20.7 0.0 collective-permute-done.1.scan_b
  20.7 0.0 collective-permute-done.4.corner_a
  20.7 0.0 collective-permute-done.5.corner_b
  20.7 10.8 %outer.1 = f32[16,16,384]{2,1,0:T(8,128)} custom-call(s32[2]{0:T(128)S(1)} %pad_add_fusion.place, f32[16,16,384]{2,1,0:T(8,128)S(1)} %copy-done.1, f32[20,16,128]{2,1,0:T(8,128)S(1)} %collective-permute-done.scan_a, f32[20,16,128]{2,1,0:T(8,128)S(1)} %collective-permute-done.1.scan_b, f32[20,8,128]{2,1,0:T(8,128)S(1)} %collective-permute-done.4.corner_a, ...), custom_call_target="tpu_custom_call" | custom-call | tf_op jit(solution)/shard_map/outer/pallas_call | solution.py:645
Async XLA Ops:
  0.1 1.0 %copy-start = (f32[16,16,384]{2,1,0:T(8,128)S(1)}, f32[16,16,384]{2,1,0:T(8,128)}, u32[]{:S(2)}) copy-start(f32[16,16,384]{2,1,0:T(8,128)} %own.5) | copy-start | bytes 1179652
  1.1 12.4 %copy-start.1 = (f32[16,16,384]{2,1,0:T(8,128)S(1)}, f32[16,16,384]{2,1,0:T(8,128)}, u32[]{:S(2)}) copy-start(f32[16,16,384]{2,1,0:T(8,128)} %own.5) | copy-start | bytes 1179652
  1.7 7.2 %collective-permute-start.2 = (f32[40,8,128]{2,1,0:T(8,128)S(1)}, f32[40,8,128]{2,1,0:T(8,128)S(1)}, u32[]{:S(2)}, u32[]{:S(2)}) collective-permute-start(f32[40,8,128]{2,1,0:T(8,128)S(1)} %get-tuple-element.24), channel_id=1, source_target_pairs={{0,1},{1,0},{2,3},{3,2},{4,5},{5,4},{6,7},{7,6},{8,9},{9,8},{10,11... | collective-permute-start | bytes 491528 | tf_op jit(solution)/shard_map/ppermute | solution.py:590
  1.9 7.5 %collective-permute-start.3 = (f32[40,8,128]{2,1,0:T(8,128)S(1)}, f32[40,8,128]{2,1,0:T(8,128)S(1)}, u32[]{:S(2)}, u32[]{:S(2)}) collective-permute-start(f32[40,8,128]{2,1,0:T(8,128)S(1)} %get-tuple-element.25), channel_id=1, source_target_pairs={{1,2},{2,1},{3,4},{4,3},{5,6},{6,5},{9,10},{10,9},{11,12},{12,11},... | collective-permute-start | bytes 491528 | tf_op jit(solution)/shard_map/ppermute | solution.py:589
  6.4 14.3 %collective-permute-start = (f32[20,16,128]{2,1,0:T(8,128)S(1)}, f32[20,16,128]{2,1,0:T(8,128)S(1)}, u32[]{:S(2)}, u32[]{:S(2)}) collective-permute-start(f32[20,16,128]{2,1,0:T(8,128)S(1)} %get-tuple-element.22), channel_id=1, source_target_pairs={{0,8},{8,0},{16,24},{24,16},{1,9},{9,1},{17,25},{25,17},{2,10},{10... | collective-permute-start | bytes 491528 | tf_op jit(solution)/shard_map/ppermute | solution.py:592
  7.7 13.0 %collective-permute-start.1 = (f32[20,16,128]{2,1,0:T(8,128)S(1)}, f32[20,16,128]{2,1,0:T(8,128)S(1)}, u32[]{:S(2)}, u32[]{:S(2)}) collective-permute-start(f32[20,16,128]{2,1,0:T(8,128)S(1)} %get-tuple-element.23), channel_id=1, source_target_pairs={{8,16},{16,8},{24,0},{0,24},{9,17},{17,9},{25,1},{1,25},{10,18},{1... | collective-permute-start | bytes 491528 | tf_op jit(solution)/shard_map/ppermute | solution.py:591
  10.1 10.6 %collective-permute-start.4 = (f32[20,8,128]{2,1,0:T(8,128)S(1)}, f32[20,8,128]{2,1,0:T(8,128)S(1)}, u32[]{:S(2)}, u32[]{:S(2)}) collective-permute-start(f32[20,8,128]{2,1,0:T(8,128)S(1)} %get-tuple-element.26), channel_id=1, source_target_pairs={{0,8},{8,0},{16,24},{24,16},{1,9},{9,1},{17,25},{25,17},{2,10},{10... | collective-permute-start | bytes 245768 | tf_op jit(solution)/shard_map/ppermute | solution.py:603
  12.2 1.3 %copy-start.4 = (s32[4]{0:T(128)S(1)}, s32[4]{0:T(128)}, u32[]{:S(2)}) copy-start(s32[4]{0:T(128)} %steps.1) | copy-start | bytes 52
  12.2 1.3 %copy-start.5 = (f32[128]{0:T(128)S(1)}, f32[128]{0:T(128)}, u32[]{:S(2)}) copy-start(f32[128]{0:T(128)} %profile.1) | copy-start | bytes 1540
  12.2 1.3 %copy-start.2 = (f32[256]{0:T(256)S(1)}, f32[256]{0:T(256)}, u32[]{:S(2)}) copy-start(f32[256]{0:T(256)} %param.6) | copy-start | bytes 3076
  12.2 1.3 %copy-start.3 = (s32[4]{0:T(128)S(1)}, s32[4]{0:T(128)}, u32[]{:S(2)}) copy-start(s32[4]{0:T(128)} %start.1) | copy-start | bytes 52
  12.2 8.5 %collective-permute-start.5 = (f32[20,8,128]{2,1,0:T(8,128)S(1)}, f32[20,8,128]{2,1,0:T(8,128)S(1)}, u32[]{:S(2)}, u32[]{:S(2)}) collective-permute-start(f32[20,8,128]{2,1,0:T(8,128)S(1)} %get-tuple-element.27), channel_id=1, source_target_pairs={{8,16},{16,8},{24,0},{0,24},{9,17},{17,9},{25,1},{1,25},{10,18},{1... | collective-permute-start | bytes 245768 | tf_op jit(solution)/shard_map/ppermute | solution.py:602

commit v4 on v3

--- a/solution.py
+++ b/solution.py
@@ -1,4 +1,5 @@
 import functools
+import math
 
 import jax
 import jax.numpy as jnp
@@ -17,10 +18,10 @@
 frequency_multiplier = 0.6
 proton_mobility = 0.15
 
+exponent = -barrier_energy / math.log(2.0)
+
 SUB = 8
 LANE = 128
-UNROLL = 2
-PAD = UNROLL + 4
 
 
 def pair_swap(size, first, wraps):
@@ -136,14 +137,26 @@
     return 0.5 * proton_mobility - 0.5 * proton_mobility * reciprocal(1.0 + warm * warm)
 
 
+class Line:
+    def __init__(self, ref, k):
+        self.ref, self.k = ref, k
+        self.shape = ref.shape[1:]
+
+    def __getitem__(self, i):
+        return self.ref[self.k, i]
+
+    def __setitem__(self, i, value):
+        self.ref[self.k, i] = value
+
+
 class Block:
     def __init__(self, sizes, first, state, tables):
         self.rows, self.cols, self.z_tiles, self.fine = sizes
         self.wide_rows = self.rows + 2 * HALO
         self.pairs = self.wide_rows // 2
         self.first = first
-        self.heat, self.cond, self.acid, self.diff, self.soft, self.left = state[:6]
-        self.part, self.deep, self.flow = state[6:]
+        self.state = state[:6]
+        self.part, self.deep = state[6:]
         self.spots, self.keeps, self.dose, self.inside, self.coeff, self.under = tables
         lane = lanes_of((SUB, LANE))
         self.last_lane = lane == LANE - 1
@@ -159,42 +172,29 @@
     def conductivity(self, warm, z):
         return self.coeff[z] * reciprocal(4.0 + warm * warm)
 
-    def fill(self, slot, warm, acid):
-        for y in range(self.fine):
-            for z in range(self.z_tiles):
-                for side in range(2):
-                    value = warm(side, y, z)
-                    self.heat[slot, self.at(side, y, z)] = value
-                    self.cond[slot, self.at(side, y, z)] = self.conductivity(value, z)
-            self.acid[slot, y] = acid(y)
-            value = halves(warm(0, y, 0), warm(1, y, 0))
-            self.soft[slot, y] = value
-            self.diff[slot, y] = mobility(value)
-
     def fill_natural(self, slot, nat, x):
         fine, z_tiles = self.fine, self.z_tiles
-
-        def take(side, y, z):
-            return nat[side, x, z, pl.ds(y, SUB, stride=fine), :]
-
-        self.fill(slot, take, lambda y: halves(take(0, y, z_tiles), take(1, y, z_tiles)))
-
-    def window(self, x):
-        place = pl.ds(x - self.first, UNROLL + 3)
-        return [
-            ref.at[place]
-            for ref in (self.heat, self.cond, self.acid, self.diff, self.soft, self.left)
-        ]
-
-    def x_faces(self, near, k):
-        heat, cond, acid, diff = near[:4]
-        faces = [
-            face(heat[k, i], heat[k + 1, i], cond[k, i], cond[k + 1, i])
-            for i in range(self.lines)
-        ]
+        heat, cond, acid, diff, soft, _ = self.state
+        for y in range(fine):
+            take = pl.ds(y, SUB, stride=fine)
+            for z in range(z_tiles):
+                for side in range(2):
+                    value = nat[side, x, z, take, :]
+                    heat[slot, self.at(side, y, z)] = value
+                    cond[slot, self.at(side, y, z)] = self.conductivity(value, z)
+            acid[slot, y] = frequency_multiplier * halves(
+                nat[0, x, z_tiles, take, :], nat[1, x, z_tiles, take, :]
+            )
+            value = halves(nat[0, x, 0, take, :], nat[1, x, 0, take, :])
+            soft[slot, y] = value
+            diff[slot, y] = mobility(value)
+
+    def x_faces(self, one, other):
+        heat, cond, acid, diff = one[:4]
+        heat_o, cond_o, acid_o, diff_o = other[:4]
+        faces = [face(heat[i], heat_o[i], cond[i], cond_o[i]) for i in range(self.lines)]
         return faces + [
-            face(acid[k, y], acid[k + 1, y], diff[k, y], diff[k + 1, y])
-            for y in range(self.fine)
+            face(acid[y], acid_o[y], diff[y], diff_o[y]) for y in range(self.fine)
         ]
 
     def y_gain(self, value, factor):
@@ -230,52 +230,50 @@
             before = turned
         return gain
 
-    def sink(self, near, k):
-        heat, cond, acid, diff = near[:4]
+    def sink(self, pair):
+        heat, cond, acid, diff = pair[:4]
         for side in range(2):
             for y in range(self.fine):
                 ids = [self.at(side, y, z) for z in range(self.z_tiles)]
-                faces = self.z_faces([heat[k, i] for i in ids], [cond[k, i] for i in ids])
+                faces = self.z_faces([heat[i] for i in ids], [cond[i] for i in ids])
                 for i, value in zip(ids, faces):
                     self.deep[i] = value
         for y in range(self.fine):
-            acd, dif = acid[k, y], diff[k, y]
+            acd, dif = acid[y], diff[y]
             self.deep[self.lines + y] = self.acid_face * face(
                 acd, pltpu.roll(acd, LANE - 1, 1), dif, pltpu.roll(dif, LANE - 1, 1)
             )
 
-    def gather(self, near, k, x, step):
-        heat, cond, acid, diff = near[:4]
+    def gather(self, pair, x, step):
+        heat, cond, acid, diff = pair[:4]
         fine, z_tiles = self.fine, self.z_tiles
         for side in range(2):
             row = x if side == 0 else self.wide_rows - 1 - x
             spot = self.spots[pl.ds(step * self.wide_rows + row, 1), :]
             ids = [[self.at(side, y, z) for y in range(fine)] for z in range(z_tiles)]
             across = [
-                self.y_gain([heat[k, i] for i in ids[z]], [cond[k, i] for i in ids[z]])
+                self.y_gain([heat[i] for i in ids[z]], [cond[i] for i in ids[z]])
                 for z in range(z_tiles)
             ]
             for y in range(fine):
                 down = self.z_gain([self.deep[ids[z][y]] for z in range(z_tiles)])
                 for z in range(z_tiles):
                     i = ids[z][y]
-                    new = heat[k, i] + spot * self.dose[y * z_tiles + z]
+                    new = heat[i] + spot * self.dose[y * z_tiles + z]
                     self.part[i] = new + across[z][y] + down[z]
-        acd = [acid[k, y] for y in range(fine)]
-        across = self.y_gain(acd, [diff[k, y] for y in range(fine)])
+        acd = [acid[y] for y in range(fine)]
+        across = self.y_gain(acd, [diff[y] for y in range(fine)])
         for y in range(fine):
             i = self.lines + y
             down = self.deep[i]
             self.part[i] = acd[y] + across[y] + (down - pltpu.roll(down, 1, 1))
 
-    def finish(self, near, k, x, step, cooling, before):
-        heat, cond, acid, _, soft, left = near
-        after = self.x_faces(near, k)
-        for y in range(self.fine):
-            rate = frequency_multiplier * jnp.exp(
-                -barrier_energy * reciprocal(1.0 + soft[k, y])
-            )
-            left[k, y] = left[k, y] * (1.0 - rate * acid[k, y])
+    def finish(self, pair, new_pair, x, step, cooling, before, after):
+        _, _, acid, _, soft, left = pair
+        new_heat, new_cond, new_acid, _, _, new_left = new_pair
+        for y in range(self.fine if x >= HALO else 0):
+            rate = jnp.exp2(exponent * reciprocal(1.0 + soft[y]))
+            new_left[y] = left[y] * (1.0 - rate * acid[y])
         for side in range(2):
             row = x if side == 0 else self.wide_rows - 1 - x
             if cooling:
@@ -288,56 +286,42 @@
                         new = new * kept
                     if y in self.edge_cols:
                         new = new * self.inside[y]
-                    heat[k, i] = new
-                    cond[k, i] = self.conductivity(new, z)
+                    new_heat[i] = new
+                    new_cond[i] = self.conductivity(new, z)
         for y in range(self.fine):
             i = self.lines + y
             new = self.part[i] + (after[i] - before[i])
             if y in self.edge_cols:
                 new = new * self.inside[y]
-            acid[k, y] = new
-        return after
-
-    def soften(self, near, k):
-        heat, diff, soft = near[0], near[3], near[4]
+            new_acid[y] = new
+
+    def soften(self, pair):
+        heat, _, _, diff, soft, _ = pair
         for y in range(self.fine):
-            warm = halves(heat[k, self.at(0, y, 0)], heat[k, self.at(1, y, 0)])
-            soft[k, y] = warm
-            diff[k, y] = mobility(warm)
-
-    def substep(self, step, cooling, begin, count):
-        first = self.window(begin)
-        self.sink(first, 1)
-        self.gather(first, 1, begin, step)
-        self.sink(first, 2)
-        for i, value in enumerate(self.x_faces(first, 0)):
-            self.flow[i] = value
-
-        def some_pairs(number, carry):
-            x = begin + number * UNROLL
-            near = self.window(x)
-            before = [self.flow[i] for i in range(self.flow.shape[0])]
-            for ahead in range(UNROLL):
-                k = ahead + 1
-                before = self.finish(near, k, x + ahead, step, cooling, before)
-                self.gather(near, k + 1, x + ahead + 1, step)
-                self.sink(near, k + 2)
-                self.soften(near, k - 1)
-            for i, value in enumerate(before):
-                self.flow[i] = value
-            return carry
-
-        lax.fori_loop(0, count, some_pairs, 0)
-        self.soften(self.window(begin + count * UNROLL), 0)
-
-
-def for_substeps(body):
-    def frame(number, carry):
-        for sub in range(SUBSTEPS):
-            body(number * SUBSTEPS + sub, sub == SUBSTEPS - 1)
-        return carry
-
-    lax.fori_loop(0, STEPS, frame, 0)
+            warm = halves(heat[self.at(0, y, 0)], heat[self.at(1, y, 0)])
+            soft[y] = warm
+            diff[y] = mobility(warm)
+
+    def slots(self, x, number):
+        return [[Line(ref, x - self.first + k) for ref in self.state] for k in range(number)]
+
+    def substep(self, step, cooling, begin, old, new):
+        number = len(new)
+        self.sink(old[1])
+        self.gather(old[1], begin, step)
+        if number > 1:
+            self.sink(old[2])
+        before = self.x_faces(old[0], old[1])
+        for ahead in range(number):
+            k = ahead + 1
+            after = self.x_faces(old[k], old[k + 1])
+            self.finish(old[k], new[ahead], begin + ahead, step, cooling, before, after)
+            self.soften(new[ahead])
+            before = after
+            if ahead + 1 < number:
+                self.gather(old[k + 1], begin + ahead + 1, step)
+            if ahead + 2 < number:
+                self.sink(old[k + 2])
 
 
 def make_tables(sizes, mesh_sizes, place, profile, start, steps, coeff, tables, column):
@@ -397,8 +381,8 @@
 def inner_kernel(
     sizes, mesh_sizes, place, start, steps, profile, coeff, own, cross_a, cross_b, *refs
 ):
-    row_heat, row_acid, row_left, next_heat, next_acid = refs[:5]
-    tables, (nat, column), state = refs[5:11], refs[11:13], refs[13:]
+    here, after, tables, refs = refs[:6], refs[6:10], refs[10:16], refs[16:]
+    nat, column, state = refs[0], refs[1], refs[2:]
     rows, cols, z_tiles, fine = sizes
     make_tables(sizes, mesh_sizes, place, profile, start, steps, coeff, tables, column)
     block = Block(sizes, HALO, state, tables)
@@ -420,38 +404,31 @@
                             value = turn(value)
                     nat[side, pair, z, pl.ds(column_at, HALO), :] = value
 
-    blank = jnp.zeros((SUB, LANE), jnp.float32)
-    for ref in (block.heat, block.cond, block.acid, block.diff, block.soft):
-        for i in range(ref.shape[1]):
-            ref[0, i] = blank
-
-    def load(x, carry):
-        block.fill_natural(x + 1, nat, x)
+    for pair in range(mine):
+        block.fill_natural(pair, nat, pair)
         for y in range(fine):
-            block.left[x + 1, y] = jnp.ones((SUB, LANE), jnp.float32)
-        return carry
-
-    lax.fori_loop(0, mine, load, 0)
-
-    def step_body(step, cooling):
+            block.state[5][pair, y] = jnp.ones((SUB, LANE), jnp.float32)
+
+    for step in range(HALO):
+        slots = block.slots(HALO, mine + 1)
+        heat, cond, acid, diff, _, _ = slots[mine]
+        heat_m, cond_m, acid_m, diff_m, _, _ = slots[mine - 1]
         for i in range(block.lines):
             j = (i + block.lines // 2) % block.lines
-            block.heat[mine + 1, i] = block.heat[mine, j]
-            block.cond[mine + 1, i] = block.cond[mine, j]
-            row_heat[step, i] = block.heat[step + 1, i]
+            heat[i] = heat_m[j]
+            cond[i] = cond_m[j]
         for y in range(fine):
-            block.acid[mine + 1, y] = turn(block.acid[mine, y])
-            block.diff[mine + 1, y] = turn(block.diff[mine, y])
-            row_acid[step, y] = block.acid[step + 1, y]
-            row_left[step, y] = block.left[step + 1, y]
-        for i in range(block.lines):
-            next_heat[step, i] = block.heat[step + 2, i]
-        for y in range(fine):
-            next_acid[step, y] = block.acid[step + 2, y]
-        count = (mine - 1 - step + UNROLL - 1) // UNROLL
-        block.substep(step, cooling, block.pairs - count * UNROLL, count)
-
-    for_substeps(step_body)
+            acid[y] = turn(acid_m[y])
+            diff[y] = turn(diff_m[y])
+        for out, ref in zip(here, slots[step]):
+            for i in range(ref.shape[0]):
+                out[step, i] = ref[i]
+        for out, ref in zip(after, slots[step + 1]):
+            for i in range(ref.shape[0]):
+                out[step, i] = ref[i]
+        if step + 1 < mine:
+            cooling = step % SUBSTEPS == SUBSTEPS - 1
+            block.substep(step, cooling, HALO + step + 1, slots[step:], slots[step + 1 : mine])
 
 
 def outer_kernel(
@@ -462,14 +439,10 @@
     scan_b,
     corner_a,
     corner_b,
-    row_heat,
-    row_acid,
-    row_left,
-    next_heat,
-    next_acid,
     *refs,
 ):
-    tables, out, nat, state = refs[:6], refs[6], refs[7], refs[8:]
+    here, after, tables, out, nat = refs[:6], refs[6:10], refs[10:16], refs[16], refs[17]
+    state = refs[18:]
     rows, cols, z_tiles, fine = sizes
     block = Block(sizes, 0, state, tables)
     odd_x = place[0] % 2
@@ -488,44 +461,29 @@
                 nat[side, x, z, :HALO, :] = restored(corner, 0, d + 1, z, z_tiles)
                 nat[side, x, z, HALO + cols :, :] = restored(corner, 1, d + 1, z, z_tiles)
 
-    blank = jnp.zeros((SUB, LANE), jnp.float32)
-    for ref in (block.heat, block.cond, block.acid, block.diff, block.soft):
-        for i in range(ref.shape[1]):
-            ref[0, i] = blank
-
-    def load(x, carry):
-        block.fill_natural(x + 1, nat, x)
-        return carry
-
-    lax.fori_loop(0, HALO, load, 0)
-
-    def step_body(step, cooling):
-        slot = step + HALO + 1
-        block.fill(
-            slot,
-            lambda side, y, z: row_heat[step, block.at(side, y, z)],
-            lambda y: row_acid[step, y],
-        )
-        for y in range(fine):
-            block.left[slot, y] = row_left[step, y]
-        block.fill(
-            slot + 1,
-            lambda side, y, z: next_heat[step, block.at(side, y, z)],
-            lambda y: next_acid[step, y],
-        )
-        block.substep(step, cooling, step + 1, HALO // UNROLL)
-
-    for_substeps(step_body)
-
-    def store(pair, carry):
-        slot = pair + HALO + 1
+    for x in range(HALO):
+        block.fill_natural(x, nat, x)
+
+    for step in range(HALO):
+
+        @pl.when(place[0] >= 0)
+        def _():
+            last = [Line(ref, step) for ref in here]
+            beyond = [Line(ref, step) for ref in after]
+            near = block.slots(step, HALO + 1)
+            cooling = step % SUBSTEPS == SUBSTEPS - 1
+            block.substep(step, cooling, step + 1, near[:HALO] + [last, beyond], near[1:])
+
+    for pair in range(mine):
+        slot = pair + HALO
+        heat, _, acid, _, _, left = block.state
         row = (pair, rows - 1 - pair)
         for y in range(fine):
             put = pl.ds(y, SUB, stride=fine)
             for side in range(2):
                 for z in range(z_tiles):
-                    nat[side, pair, z, put, :] = block.heat[slot, block.at(side, y, z)]
-            acd, kept = block.acid[slot, y], block.left[slot, y]
+                    nat[side, pair, z, put, :] = heat[slot, block.at(side, y, z)]
+            acd, kept = acid[slot, y] * (1.0 / frequency_multiplier), left[slot, y]
             low = lanes_of(acd.shape) < LANE // 2
             nat[0, pair, z_tiles, put, :] = jnp.where(low, acd, turn(kept))
             nat[1, pair, z_tiles, put, :] = jnp.where(low, turn(acd), kept)
@@ -538,9 +496,6 @@
             begun = own[row[side], :, z_tiles * LANE :]
             low = lanes_of(mixed.shape) < LANE // 2
             out[row[side], :, z_tiles * LANE :] = jnp.where(low, mixed, mixed * begun)
-        return carry
-
-    lax.fori_loop(0, mine, store, 0)
 
 
 def shards(wafer_state, layer_heat_coefficients, beam_profile, beam_start, beam_steps):
@@ -561,15 +516,10 @@
     def array(*shape):
         return jax.ShapeDtypeStruct(shape, jnp.float32)
 
+    wide = (lines, lines, fine, fine, fine, fine)
+
     def state(pairs):
-        return [
-            pltpu.VMEM((pairs + PAD, lines, SUB, LANE), jnp.float32),
-            pltpu.VMEM((pairs + PAD, lines, SUB, LANE), jnp.float32),
-            pltpu.VMEM((pairs + PAD, fine, SUB, LANE), jnp.float32),
-            pltpu.VMEM((pairs + PAD, fine, SUB, LANE), jnp.float32),
-            pltpu.VMEM((pairs + PAD, fine, SUB, LANE), jnp.float32),
-            pltpu.VMEM((pairs + PAD, fine, SUB, LANE), jnp.float32),
-            pltpu.VMEM((lines + fine, SUB, LANE), jnp.float32),
+        return [pltpu.VMEM((pairs, n, SUB, LANE), jnp.float32) for n in wide] + [
             pltpu.VMEM((lines + fine, SUB, LANE), jnp.float32),
             pltpu.VMEM((lines + fine, SUB, LANE), jnp.float32),
         ]
@@ -602,13 +552,7 @@
     corner_b = lax.ppermute(corner_b, "scan", pair_swap(scan_count, 1, True))
     corner_a = lax.ppermute(corner_a, "scan", pair_swap(scan_count, 0, True))
 
-    row_shapes = (
-        array(HALO, lines, SUB, LANE),
-        array(HALO, fine, SUB, LANE),
-        array(HALO, fine, SUB, LANE),
-        array(HALO, lines, SUB, LANE),
-        array(HALO, fine, SUB, LANE),
-    )
+    row_shapes = tuple(array(HALO, n, SUB, LANE) for n in wide + wide[:4])
     table_shapes = (
         array(HALO * wide_rows, LANE),
         array(STEPS * wide_rows, LANE),
@@ -626,7 +570,7 @@
             pltpu.VMEM((2, mine, z_tiles + 1, wide_cols, LANE), jnp.float32),
             pltpu.VMEM((wide_cols, LANE), jnp.float32),
         ]
-        + state(mine),
+        + state(mine + 1),
         compiler_params=params,
         cost_estimate=pl.CostEstimate(
             flops=50_000_000, bytes_accessed=8_000_000, transcendentals=1_000_000

time: 31.7 us -> 28.2 us (0.89)
  the two profiles are of different devices: /device:TPU:1 before, /device:TPU:11 now
where the time goes in v4:
time: 28.2 us; the launch traced here: 28.1 us
  Pallas kernels  14.3 us (51%)
  starting transfers between devices  8.88 us (31%)
  waiting for transfers between devices  3.72 us (13%)
  local copies, waits for them, and re-layouts  1.01 us (4%)
    pallas_call x1, Pallas kernels, shards(): pl.pallas_call(functools.partial(outer_kernel, sizes), out_shape=jax.Shap...  8.59 us
    pallas_call x1, Pallas kernels, shards(): pl.pallas_call(functools.partial(inner_kernel, sizes, (scan_count, cross_...  4.36 us
    ppermute x1, starting transfers between devices, shards(): cross_b = lax.ppermute(cross_b, 'cross', pair_swap(cross_count, 1, False))  3.1 us
    ppermute x1, waiting for transfers between devices, shards(): corner_b = lax.ppermute(corner_b, 'scan', pair_swap(scan_count, 1, True))  2.39 us
    ppermute x1, starting transfers between devices, shards(): corner_b = lax.ppermute(corner_b, 'scan', pair_swap(scan_count, 1, True))  2.23 us
    ppermute x1, starting transfers between devices, shards(): scan_b = lax.ppermute(scan_b, 'scan', pair_swap(scan_count, 1, True))  2.17 us
    ppermute x1, waiting for transfers between devices, shards(): cross_b = lax.ppermute(cross_b, 'cross', pair_swap(cross_count, 1, False))  1.32 us
    unnamed x12, local copies, waits for them, and re-layouts  1.01 us
  transfers between devices with their start and end apart: 6, of which 2 were waited for; matrix products, arithmetic and copies ran while one was open for 0% of the time, Pallas kernels for 18%

profile of v4, /device:TPU:11, one launch (start us, length us, event | category | flops | bytes accessed | tf_op | source)
XLA Modules:
  0.0 28.1 jit_solution(8560558298040342884)
XLA Ops:
  0.0 0.1 pad_add_fusion.place
  0.1 0.0 copy-start
  0.1 1.0 %copy-done = f32[16,16,384]{2,1,0:T(8,128)S(1)} copy-done((f32[16,16,384]{2,1,0:T(8,128)S(1)}, f32[16,16,384]{2,1,0:T(8,128)}, u32[]{:S(2)}) %copy-start) | copy-done | bytes 393240
  1.1 0.0 copy-start.1
  1.1 0.7 %pack.1 = (f32[20,16,128]{2,1,0:T(8,128)S(1)}, f32[20,16,128]{2,1,0:T(8,128)S(1)}, f32[40,8,128]{2,1,0:T(8,128)S(1)}, f32[40,8,128]{2,1,0:T(8,128)S(1)}) custom-call(s32[2]{0:T(128)S(1)} %pad_add_fusion.place, f32[16,16,384]{2,1,0:T(8,128)S(1)} %copy-done), custom_call_target="tpu_custom_call" | custom-call | tf_op jit(solution)/shard_map/pack/pallas_call | solution.py:530
  1.7 0.7 %collective-permute-start.2 = (f32[40,8,128]{2,1,0:T(8,128)S(1)}, f32[40,8,128]{2,1,0:T(8,128)S(1)}, u32[]{:S(2)}, u32[]{:S(2)}) collective-permute-start(f32[40,8,128]{2,1,0:T(8,128)S(1)} %get-tuple-element.29), channel_id=1, source_target_pairs={{0,1},{1,0},{2,3},{3,2},{4,5},{5,4},{6,7},{7,6},{8,9},{9,8},{10,11... | collective-permute-start | bytes 491528 | tf_op jit(solution)/shard_map/ppermute | solution.py:540
  2.5 3.1 %collective-permute-start.3 = (f32[40,8,128]{2,1,0:T(8,128)S(1)}, f32[40,8,128]{2,1,0:T(8,128)S(1)}, u32[]{:S(2)}, u32[]{:S(2)}) collective-permute-start(f32[40,8,128]{2,1,0:T(8,128)S(1)} %get-tuple-element.30), channel_id=1, source_target_pairs={{1,2},{2,1},{3,4},{4,3},{5,6},{6,5},{9,10},{10,9},{11,12},{12,11},... | collective-permute-start | bytes 491528 | tf_op jit(solution)/shard_map/ppermute | solution.py:539
  5.6 0.3 %collective-permute-start = (f32[20,16,128]{2,1,0:T(8,128)S(1)}, f32[20,16,128]{2,1,0:T(8,128)S(1)}, u32[]{:S(2)}, u32[]{:S(2)}) collective-permute-start(f32[20,16,128]{2,1,0:T(8,128)S(1)} %get-tuple-element.27), channel_id=1, source_target_pairs={{0,8},{8,0},{16,24},{24,16},{1,9},{9,1},{17,25},{25,17},{2,10},{10... | collective-permute-start | bytes 491528 | tf_op jit(solution)/shard_map/ppermute | solution.py:542
  5.9 2.2 %collective-permute-start.1 = (f32[20,16,128]{2,1,0:T(8,128)S(1)}, f32[20,16,128]{2,1,0:T(8,128)S(1)}, u32[]{:S(2)}, u32[]{:S(2)}) collective-permute-start(f32[20,16,128]{2,1,0:T(8,128)S(1)} %get-tuple-element.28), channel_id=1, source_target_pairs={{8,16},{16,8},{24,0},{0,24},{9,17},{17,9},{25,1},{1,25},{10,18},{1... | collective-permute-start | bytes 491528 | tf_op jit(solution)/shard_map/ppermute | solution.py:541
  8.1 0.0 collective-permute-done.2.cross_a
  8.1 1.3 %collective-permute-done.3.cross_b = f32[40,8,128]{2,1,0:T(8,128)S(1)} collective-permute-done((f32[40,8,128]{2,1,0:T(8,128)S(1)}, f32[40,8,128]{2,1,0:T(8,128)S(1)}, u32[]{:S(2)}, u32[]{:S(2)}) %collective-permute-start.3) | collective-permute-done | bytes 163872 | tf_op jit(solution)/shard_map/ppermute | solution.py:539
  9.4 0.7 %corners.1 = (f32[20,8,128]{2,1,0:T(8,128)S(1)}, f32[20,8,128]{2,1,0:T(8,128)S(1)}) custom-call(s32[2]{0:T(128)S(1)} %pad_add_fusion.place, f32[40,8,128]{2,1,0:T(8,128)S(1)} %collective-permute-done.2.cross_a, f32[40,8,128]{2,1,0:T(8,128)S(1)} %collective-permute-done.3.cross_b), custom_call_target="tpu_custom_call" | custom-call | tf_op jit(solution)/shard_map/corners/pallas_call | solution.py:544
  10.1 0.3 %collective-permute-start.4 = (f32[20,8,128]{2,1,0:T(8,128)S(1)}, f32[20,8,128]{2,1,0:T(8,128)S(1)}, u32[]{:S(2)}, u32[]{:S(2)}) collective-permute-start(f32[20,8,128]{2,1,0:T(8,128)S(1)} %get-tuple-element.31), channel_id=1, source_target_pairs={{0,8},{8,0},{16,24},{24,16},{1,9},{9,1},{17,25},{25,17},{2,10},{10... | collective-permute-start | bytes 245768 | tf_op jit(solution)/shard_map/ppermute | solution.py:553
  10.4 0.0 copy-start.4
  10.4 0.0 copy-start.5
  10.4 0.0 copy-start.2
  10.4 0.0 copy-start.3
  10.5 2.2 %collective-permute-start.5 = (f32[20,8,128]{2,1,0:T(8,128)S(1)}, f32[20,8,128]{2,1,0:T(8,128)S(1)}, u32[]{:S(2)}, u32[]{:S(2)}) collective-permute-start(f32[20,8,128]{2,1,0:T(8,128)S(1)} %get-tuple-element.32), channel_id=1, source_target_pairs={{8,16},{16,8},{24,0},{0,24},{9,17},{17,9},{25,1},{1,25},{10,18},{1... | collective-permute-start | bytes 245768 | tf_op jit(solution)/shard_map/ppermute | solution.py:552
  12.7 0.0 copy-done.1
  12.7 0.0 copy-done.4
  12.7 0.0 copy-done.5
  12.7 0.0 copy-done.2
  12.7 0.0 copy-done.3
  12.7 4.4 %inner.1 = (f32[8,16,8,128]{3,2,1,0:T(8,128)S(1)}, f32[8,16,8,128]{3,2,1,0:T(8,128)S(1)}, f32[8,4,8,128]{3,2,1,0:T(8,128)S(1)}, f32[8,4,8,128]{3,2,1,0:T(8,128)S...) custom-call(s32[2]{0:T(128)S(1)} %pad_add_fusion.place, ...), custom_call_target="tpu_custom_call" | custom-call | flops 50000000 | bytes 8000000 | tf_op jit(solution)/shard_map/inner/pallas_call | solution.py:564
  17.1 0.0 collective-permute-done.scan_a
  17.1 0.0 collective-permute-done.1.scan_b
  17.1 0.0 collective-permute-done.4.corner_a
  17.1 2.4 %collective-permute-done.5.corner_b = f32[20,8,128]{2,1,0:T(8,128)S(1)} collective-permute-done((f32[20,8,128]{2,1,0:T(8,128)S(1)}, f32[20,8,128]{2,1,0:T(8,128)S(1)}, u32[]{:S(2)}, u32[]{:S(2)}) %collective-permute-start.5) | collective-permute-done | bytes 81952 | tf_op jit(solution)/shard_map/ppermute | solution.py:552
  19.5 8.6 %outer.1 = f32[16,16,384]{2,1,0:T(8,128)} custom-call(s32[2]{0:T(128)S(1)} %pad_add_fusion.place, f32[16,16,384]{2,1,0:T(8,128)S(1)} %copy-done.1, f32[20,16,128]{2,1,0:T(8,128)S(1)} %collective-permute-done.scan_a, f32[20,16,128]{2,1,0:T(8,128)S(1)} %collective-permute-done.1.scan_b, f32[20,8,128]{2,1,0:T(8,128)S(1)} %collective-permute-done.4.corner_a, ...), custom_call_target="tpu_custom_call" | custom-call | tf_op jit(solution)/shard_map/outer/pallas_call | solution.py:589
Async XLA Ops:
  0.1 1.0 %copy-start = (f32[16,16,384]{2,1,0:T(8,128)S(1)}, f32[16,16,384]{2,1,0:T(8,128)}, u32[]{:S(2)}) copy-start(f32[16,16,384]{2,1,0:T(8,128)} %own.5) | copy-start | bytes 1179652
  1.1 11.6 %copy-start.1 = (f32[16,16,384]{2,1,0:T(8,128)S(1)}, f32[16,16,384]{2,1,0:T(8,128)}, u32[]{:S(2)}) copy-start(f32[16,16,384]{2,1,0:T(8,128)} %own.5) | copy-start | bytes 1179652
  1.7 6.3 %collective-permute-start.2 = (f32[40,8,128]{2,1,0:T(8,128)S(1)}, f32[40,8,128]{2,1,0:T(8,128)S(1)}, u32[]{:S(2)}, u32[]{:S(2)}) collective-permute-start(f32[40,8,128]{2,1,0:T(8,128)S(1)} %get-tuple-element.29), channel_id=1, source_target_pairs={{0,1},{1,0},{2,3},{3,2},{4,5},{5,4},{6,7},{7,6},{8,9},{9,8},{10,11... | collective-permute-start | bytes 491528 | tf_op jit(solution)/shard_map/ppermute | solution.py:540
  2.5 6.9 %collective-permute-start.3 = (f32[40,8,128]{2,1,0:T(8,128)S(1)}, f32[40,8,128]{2,1,0:T(8,128)S(1)}, u32[]{:S(2)}, u32[]{:S(2)}) collective-permute-start(f32[40,8,128]{2,1,0:T(8,128)S(1)} %get-tuple-element.30), channel_id=1, source_target_pairs={{1,2},{2,1},{3,4},{4,3},{5,6},{6,5},{9,10},{10,9},{11,12},{12,11},... | collective-permute-start | bytes 491528 | tf_op jit(solution)/shard_map/ppermute | solution.py:539
  5.6 11.5 %collective-permute-start = (f32[20,16,128]{2,1,0:T(8,128)S(1)}, f32[20,16,128]{2,1,0:T(8,128)S(1)}, u32[]{:S(2)}, u32[]{:S(2)}) collective-permute-start(f32[20,16,128]{2,1,0:T(8,128)S(1)} %get-tuple-element.27), channel_id=1, source_target_pairs={{0,8},{8,0},{16,24},{24,16},{1,9},{9,1},{17,25},{25,17},{2,10},{10... | collective-permute-start | bytes 491528 | tf_op jit(solution)/shard_map/ppermute | solution.py:542
  5.9 11.2 %collective-permute-start.1 = (f32[20,16,128]{2,1,0:T(8,128)S(1)}, f32[20,16,128]{2,1,0:T(8,128)S(1)}, u32[]{:S(2)}, u32[]{:S(2)}) collective-permute-start(f32[20,16,128]{2,1,0:T(8,128)S(1)} %get-tuple-element.28), channel_id=1, source_target_pairs={{8,16},{16,8},{24,0},{0,24},{9,17},{17,9},{25,1},{1,25},{10,18},{1... | collective-permute-start | bytes 491528 | tf_op jit(solution)/shard_map/ppermute | solution.py:541
  10.1 7.0 %collective-permute-start.4 = (f32[20,8,128]{2,1,0:T(8,128)S(1)}, f32[20,8,128]{2,1,0:T(8,128)S(1)}, u32[]{:S(2)}, u32[]{:S(2)}) collective-permute-start(f32[20,8,128]{2,1,0:T(8,128)S(1)} %get-tuple-element.31), channel_id=1, source_target_pairs={{0,8},{8,0},{16,24},{24,16},{1,9},{9,1},{17,25},{25,17},{2,10},{10... | collective-permute-start | bytes 245768 | tf_op jit(solution)/shard_map/ppermute | solution.py:553
  10.4 2.2 %copy-start.4 = (s32[4]{0:T(128)S(1)}, s32[4]{0:T(128)}, u32[]{:S(2)}) copy-start(s32[4]{0:T(128)} %steps.1) | copy-start | bytes 52
  10.4 2.2 %copy-start.5 = (f32[128]{0:T(128)S(1)}, f32[128]{0:T(128)}, u32[]{:S(2)}) copy-start(f32[128]{0:T(128)} %profile.1) | copy-start | bytes 1540
  10.4 2.2 %copy-start.2 = (f32[256]{0:T(256)S(1)}, f32[256]{0:T(256)}, u32[]{:S(2)}) copy-start(f32[256]{0:T(256)} %param.6) | copy-start | bytes 3076
  10.4 2.3 %copy-start.3 = (s32[4]{0:T(128)S(1)}, s32[4]{0:T(128)}, u32[]{:S(2)}) copy-start(s32[4]{0:T(128)} %start.1) | copy-start | bytes 52
  10.5 9.0 %collective-permute-start.5 = (f32[20,8,128]{2,1,0:T(8,128)S(1)}, f32[20,8,128]{2,1,0:T(8,128)S(1)}, u32[]{:S(2)}, u32[]{:S(2)}) collective-permute-start(f32[20,8,128]{2,1,0:T(8,128)S(1)} %get-tuple-element.32), channel_id=1, source_target_pairs={{8,16},{16,8},{24,0},{0,24},{9,17},{17,9},{25,1},{1,25},{10,18},{1... | collective-permute-start | bytes 245768 | tf_op jit(solution)/shard_map/ppermute | solution.py:552

commit v5 on v4

--- a/solution.py
+++ b/solution.py
@@ -52,34 +52,50 @@
     return jnp.where(lanes_of(low.shape) < LANE // 2, low, turn(high))
 
 
-def pack_kernel(z_tiles, place, own, scan_a, scan_b, cross_a, cross_b):
+def position():
+    return lax.axis_index("scan"), lax.axis_index("cross")
+
+
+def acid_pair(z_tiles, own, first, second, span):
+    tile = slice(z_tiles * LANE, (z_tiles + 1) * LANE)
+    return halves(own[first, span, tile], own[second, span, tile])
+
+
+def pack_scan(z_tiles, own, out, low_end):
+    rows = own.shape[0]
+
+    def row(d):
+        return jnp.where(low_end == 1, rows - 1 - d, d)
+
+    for d in range(HALO):
+        for z in range(z_tiles):
+            out[d * z_tiles + z] = own[row(d), :, z * LANE : (z + 1) * LANE]
+    for d in range(HALO // 2):
+        out[HALO * z_tiles + d] = acid_pair(
+            z_tiles, own, row(d), row(d + HALO // 2), slice(None)
+        )
+
+
+def first_pack_kernel(z_tiles, own, scan_b):
+    pack_scan(z_tiles, own, scan_b, position()[0] % 2)
+
+
+def second_pack_kernel(z_tiles, own, _, scan_a, cross_a, cross_b):
     rows, cols, _ = own.shape
-    odd_x, odd_y = place[0] % 2, place[1] % 2
-
-    def acid_pair(first, second, span):
-        tile = slice(z_tiles * LANE, (z_tiles + 1) * LANE)
-        return halves(own[first, span, tile], own[second, span, tile])
-
-    for out, low_end in ((scan_a, 1 - odd_x), (scan_b, odd_x)):
-        def row(d):
-            return jnp.where(low_end == 1, rows - 1 - d, d)
-
-        for d in range(HALO):
-            for z in range(z_tiles):
-                out[d * z_tiles + z] = own[row(d), :, z * LANE : (z + 1) * LANE]
-        for d in range(HALO // 2):
-            out[HALO * z_tiles + d] = acid_pair(row(d), row(d + HALO // 2), slice(None))
+    odd_x, odd_y = position()[0] % 2, position()[1] % 2
     for out, right_end in ((cross_a, 1 - odd_y), (cross_b, odd_y)):
         span = pl.ds(pl.multiple_of(right_end * (cols - HALO), SUB), HALO)
         for x in range(rows):
             for z in range(z_tiles):
                 out[x * z_tiles + z] = own[x, span, z * LANE : (z + 1) * LANE]
         for x in range(rows // 2):
-            out[rows * z_tiles + x] = acid_pair(x, x + rows // 2, span)
-
-
-def corner_kernel(z_tiles, place, cross_a, cross_b, corner_a, corner_b):
+            out[rows * z_tiles + x] = acid_pair(z_tiles, own, x, x + rows // 2, span)
+    pack_scan(z_tiles, own, scan_a, 1 - odd_x)
+
+
+def corner_kernel(z_tiles, cross_a, cross_b, corner_a, corner_b):
     rows = cross_a.shape[0] * 2 // (2 * z_tiles + 1)
+    place = position()
     odd_x, odd_y = place[0] % 2, place[1] % 2
     half = HALO // 2
     spot = lax.broadcasted_iota(jnp.int32, (SUB, LANE), 0)
@@ -379,11 +395,12 @@
 
 
 def inner_kernel(
-    sizes, mesh_sizes, place, start, steps, profile, coeff, own, cross_a, cross_b, *refs
+    sizes, mesh_sizes, start, steps, profile, coeff, own, cross_a, cross_b, *refs
 ):
     here, after, tables, refs = refs[:6], refs[6:10], refs[10:16], refs[16:]
     nat, column, state = refs[0], refs[1], refs[2:]
     rows, cols, z_tiles, fine = sizes
+    place = position()
     make_tables(sizes, mesh_sizes, place, profile, start, steps, coeff, tables, column)
     block = Block(sizes, HALO, state, tables)
     odd_y = place[1] % 2
@@ -433,7 +450,6 @@
 
 def outer_kernel(
     sizes,
-    place,
     own,
     scan_a,
     scan_b,
@@ -445,6 +461,7 @@
     state = refs[18:]
     rows, cols, z_tiles, fine = sizes
     block = Block(sizes, 0, state, tables)
+    place = position()
     odd_x = place[0] % 2
     mine = block.pairs - HALO
     for scan, corner, side in ((scan_a, corner_a, 1 - odd_x), (scan_b, corner_b, odd_x)):
@@ -502,7 +519,6 @@
     rows, cols, depth = wafer_state.shape
     deep = layer_heat_coefficients.shape[0]
     scan_count, cross_count = lax.axis_size("scan"), lax.axis_size("cross")
-    place = jnp.stack([lax.axis_index("scan"), lax.axis_index("cross")]).astype(jnp.int32)
     wide_rows, wide_cols = rows + 2 * HALO, cols + 2 * HALO
     z_tiles = deep // LANE
     fine = wide_cols // SUB
@@ -527,28 +543,36 @@
     scan_message = array(HALO * z_tiles + HALO // 2, cols, LANE)
     cross_message = array(rows * z_tiles + rows // 2, HALO, LANE)
     corner_message = array(HALO * z_tiles + HALO // 2, HALO, LANE)
-    scan_a, scan_b, cross_a, cross_b = pl.pallas_call(
-        functools.partial(pack_kernel, z_tiles),
-        out_shape=(scan_message, scan_message, cross_message, cross_message),
-        in_specs=[smem, vmem],
-        out_specs=(vmem,) * 4,
+    scan_b = pl.pallas_call(
+        functools.partial(first_pack_kernel, z_tiles),
+        out_shape=scan_message,
+        in_specs=[vmem],
+        out_specs=vmem,
         compiler_params=params,
-        name="pack",
-    )(place, wafer_state)
-
+        name="pack_first",
+    )(wafer_state)
+    scan_a, cross_a, cross_b = pl.pallas_call(
+        functools.partial(second_pack_kernel, z_tiles),
+        out_shape=(scan_message, cross_message, cross_message),
+        in_specs=[vmem, pl.BlockSpec(memory_space=pl.ANY)],
+        out_specs=(vmem,) * 3,
+        compiler_params=params,
+        name="pack_second",
+    )(wafer_state, scan_b)
+
+    scan_b = lax.ppermute(scan_b, "scan", pair_swap(scan_count, 1, True))
     cross_b = lax.ppermute(cross_b, "cross", pair_swap(cross_count, 1, False))
     cross_a = lax.ppermute(cross_a, "cross", pair_swap(cross_count, 0, False))
-    scan_b = lax.ppermute(scan_b, "scan", pair_swap(scan_count, 1, True))
     scan_a = lax.ppermute(scan_a, "scan", pair_swap(scan_count, 0, True))
 
     corner_a, corner_b = pl.pallas_call(
         functools.partial(corner_kernel, z_tiles),
         out_shape=(corner_message, corner_message),
-        in_specs=[smem, vmem, vmem],
+        in_specs=[vmem, vmem],
         out_specs=(vmem,) * 2,
         compiler_params=params,
         name="corners",
-    )(place, cross_a, cross_b)
+    )(cross_a, cross_b)
     corner_b = lax.ppermute(corner_b, "scan", pair_swap(scan_count, 1, True))
     corner_a = lax.ppermute(corner_a, "scan", pair_swap(scan_count, 0, True))
 
@@ -564,7 +588,7 @@
     inner = pl.pallas_call(
         functools.partial(inner_kernel, sizes, (scan_count, cross_count)),
         out_shape=row_shapes + table_shapes,
-        in_specs=[smem] * 4 + [vmem] * 4,
+        in_specs=[smem] * 3 + [vmem] * 4,
         out_specs=(vmem,) * (len(row_shapes) + len(table_shapes)),
         scratch_shapes=[
             pltpu.VMEM((2, mine, z_tiles + 1, wide_cols, LANE), jnp.float32),
@@ -577,7 +601,6 @@
         ),
         name="inner",
     )(
-        place,
         beam_start,
         beam_steps,
         beam_profile,
@@ -589,13 +612,13 @@
     result = pl.pallas_call(
         functools.partial(outer_kernel, sizes),
         out_shape=jax.ShapeDtypeStruct(wafer_state.shape, wafer_state.dtype),
-        in_specs=[smem] + [vmem] * (5 + len(inner)),
+        in_specs=[vmem] * (5 + len(inner)),
         out_specs=vmem,
         scratch_shapes=[pltpu.VMEM((2, mine, z_tiles + 1, wide_cols, LANE), jnp.float32)]
         + state(HALO + mine),
         compiler_params=params,
         name="outer",
-    )(place, wafer_state, scan_a, scan_b, corner_a, corner_b, *inner)
+    )(wafer_state, scan_a, scan_b, corner_a, corner_b, *inner)
     lag_blocks = STEPS % scan_count
     if lag_blocks:
         pairs = [(source, (source - lag_blocks) % scan_count) for source in range(scan_count)]

time: 28.2 us -> 27.5 us (0.975)
  the two profiles are of different devices: /device:TPU:11 before, /device:TPU:13 now
where the time goes in v5:
time: 27.5 us; the launch traced here: 27.3 us
  Pallas kernels  13 us (47%)
  starting transfers between devices  6.85 us (25%)
  waiting for transfers between devices  5.96 us (22%)
  local copies, waits for them, and re-layouts  1.44 us (5%)
    pallas_call x1, Pallas kernels, shards(): pl.pallas_call(functools.partial(outer_kernel, sizes), out_shape=jax.Shap...  8.45 us
    pallas_call x1, Pallas kernels, shards(): pl.pallas_call(functools.partial(inner_kernel, sizes, (scan_count, cross_...  4.23 us
    ppermute x1, starting transfers between devices, shards(): cross_b = lax.ppermute(cross_b, 'cross', pair_swap(cross_count, 1, False))  3.1 us
    ppermute x1, waiting for transfers between devices, shards(): corner_b = lax.ppermute(corner_b, 'scan', pair_swap(scan_count, 1, True))  2.69 us
    ppermute x1, waiting for transfers between devices, shards(): cross_b = lax.ppermute(cross_b, 'cross', pair_swap(cross_count, 1, False))  2.33 us
    unnamed x12, local copies, waits for them, and re-layouts  1.44 us
    ppermute x1, starting transfers between devices, shards(): corner_a = lax.ppermute(corner_a, 'scan', pair_swap(scan_count, 0, True))  1.28 us
    ppermute x1, starting transfers between devices, shards(): scan_b = lax.ppermute(scan_b, 'scan', pair_swap(scan_count, 1, True))  1.22 us
  transfers between devices with their start and end apart: 6, of which 3 were waited for; matrix products, arithmetic and copies ran while one was open for 0% of the time, Pallas kernels for 16%

profile of v5, /device:TPU:13, one launch (start us, length us, event | category | flops | bytes accessed | tf_op | source)
XLA Modules:
  0.0 27.3 jit_solution(9444108100244956876)
XLA Ops:
  0.0 0.0 copy-start
  0.0 1.0 %copy-done = f32[16,16,384]{2,1,0:T(8,128)S(1)} copy-done((f32[16,16,384]{2,1,0:T(8,128)S(1)}, f32[16,16,384]{2,1,0:T(8,128)}, u32[]{:S(2)}) %copy-start) | copy-done | bytes 393240
  1.0 0.1 pack_first.1._
  1.1 0.0 copy-start.1
  1.1 0.1 pack_second.1
  1.2 0.7 %collective-permute-start.2 = (f32[40,8,128]{2,1,0:T(8,128)S(1)}, f32[40,8,128]{2,1,0:T(8,128)S(1)}, u32[]{:S(2)}, u32[]{:S(2)}) collective-permute-start(f32[40,8,128]{2,1,0:T(8,128)S(1)} %get-tuple-element.27), channel_id=1, source_target_pairs={{0,1},{1,0},{2,3},{3,2},{4,5},{5,4},{6,7},{7,6},{8,9},{9,8},{10,11... | collective-permute-start | bytes 491528 | tf_op jit(solution)/shard_map/ppermute | solution.py:565
  1.9 3.1 %collective-permute-start.3 = (f32[40,8,128]{2,1,0:T(8,128)S(1)}, f32[40,8,128]{2,1,0:T(8,128)S(1)}, u32[]{:S(2)}, u32[]{:S(2)}) collective-permute-start(f32[40,8,128]{2,1,0:T(8,128)S(1)} %get-tuple-element.28), channel_id=1, source_target_pairs={{1,2},{2,1},{3,4},{4,3},{5,6},{6,5},{9,10},{10,9},{11,12},{12,11},... | collective-permute-start | bytes 491528 | tf_op jit(solution)/shard_map/ppermute | solution.py:564
  5.0 1.2 %collective-permute-start.1 = (f32[20,16,128]{2,1,0:T(8,128)S(1)}, f32[20,16,128]{2,1,0:T(8,128)S(1)}, u32[]{:S(2)}, u32[]{:S(2)}) collective-permute-start(f32[20,16,128]{2,1,0:T(8,128)S(1)} %pack_first.1._), channel_id=1, source_target_pairs={{8,16},{16,8},{24,0},{0,24},{9,17},{17,9},{25,1},{1,25},{10,18},{1... | collective-permute-start | bytes 491528 | tf_op jit(solution)/shard_map/ppermute | solution.py:563
  6.3 0.3 collective-permute-start
  6.5 0.0 collective-permute-done.2.cross_a
  6.5 2.3 %collective-permute-done.3.cross_b = f32[40,8,128]{2,1,0:T(8,128)S(1)} collective-permute-done((f32[40,8,128]{2,1,0:T(8,128)S(1)}, f32[40,8,128]{2,1,0:T(8,128)S(1)}, u32[]{:S(2)}, u32[]{:S(2)}) %collective-permute-start.3) | collective-permute-done | bytes 163872 | tf_op jit(solution)/shard_map/ppermute | solution.py:564
  8.9 0.2 corners.1
  9.0 1.3 %collective-permute-start.4 = (f32[20,8,128]{2,1,0:T(8,128)S(1)}, f32[20,8,128]{2,1,0:T(8,128)S(1)}, u32[]{:S(2)}, u32[]{:S(2)}) collective-permute-start(f32[20,8,128]{2,1,0:T(8,128)S(1)} %get-tuple-element.29), channel_id=1, source_target_pairs={{0,8},{8,0},{16,24},{24,16},{1,9},{9,1},{17,25},{25,17},{2,10},{10... | collective-permute-start | bytes 245768 | tf_op jit(solution)/shard_map/ppermute | solution.py:577
  10.3 0.0 copy-start.4
  10.3 0.0 copy-start.5
  10.3 0.0 copy-start.2
  10.3 0.0 copy-start.3
  10.3 0.3 collective-permute-start.5
  10.6 0.0 copy-done.1
  10.6 0.4 %copy-done.4 = s32[4]{0:T(128)S(1)} copy-done((s32[4]{0:T(128)S(1)}, s32[4]{0:T(128)}, u32[]{:S(2)}) %copy-start.4) | copy-done | bytes 40
  11.0 0.0 copy-done.5
  11.0 0.0 copy-done.2
  11.0 0.0 copy-done.3
  11.0 4.2 %inner.1 = (f32[8,16,8,128]{3,2,1,0:T(8,128)S(1)}, f32[8,16,8,128]{3,2,1,0:T(8,128)S(1)}, f32[8,4,8,128]{3,2,1,0:T(8,128)S(1)}, f32[8,4,8,128]{3,2,1,0:T(8,128)S...) custom-call(s32[4]{0:T(128)S(1)} %copy-done.3, ...), custom_call_target="tpu_custom_call" | custom-call | flops 50000000 | bytes 8000000 | tf_op jit(solution)/shard_map/inner/pallas_call | solution.py:588
  15.3 0.0 collective-permute-done.1.scan_b
  15.3 0.0 collective-permute-done.scan_a
  15.3 0.9 %collective-permute-done.4.corner_a = f32[20,8,128]{2,1,0:T(8,128)S(1)} collective-permute-done((f32[20,8,128]{2,1,0:T(8,128)S(1)}, f32[20,8,128]{2,1,0:T(8,128)S(1)}, u32[]{:S(2)}, u32[]{:S(2)}) %collective-permute-start.4) | collective-permute-done | bytes 81952 | tf_op jit(solution)/shard_map/ppermute | solution.py:577
  16.2 2.7 %collective-permute-done.5.corner_b = f32[20,8,128]{2,1,0:T(8,128)S(1)} collective-permute-done((f32[20,8,128]{2,1,0:T(8,128)S(1)}, f32[20,8,128]{2,1,0:T(8,128)S(1)}, u32[]{:S(2)}, u32[]{:S(2)}) %collective-permute-start.5) | collective-permute-done | bytes 81952 | tf_op jit(solution)/shard_map/ppermute | solution.py:576
  18.9 8.4 %outer.1 = f32[16,16,384]{2,1,0:T(8,128)} custom-call(f32[16,16,384]{2,1,0:T(8,128)S(1)} %copy-done.1, f32[20,16,128]{2,1,0:T(8,128)S(1)} %collective-permute-done.scan_a, f32[20,16,128]{2,1,0:T(8,128)S(1)} %collective-permute-done.1.scan_b, f32[20,8,128]{2,1,0:T(8,128)S(1)} %collective-permute-done.4.corner_a, ...), custom_call_target="tpu_custom_call" | custom-call | tf_op jit(solution)/shard_map/outer/pallas_call | solution.py:612
Async XLA Ops:
  0.0 1.0 %copy-start = (f32[16,16,384]{2,1,0:T(8,128)S(1)}, f32[16,16,384]{2,1,0:T(8,128)}, u32[]{:S(2)}) copy-start(f32[16,16,384]{2,1,0:T(8,128)} %own.7) | copy-start | bytes 1179652
  1.1 9.5 %copy-start.1 = (f32[16,16,384]{2,1,0:T(8,128)S(1)}, f32[16,16,384]{2,1,0:T(8,128)}, u32[]{:S(2)}) copy-start(f32[16,16,384]{2,1,0:T(8,128)} %own.7) | copy-start | bytes 1179652
  1.2 5.3 %collective-permute-start.2 = (f32[40,8,128]{2,1,0:T(8,128)S(1)}, f32[40,8,128]{2,1,0:T(8,128)S(1)}, u32[]{:S(2)}, u32[]{:S(2)}) collective-permute-start(f32[40,8,128]{2,1,0:T(8,128)S(1)} %get-tuple-element.27), channel_id=1, source_target_pairs={{0,1},{1,0},{2,3},{3,2},{4,5},{5,4},{6,7},{7,6},{8,9},{9,8},{10,11... | collective-permute-start | bytes 491528 | tf_op jit(solution)/shard_map/ppermute | solution.py:565
  1.9 6.9 %collective-permute-start.3 = (f32[40,8,128]{2,1,0:T(8,128)S(1)}, f32[40,8,128]{2,1,0:T(8,128)S(1)}, u32[]{:S(2)}, u32[]{:S(2)}) collective-permute-start(f32[40,8,128]{2,1,0:T(8,128)S(1)} %get-tuple-element.28), channel_id=1, source_target_pairs={{1,2},{2,1},{3,4},{4,3},{5,6},{6,5},{9,10},{10,9},{11,12},{12,11},... | collective-permute-start | bytes 491528 | tf_op jit(solution)/shard_map/ppermute | solution.py:564
  5.0 10.2 %collective-permute-start.1 = (f32[20,16,128]{2,1,0:T(8,128)S(1)}, f32[20,16,128]{2,1,0:T(8,128)S(1)}, u32[]{:S(2)}, u32[]{:S(2)}) collective-permute-start(f32[20,16,128]{2,1,0:T(8,128)S(1)} %pack_first.1._), channel_id=1, source_target_pairs={{8,16},{16,8},{24,0},{0,24},{9,17},{17,9},{25,1},{1,25},{10,18},{1... | collective-permute-start | bytes 491528 | tf_op jit(solution)/shard_map/ppermute | solution.py:563
  6.3 9.0 %collective-permute-start = (f32[20,16,128]{2,1,0:T(8,128)S(1)}, f32[20,16,128]{2,1,0:T(8,128)S(1)}, u32[]{:S(2)}, u32[]{:S(2)}) collective-permute-start(f32[20,16,128]{2,1,0:T(8,128)S(1)} %get-tuple-element.26), channel_id=1, source_target_pairs={{0,8},{8,0},{16,24},{24,16},{1,9},{9,1},{17,25},{25,17},{2,10},{10... | collective-permute-start | bytes 491528 | tf_op jit(solution)/shard_map/ppermute | solution.py:566
  9.0 7.2 %collective-permute-start.4 = (f32[20,8,128]{2,1,0:T(8,128)S(1)}, f32[20,8,128]{2,1,0:T(8,128)S(1)}, u32[]{:S(2)}, u32[]{:S(2)}) collective-permute-start(f32[20,8,128]{2,1,0:T(8,128)S(1)} %get-tuple-element.29), channel_id=1, source_target_pairs={{0,8},{8,0},{16,24},{24,16},{1,9},{9,1},{17,25},{25,17},{2,10},{10... | collective-permute-start | bytes 245768 | tf_op jit(solution)/shard_map/ppermute | solution.py:577
  10.3 0.7 %copy-start.4 = (s32[4]{0:T(128)S(1)}, s32[4]{0:T(128)}, u32[]{:S(2)}) copy-start(s32[4]{0:T(128)} %steps.1) | copy-start | bytes 52
  10.3 0.7 %copy-start.5 = (f32[128]{0:T(128)S(1)}, f32[128]{0:T(128)}, u32[]{:S(2)}) copy-start(f32[128]{0:T(128)} %profile.1) | copy-start | bytes 1540
  10.3 0.7 %copy-start.2 = (f32[256]{0:T(256)S(1)}, f32[256]{0:T(256)}, u32[]{:S(2)}) copy-start(f32[256]{0:T(256)} %param.6) | copy-start | bytes 3076
  10.3 0.7 %copy-start.3 = (s32[4]{0:T(128)S(1)}, s32[4]{0:T(128)}, u32[]{:S(2)}) copy-start(s32[4]{0:T(128)} %start.1) | copy-start | bytes 52
  10.3 8.6 %collective-permute-start.5 = (f32[20,8,128]{2,1,0:T(8,128)S(1)}, f32[20,8,128]{2,1,0:T(8,128)S(1)}, u32[]{:S(2)}, u32[]{:S(2)}) collective-permute-start(f32[20,8,128]{2,1,0:T(8,128)S(1)} %get-tuple-element.30), channel_id=1, source_target_pairs={{8,16},{16,8},{24,0},{0,24},{9,17},{17,9},{25,1},{1,25},{10,18},{1... | collective-permute-start | bytes 245768 | tf_op jit(solution)/shard_map/ppermute | solution.py:576
